TPU v7x, 32 devices: a whole 2x2x4 slice. The times are simulated.
32 devices in a mesh: px: 8 (over y, x, core), py: 4 (over z).
Axes of the slice: x: 2, y: 2, z: 4, core: 2. Of those that a mesh axis runs over, the one named last changes fastest.
Arguments:
- fields: bfloat16 [4, 16, 1024, 1024], P(None, None, 'px', 'py'), may hold values from -6 to 6
- x_operators: bfloat16 [3, 1024, 1024], replicated
- y_operators: bfloat16 [3, 1024, 1024], replicated
- viscosity: float32 [4], replicated, may hold values from 0.1 to 1
- wall_tile: int32 [4096], P(('px', 'py')), may hold values from 0 to 2047
- wall_owner: int32 [4096, 1], P(('px', 'py')), may hold values from 0 to 31; in each aligned block of 128 rows (0 to 127, 128 to 255, ...) at most 16 rows name the same one
- wall_row: int32 [4096], P(('px', 'py')), may hold values from 0 to 63
- solid_temp: float32 [512, 1024], P('px', 'py'), may hold values from -6 to 6
- conductivity: float32 [512, 1024], P('px', 'py'), may hold values from 0.2 to 1
Outputs:
- new_fields: bfloat16 [4, 16, 1024, 1024], P(None, None, 'px', 'py')
- new_solid: float32 [512, 1024], P('px', 'py')
Inputs may be any that keep to these rules, and one draw needn't show every extreme that they name: `wall_owner`: at most 16 of one device's wall slots name the same owner, and some owner receives exactly 16 of them. `wall_tile`: A y-line of the sending device's own block, numbered z times its x cells plus its local x.
All inputs are finite; a program needn't handle non-finite values.
Results may differ from a plain program's by a relative error of at most 0.0054.
Values may be sent and summed in bfloat16 or wider, within the bound.
No kernel may reach another device: no remote copies, remote signals or barrier semaphores. Data moves between devices by JAX's collectives and lax.ppermute only.
A program may use at most 128 MiB of HBM per device.

v0:
```python
import jax
import jax.numpy as jnp
from jax import lax
from jax.sharding import PartitionSpec as P

COND_STEPS = 8


time_step = 0.25
wall_gain = 0.5
diffusion_rate = 0.24
source_gain = 0.1


def with_halo(block, sides, width):
    for axis, dim in sides:
        count = lax.axis_size(axis)
        forward = [(i, i + 1) for i in range(count - 1)]
        backward = [(target, source) for source, target in forward]
        low = lax.ppermute(
            lax.slice_in_dim(block, block.shape[dim] - width, None, axis=dim), axis, forward
        )
        high = lax.ppermute(lax.slice_in_dim(block, 0, width, axis=dim), axis, backward)
        block = jnp.concatenate([low, block, high], axis=dim)
    return block


def on_device(
    fields,
    x_operators,
    y_operators,
    viscosity,
    wall_tile,
    wall_owner,
    wall_row,
    solid_temp,
    conductivity,
):
    rates = viscosity[:, None, None, None]
    x_rows = lax.all_to_all(fields, "px", split_axis=1, concat_axis=2, tiled=True)
    result = jnp.einsum("oij,fzjy->ofziy", x_operators, x_rows, preferred_element_type=jnp.float32)
    speed = x_rows[0].astype(jnp.float32)
    half_step = lax.all_to_all(
        (result[2] + time_step * (-speed * result[0] + rates * result[1])).astype(jnp.bfloat16),
        "px",
        split_axis=2,
        concat_axis=1,
        tiled=True,
    )
    y_rows = lax.all_to_all(half_step, "py", split_axis=1, concat_axis=3, tiled=True)
    result = jnp.einsum("oij,fzxj->ofzxi", y_operators, y_rows, preferred_element_type=jnp.float32)
    speed = y_rows[1].astype(jnp.float32)
    new_fields = lax.all_to_all(
        (result[2] + time_step * (-speed * result[0] + rates * result[1])).astype(jnp.bfloat16),
        "py",
        split_axis=3,
        concat_axis=1,
        tiled=True,
    )
    width = new_fields.shape[3]
    theta_lines = new_fields[3].reshape(-1, width)
    flux = wall_gain * jnp.take(theta_lines, wall_tile, axis=0).astype(jnp.float32)
    owner = wall_owner[:, 0]
    across_px = lax.axis_size("px")
    across_py = lax.axis_size("py")
    devices = across_px * across_py
    capacity = max(2, 4 * wall_tile.shape[0] // devices)
    onehot = (owner[:, None] == jnp.arange(devices, dtype=jnp.int32)[None, :]).astype(jnp.int32)
    earlier = jnp.cumsum(onehot, axis=0) - onehot
    position = jnp.sum(earlier * onehot, axis=1)
    sending = jnp.zeros((devices, capacity, width), jnp.float32).at[owner, position].set(flux)
    labels = jnp.full((devices, capacity), -1, jnp.int32).at[owner, position].set(wall_row)
    arrived, tags = (
        lax.all_to_all(
            sending.astype(jnp.bfloat16), ("px", "py"), split_axis=0, concat_axis=0, tiled=True
        ).astype(sending.dtype),
        lax.all_to_all(labels, ("px", "py"), split_axis=0, concat_axis=0, tiled=True),
    )
    solid_rows = solid_temp.shape[0]
    selector = (
        tags.reshape(-1)[None, :] == jnp.arange(solid_rows, dtype=jnp.int32)[:, None]
    ).astype(jnp.float32)
    source = jnp.dot(
        selector,
        arrived.reshape(-1, width),
        precision=lax.Precision.HIGHEST,
        preferred_element_type=jnp.float32,
    )
    margin_max = COND_STEPS
    kappa_ext, source_ext = (
        with_halo(conductivity, (("px", 0), ("py", 1)), margin_max),
        with_halo(source, (("px", 0), ("py", 1)), margin_max),
    )
    row_index = (
        lax.axis_index("px") * solid_rows
        - margin_max
        + jnp.arange(solid_rows + 2 * margin_max, dtype=jnp.int32)
    )
    col_index = (
        lax.axis_index("py") * width
        - margin_max
        + jnp.arange(width + 2 * margin_max, dtype=jnp.int32)
    )
    row_valid = (row_index >= 0) & (row_index < across_px * solid_rows)
    col_valid = (col_index >= 0) & (col_index < across_py * width)
    inside = (row_valid[:, None] & col_valid[None, :]).astype(jnp.float32)
    depth = 8
    temp = solid_temp
    extended = with_halo(temp, (("px", 0), ("py", 1)), depth)
    temp = extended
    kappa = kappa_ext
    heat = source_ext
    keep = inside
    for _ in range(depth):
        centre = temp[1:-1, 1:-1]
        kcentre = kappa[1:-1, 1:-1]
        near = [
            (temp[2:, 1:-1], kappa[2:, 1:-1]),
            (temp[:-2, 1:-1], kappa[:-2, 1:-1]),
            (temp[1:-1, 2:], kappa[1:-1, 2:]),
            (temp[1:-1, :-2], kappa[1:-1, :-2]),
        ]
        laplace = jnp.zeros(centre.shape, jnp.float32)
        for tnear, knear in near:
            laplace = laplace + 0.5 * (kcentre + knear) * (tnear - centre)
        temp = (centre + diffusion_rate * laplace + source_gain * heat[1:-1, 1:-1]) * keep[
            1:-1, 1:-1
        ]
        kappa = kcentre
        heat = heat[1:-1, 1:-1]
        keep = keep[1:-1, 1:-1]
    return (new_fields, temp)


def solution(mesh):
    return jax.shard_map(
        on_device,
        mesh=mesh,
        in_specs=(
            P(None, None, "px", "py"),
            P(),
            P(),
            P(),
            P(("px", "py")),
            P(("px", "py"), None),
            P(("px", "py")),
            P("px", "py"),
            P("px", "py"),
        ),
        out_specs=(P(None, None, "px", "py"), P("px", "py")),
        check_vma=False,
    )
```

profile of v0, /device:TPU:8, one launch (start us, length us, event | category | flops | bytes accessed | tf_op | source)
XLA Modules:
  0.0 488.3 jit_solution(10839279836841378847)
XLA Ops:
  3.1 52.7 %all_to_all.86 = bf16[4,16,128,256]{3,2,0,1:T(8,128)(2,1)} all-to-all(bf16[4,16,128,256]{3,2,0,1:T(8,128)(2,1)S(1)} %copy.55), channel_id=1, replica_groups=mesh['px'=8,'py'=4] {'px'}, dimensions={1} | all-to-all | bytes 8388608 | tf_op jit(solution)/shard_map/all_to_all | solution.py:40
  55.8 7.5 %copy.56 = bf16[4,8,2,128,256]{3,1,4,2,0:T(8,128)(2,1)} copy(bf16[4,8,2,128,256]{4,3,0,2,1:T(8,128)(2,1)} %bitcast.111) | data formatting | bytes 8388608 | tf_op jit(solution)/shard_map/all_to_all | solution.py:40
  66.0 7.3 %reshape.88 = bf16[4,2,1024,256,1]{2,3,1,0,4:T(8,128)(2,1)} reshape(bf16[4,2,8,128,256]{3,2,4,1,0:T(8,128)(2,1)} %bitcast.110) | data formatting | bytes 8388608 | tf_op jit(solution)/shard_map/all_to_all | solution.py:40
  75.0 20.0 %convolution_bitcast_fusion.1 = f32[3,4,2,1024,256]{3,4,0,2,1:T(8,128)} fusion(bf16[3,1024,1024]{2,1,0:T(8,128)(2,1)} %param.10, bf16[4,2,1024,256,1]{2,3,1,0,4:T(8,128)(2,1)} %reshape.88), kind=kOutput, calls=%fused_computation.4 | convolution fusion | flops 12884901888 | bytes 35651584 | tf_op jit(solution)/shard_map/oij,fzjy->ofziy/dot_general | solution.py:41
  95.0 12.1 %fusion.10 = bf16[4,2,1024,256]{2,3,1,0:T(8,128)(2,1)} fusion(f32[3,4,2,1024,256]{3,4,0,2,1:T(8,128)} %convolution_bitcast_fusion.1, f32[4]{0:T(128)S(1)} %copy-done.3, f32[2,1024,256]{1,2,0:T(8,128)S(1)} %neg.21), kind=kLoop, calls=%fused_computation.19 | loop fusion | flops 12582912 | bytes 31457296 | tf_op jit(solution)/shard_map/convert_element_type | solution.py:44
  107.1 11.2 %copy.59 = bf16[4,2,1024,256]{3,1,0,2:T(2,128)(2,1)} copy(bf16[4,2,1024,256]{2,3,1,0:T(8,128)(2,1)} %fusion.10) | data formatting | bytes 8388608 | tf_op jit(solution)/shard_map/convert_element_type | solution.py:44
  118.3 52.7 %all_to_all.87 = bf16[4,2,1024,256]{3,1,0,2:T(2,128)(2,1)S(1)} all-to-all(bf16[4,2,1024,256]{3,1,0,2:T(2,128)(2,1)} %copy.59), channel_id=1, replica_groups=mesh['px'=8,'py'=4] {'px'}, dimensions={2} | all-to-all | bytes 8388608 | tf_op jit(solution)/shard_map/all_to_all | solution.py:43
  174.6 5.4 %all-to-all-start.2 = ((bf16[4,16,128,256]{3,2,0,1:T(8,128)(2,1)}), bf16[4,16,128,256]{3,2,0,1:T(8,128)(2,1)}, u32[]{:S(2)}, u32[]{:S(2)}) async-start(bf16[4,16,128,256]{3,2,0,1:T(8,128)(2,1)} %copy.62), calls=%async_computation.2 | async-start | bytes 8388608 | tf_op jit(solution)/shard_map/all_to_all | solution.py:50
  180.5 7.1 %scatter_fusion = s32[32,16]{0,1:T(8,128)S(1)} fusion(s32[32,16]{0,1:T(8,128)S(1)} %broadcast_in_dim.16, s32[128]{0:T(128)S(1)} %fusion.144, s32[128]{0:T(128)S(1)} %copy-done.4), kind=kCustom, calls=%fused_computation.1 | custom fusion | bytes 2560 | tf_op jit(solution)/shard_map/scatter | solution.py:72
  188.3 81.1 %all-to-all-done.2 = bf16[4,16,128,256]{3,2,0,1:T(8,128)(2,1)} async-done(((bf16[4,16,128,256]{3,2,0,1:T(8,128)(2,1)}), bf16[4,16,128,256]{3,2,0,1:T(8,128)(2,1)}, u32[]{:S(2)}, u32[]{:S(2)}) %all-to-all-start.2) | async-done | bytes 4194336 | tf_op jit(solution)/shard_map/all_to_all | solution.py:50
  269.5 5.7 %all-to-all-start.4 = ((s32[32,1,16]{2,1,0:T(1,128)}), s32[32,1,16]{2,1,0:T(1,128)S(1)}, u32[]{:S(2)}, u32[]{:S(2)}) async-start(s32[32,1,16]{2,1,0:T(1,128)} %copy.71), calls=%async_computation.4 | async-start | bytes 32768 | tf_op jit(solution)/shard_map/all_to_all | solution.py:77
  275.2 7.7 %copy.64 = bf16[4,4,128,4,256]{4,3,2,1,0:T(4,128)(2,1)} copy(bf16[4,4,128,4,256]{4,2,0,1,3:T(8,128)(2,1)} %bitcast.14) | data formatting | bytes 8388608 | tf_op jit(solution)/shard_map/all_to_all | solution.py:50
  282.9 7.8 %reshape.90 = bf16[4,4,128,1024,1]{3,2,1,0,4:T(8,128)(2,1)} reshape(bf16[4,4,128,4,256]{4,3,2,1,0:T(4,128)(2,1)} %copy.64) | data formatting | bytes 8388608 | tf_op jit(solution)/shard_map/all_to_all | solution.py:50
  297.1 19.8 %convolution_bitcast_fusion = f32[3,4,4,128,1024]{4,3,0,2,1:T(8,128)} fusion(bf16[3,1024,1024]{2,1,0:T(8,128)(2,1)} %param.11, bf16[4,4,128,1024,1]{3,2,1,0,4:T(8,128)(2,1)} %reshape.90), kind=kOutput, calls=%fused_computation.3 | convolution fusion | flops 12884901888 | bytes 35651584 | tf_op jit(solution)/shard_map/oij,fzxj->ofzxi/dot_general | solution.py:51
  316.9 12.1 %fusion.4 = bf16[4,4,128,1024]{3,2,1,0:T(8,128)(2,1)} fusion(f32[3,4,4,128,1024]{4,3,0,2,1:T(8,128)} %convolution_bitcast_fusion, f32[4]{0:T(128)S(1)} %copy-done.3, f32[4,128,1024]{2,1,0:T(8,128)S(1)} %copy.67), kind=kLoop, calls=%fused_computation.10 | loop fusion | flops 12582912 | bytes 31457296 | tf_op jit(solution)/shard_map/convert_element_type | solution.py:54
  329.0 7.9 %copy.69 = bf16[4,4,128,1024]{2,1,0,3:T(4,128)(2,1)} copy(bf16[4,4,128,1024]{3,2,1,0:T(8,128)(2,1)} %fusion.4) | data formatting | bytes 8388608 | tf_op jit(solution)/shard_map/convert_element_type | solution.py:54
  336.9 5.4 %all-to-all-start.3 = ((bf16[4,4,128,1024]{2,1,0,3:T(4,128)(2,1)}), bf16[4,4,128,1024]{2,1,0,3:T(4,128)(2,1)}, u32[]{:S(2)}, u32[]{:S(2)}) async-start(bf16[4,4,128,1024]{2,1,0,3:T(4,128)(2,1)} %copy.69), calls=%async_computation.3 | async-start | bytes 8388608 | tf_op jit(solution)/shard_map/all_to_all | solution.py:53
  347.9 4.0 collective-permute-start
  353.4 79.2 %all-to-all-done.3 = bf16[4,4,128,1024]{2,1,0,3:T(4,128)(2,1)} async-done(((bf16[4,4,128,1024]{2,1,0,3:T(4,128)(2,1)}), bf16[4,4,128,1024]{2,1,0,3:T(4,128)(2,1)}, u32[]{:S(2)}, u32[]{:S(2)}) %all-to-all-start.3) | async-done | bytes 4194336 | tf_op jit(solution)/shard_map/all_to_all | solution.py:53
  432.6 7.3 %copy.70 = bf16[4,4,128,4,256]{4,2,1,3,0:T(8,128)(2,1)} copy(bf16[4,4,128,4,256]{2,1,0,4,3:T(4,128)(2,1)} %bitcast.24) | data formatting | bytes 8388608 | tf_op jit(solution)/shard_map/all_to_all | solution.py:53
  442.2 7.1 %scatter_fusion.1 = f32[32,16,256]{2,1,0:T(8,128)S(1)} fusion(f32[32,16,256]{2,1,0:T(8,128)S(1)} %broadcast_in_dim.17, s32[128]{0:T(128)S(1)} %fusion.144, f32[128,256]{1,0:T(8,128)S(1)} %convert_multiply_fusion), kind=kCustom, calls=%fused_computation.2 | custom fusion | bytes 394240 | tf_op jit(solution)/shard_map/scatter | solution.py:71
  450.1 6.9 %all-to-all-start.5 = ((bf16[32,16,256]{2,1,0:T(8,128)(2,1)}), bf16[32,16,256]{2,1,0:T(8,128)(2,1)S(1)}, u32[]{:S(2)}, u32[]{:S(2)}) async-start(bf16[32,16,256]{2,1,0:T(8,128)(2,1)} %convert_element_type.42), calls=%async_computation.5 | async-start | bytes 524288 | tf_op jit(solution)/shard_map/all_to_all | solution.py:74
  459.2 3.7 collective-permute-start.6
  475.2 3.4 collective-permute-start.10
  (90 shorter events, 52.1 us)
Async XLA Ops:
  75.0 20.0 %copy-start.3 = (f32[4]{0:T(128)S(1)}, f32[4]{0:T(128)}, u32[]{:S(2)}) copy-start(f32[4]{0:T(128)} %param.12) | copy-start | bytes 52
  174.6 5.5 %copy-start.2 = (s32[128,1]{0,1:T(1,128)S(1)}, s32[128,1]{0,1:T(1,128)}, u32[]{:S(2)}) copy-start(s32[128,1]{0,1:T(1,128)} %param.14) | copy-start | bytes 1540
  174.6 5.9 %copy-start.4 = (s32[128]{0:T(128)S(1)}, s32[128]{0:T(128)}, u32[]{:S(2)}) copy-start(s32[128]{0:T(128)} %param.15) | copy-start | bytes 1540
  174.6 94.9 %all-to-all-start.2 = ((bf16[4,16,128,256]{3,2,0,1:T(8,128)(2,1)}), bf16[4,16,128,256]{3,2,0,1:T(8,128)(2,1)}, u32[]{:S(2)}, u32[]{:S(2)}) async-start(bf16[4,16,128,256]{3,2,0,1:T(8,128)(2,1)} %copy.62), calls=%async_computation.2 | async-start | bytes 8388608 | tf_op jit(solution)/shard_map/all_to_all | solution.py:50
  269.5 67.4 %all-to-all-start.4 = ((s32[32,1,16]{2,1,0:T(1,128)}), s32[32,1,16]{2,1,0:T(1,128)S(1)}, u32[]{:S(2)}, u32[]{:S(2)}) async-start(s32[32,1,16]{2,1,0:T(1,128)} %copy.71), calls=%async_computation.4 | async-start | bytes 32768 | tf_op jit(solution)/shard_map/all_to_all | solution.py:77
  336.8 5.4 %copy-start = (f32[64,256]{1,0:T(8,128)S(1)}, f32[64,256]{1,0:T(8,128)}, u32[]{:S(2)}) copy-start(f32[64,256]{1,0:T(8,128)} %param.17) | copy-start | bytes 196612
  336.8 9.7 %copy-start.1 = (f32[64,256]{1,0:T(8,128)S(1)}, f32[64,256]{1,0:T(8,128)}, u32[]{:S(2)}) copy-start(f32[64,256]{1,0:T(8,128)} %param.16) | copy-start | bytes 196612
  336.8 15.0 %copy-start.5 = (s32[128]{0:T(128)S(1)}, s32[128]{0:T(128)}, u32[]{:S(2)}) copy-start(s32[128]{0:T(128)} %param.13) | copy-start | bytes 1540
  336.9 95.8 %all-to-all-start.3 = ((bf16[4,4,128,1024]{2,1,0,3:T(4,128)(2,1)}), bf16[4,4,128,1024]{2,1,0,3:T(4,128)(2,1)}, u32[]{:S(2)}, u32[]{:S(2)}) async-start(bf16[4,4,128,1024]{2,1,0,3:T(4,128)(2,1)} %copy.69), calls=%async_computation.3 | async-start | bytes 8388608 | tf_op jit(solution)/shard_map/all_to_all | solution.py:53
  342.2 11.1 %collective-permute-start.5 = (f32[8,256]{1,0:T(8,128)S(1)}, f32[8,256]{1,0:T(8,128)S(1)}, u32[]{:S(2)}, u32[]{:S(2)}) collective-permute-start(f32[8,256]{1,0:T(8,128)S(1)} %get-tuple-element.12), channel_id=1, source_target_pairs={{4,0},{8,4},{12,8},{16,12},{20,16},{24,20},{28,24},{5,1},{9,5},{13... | collective-permute-start | bytes 24584 | tf_op jit(solution)/shard_map/ppermute | solution.py:23
  343.5 9.8 %collective-permute-start.4 = (f32[8,256]{1,0:T(8,128)S(1)}, f32[8,256]{1,0:T(8,128)S(1)}, u32[]{:S(2)}, u32[]{:S(2)}) collective-permute-start(f32[8,256]{1,0:T(8,128)S(1)} %get-tuple-element.13), channel_id=1, source_target_pairs={{0,4},{4,8},{8,12},{12,16},{16,20},{20,24},{24,28},{1,5},{5,9},{9,... | collective-permute-start | bytes 24584 | tf_op jit(solution)/shard_map/ppermute | solution.py:20
  346.6 116.3 %collective-permute-start.1 = (f32[8,256]{1,0:T(8,128)S(1)}, f32[8,256]{1,0:T(8,128)S(1)}, u32[]{:S(2)}, u32[]{:S(2)}) collective-permute-start(f32[8,256]{1,0:T(8,128)S(1)} %get-tuple-element.8), channel_id=1, source_target_pairs={{4,0},{8,4},{12,8},{16,12},{20,16},{24,20},{28,24},{5,1},{9,5},{13... | collective-permute-start | bytes 24584 | tf_op jit(solution)/shard_map/ppermute | solution.py:23
  347.9 109.1 %collective-permute-start = (f32[8,256]{1,0:T(8,128)S(1)}, f32[8,256]{1,0:T(8,128)S(1)}, u32[]{:S(2)}, u32[]{:S(2)}) collective-permute-start(f32[8,256]{1,0:T(8,128)S(1)} %get-tuple-element.9), channel_id=1, source_target_pairs={{0,4},{4,8},{8,12},{12,16},{16,20},{20,24},{24,28},{1,5},{5,9},{9,... | collective-permute-start | bytes 24584 | tf_op jit(solution)/shard_map/ppermute | solution.py:20
  450.1 18.8 %all-to-all-start.5 = ((bf16[32,16,256]{2,1,0:T(8,128)(2,1)}), bf16[32,16,256]{2,1,0:T(8,128)(2,1)S(1)}, u32[]{:S(2)}, u32[]{:S(2)}) async-start(bf16[32,16,256]{2,1,0:T(8,128)(2,1)} %convert_element_type.42), calls=%async_computation.5 | async-start | bytes 524288 | tf_op jit(solution)/shard_map/all_to_all | solution.py:74
  457.1 24.0 %collective-permute-start.7 = (f32[80,8]{1,0:T(8,128)S(1)}, f32[80,8]{1,0:T(8,128)S(1)}, u32[]{:S(2)}, u32[]{:S(2)}) collective-permute-start(f32[80,8]{1,0:T(8,128)S(1)} %get-tuple-element.6), channel_id=1, source_target_pairs={{1,0},{2,1},{3,2},{5,4},{6,5},{7,6},{9,8},{10,9},{11,10},{13,12},{... | collective-permute-start | bytes 7688 | tf_op jit(solution)/shard_map/ppermute | solution.py:23
  459.2 21.9 %collective-permute-start.6 = (f32[80,8]{1,0:T(8,128)S(1)}, f32[80,8]{1,0:T(8,128)S(1)}, u32[]{:S(2)}, u32[]{:S(2)}) collective-permute-start(f32[80,8]{1,0:T(8,128)S(1)} %get-tuple-element.7), channel_id=1, source_target_pairs={{0,1},{1,2},{2,3},{4,5},{5,6},{6,7},{8,9},{9,10},{10,11},{12,13},{... | collective-permute-start | bytes 7688 | tf_op jit(solution)/shard_map/ppermute | solution.py:20
  463.0 7.3 %collective-permute-start.2 = (f32[80,8]{1,0:T(8,128)S(1)}, f32[80,8]{1,0:T(8,128)S(1)}, u32[]{:S(2)}, u32[]{:S(2)}) collective-permute-start(f32[80,8]{1,0:T(8,128)S(1)} %get-tuple-element.2), channel_id=1, source_target_pairs={{0,1},{1,2},{2,3},{4,5},{5,6},{6,7},{8,9},{9,10},{10,11},{12,13},{... | collective-permute-start | bytes 7688 | tf_op jit(solution)/shard_map/ppermute | solution.py:20
  466.4 5.9 %collective-permute-start.3 = (f32[80,8]{1,0:T(8,128)S(1)}, f32[80,8]{1,0:T(8,128)S(1)}, u32[]{:S(2)}, u32[]{:S(2)}) collective-permute-start(f32[80,8]{1,0:T(8,128)S(1)} %get-tuple-element.3), channel_id=1, source_target_pairs={{1,0},{2,1},{3,2},{5,4},{6,5},{7,6},{9,8},{10,9},{11,10},{13,12},{... | collective-permute-start | bytes 7688 | tf_op jit(solution)/shard_map/ppermute | solution.py:23
  469.1 3.3 collective-permute-start.8
  470.4 4.8 collective-permute-start.9
  475.2 6.0 %collective-permute-start.10 = (f32[80,8]{1,0:T(8,128)S(1)}, f32[80,8]{1,0:T(8,128)S(1)}, u32[]{:S(2)}, u32[]{:S(2)}) collective-permute-start(f32[80,8]{1,0:T(8,128)S(1)} %get-tuple-element.4), channel_id=1, source_target_pairs={{0,1},{1,2},{2,3},{4,5},{5,6},{6,7},{8,9},{9,10},{10,11},{12,13},{... | collective-permute-start | bytes 7688 | tf_op jit(solution)/shard_map/ppermute | solution.py:20
  478.6 5.9 %collective-permute-start.11 = (f32[80,8]{1,0:T(8,128)S(1)}, f32[80,8]{1,0:T(8,128)S(1)}, u32[]{:S(2)}, u32[]{:S(2)}) collective-permute-start(f32[80,8]{1,0:T(8,128)S(1)} %get-tuple-element.5), channel_id=1, source_target_pairs={{1,0},{2,1},{3,2},{5,4},{6,5},{7,6},{9,8},{10,9},{11,10},{13,12},{... | collective-permute-start | bytes 7688 | tf_op jit(solution)/shard_map/ppermute | solution.py:23
where the time goes:
time: 493 us; the launch traced here: 488 us
  waiting for transfers between devices  167 us (34%)
  blocking collectives  105 us (21%)
  local copies, waits for them, and re-layouts  88.6 us (18%)
  starting transfers between devices  53.1 us (11%)
  matrix products  40 us (8%)
  other arithmetic  33.1 us (7%)
    all_to_all x1, waiting for transfers between devices, on_device(): lax.all_to_all(half_step, 'py', split_axis=1, concat_axis=3, tiled=True)  81.1 us
    all_to_all x1, waiting for transfers between devices, on_device(): lax.all_to_all((result[2] + time_step * (-speed * result[0] + rates * res...  79.2 us
    all_to_all x1, blocking collectives, on_device(): lax.all_to_all(fields, 'px', split_axis=1, concat_axis=2, tiled=True)  52.7 us
    all_to_all x1, blocking collectives, on_device(): lax.all_to_all((result[2] + time_step * (-speed * result[0] + rates * res...  52.7 us
    convert_element_type x2, other arithmetic, on_device(): (result[2] + time_step * (-speed * result[0] + rates * result[1])).astype...  24.2 us
    dot_general x1, matrix products, on_device(): jnp.einsum('oij,fzjy->ofziy', x_operators, x_rows, preferred_element_type...  20 us
    dot_general x1, matrix products, on_device(): jnp.einsum('oij,fzxj->ofzxi', y_operators, y_rows, preferred_element_type...  19.8 us
    convert_element_type x2, local copies, waits for them, and re-layouts, on_device(): (result[2] + time_step * (-speed * result[0] + rates * result[1])).astype...  19.1 us
  transfers between devices with their start and end apart: 16, of which 5 were waited for; matrix products, arithmetic and copies ran while one was open for 18% of the time, Pallas kernels for 0%

commit v1 on v0

v1 whole, which is shorter than its diff:
```python
import functools

import jax
import jax.numpy as jnp
from jax import lax
from jax.experimental import pallas as pl
from jax.experimental.pallas import tpu as pltpu
from jax.sharding import PartitionSpec as P

COND_STEPS = 8

time_step = 0.25
wall_gain = 0.5
diffusion_rate = 0.24
source_gain = 0.1

U, V, W, THETA = 0, 1, 2, 3
FORWARD = (U, V, THETA, W)
BACK = (V, THETA, U, W)
VMEM_BYTES = 40 * 1024 * 1024

smem = pl.BlockSpec(memory_space=pltpu.SMEM)
vmem = pl.BlockSpec(memory_space=pltpu.VMEM)
anywhere = pl.BlockSpec(memory_space=pl.ANY)


def params():
    return pltpu.CompilerParams(vmem_limit_bytes=VMEM_BYTES)


def with_halo(block, sides, width):
    for axis, dim in sides:
        count = lax.axis_size(axis)
        forward = [(i, i + 1) for i in range(count - 1)]
        backward = [(target, source) for source, target in forward]
        low = lax.ppermute(
            lax.slice_in_dim(block, block.shape[dim] - width, None, axis=dim), axis, forward
        )
        high = lax.ppermute(lax.slice_in_dim(block, 0, width, axis=dim), axis, backward)
        block = jnp.concatenate([low, block, high], axis=dim)
    return block


def shuffle(inputs, place, take):
    outer, block = len(inputs), inputs[0].shape[1:]
    inner = inputs[0].shape[0]

    def kernel(at, *refs):
        for k in range(inner):
            for j in range(outer):
                refs[outer + k][at[0] ^ j] = refs[j][at[1] ^ k]

    return pl.pallas_call(
        kernel,
        in_specs=[smem] + [vmem] * outer,
        out_specs=[vmem] * inner,
        out_shape=[jax.ShapeDtypeStruct((outer,) + block, inputs[0].dtype)] * inner,
        compiler_params=params(),
        name="shuffle",
    )(jnp.stack([place, take]), *inputs)


def x_pass(field, at, operators, viscosity, own, others, speed):
    groups, members = len(own), len(others) + 1
    blocks, xb, yb = own[0].shape
    part = blocks // members
    width = part * yb
    length = groups * members * xb
    many = min(groups, max(1, 256 // xb))
    steps = groups // many
    first = field == U

    def kernel(at_ref, visc_ref, op_ref, *refs):
        own_refs, other_refs = refs[:groups], refs[groups : groups + members - 1]
        rest = refs[groups + members - 1 :]
        if first:
            outs, lines = rest[:members], rest[members]
        else:
            speed_ref, outs, lines = rest[0], rest[1 : 1 + members], rest[1 + members]
        step = pl.program_id(0)
        q, m = at_ref[0], at_ref[1]

        def start(group, member):
            return pl.multiple_of(((q ^ group) * members + (m ^ member)) * xb, xb)

        @pl.when(step == 0)
        def _():
            for t in range(groups):
                for j in range(part):
                    lines[pl.ds(start(t, 0), xb), j * yb : (j + 1) * yb] = own_refs[t][j]
                    for r in range(1, members):
                        lines[pl.ds(start(t, r), xb), j * yb : (j + 1) * yb] = other_refs[r - 1][t, j]

        result = jnp.dot(
            op_ref[...].reshape(3 * many * xb, length), lines[...], preferred_element_type=jnp.float32
        ).reshape(3, many, xb, width)
        turn = step // steps
        for c in range(many):
            if first:
                row = ((step % steps * many + c) * members + (m ^ turn)) * xb
                u = lines[pl.ds(pl.multiple_of(row, xb), xb), :]
            else:
                u = speed_ref[c, 0]
            value = result[2, c] + time_step * (
                -u.astype(jnp.float32) * result[0, c] + visc_ref[field] * result[1, c]
            )
            value = value.astype(jnp.bfloat16)
            for r in range(members):

                @pl.when(turn == r)
                def _():
                    outs[r][c] = value

    def out_block(r):
        return pl.BlockSpec(
            (many, xb, width), lambda i, at: (jnp.clip(i - r * steps, 0, steps - 1), 0, 0)
        )

    def rows(i, at):
        return i % steps, at[1] ^ (i // steps), 0, 0

    in_specs = [
        smem,
        pl.BlockSpec((3, many, 1, xb, length), lambda i, at: (0,) + rows(i, at)),
    ]
    in_specs += [pl.BlockSpec((part, xb, yb), lambda i, at: (at[1], 0, 0))] * groups
    in_specs += [pl.BlockSpec((groups, part, xb, yb), lambda i, at: (0, 0, 0, 0))] * (members - 1)
    args = [viscosity, operators.reshape(3, groups, members, xb, length), *own, *others]
    out_specs = [out_block(r) for r in range(members)]
    out_shape = [jax.ShapeDtypeStruct((groups, xb, width), jnp.bfloat16)] * members
    scratch = []
    if first:
        out_specs.append(pl.BlockSpec((length, width), lambda i, at: (0, 0)))
        out_shape.append(jax.ShapeDtypeStruct((length, width), jnp.bfloat16))
    else:
        in_specs.append(pl.BlockSpec((many, 1, xb, width), rows))
        args.append(speed.reshape(groups, members, xb, width))
        scratch = [pltpu.VMEM((length, width), jnp.bfloat16)]
    outs = pl.pallas_call(
        kernel,
        grid_spec=pltpu.PrefetchScalarGridSpec(
            num_scalar_prefetch=1,
            grid=(steps * members,),
            in_specs=in_specs,
            out_specs=out_specs,
            scratch_shapes=scratch,
        ),
        out_shape=out_shape,
        compiler_params=params(),
        cost_estimate=pl.CostEstimate(
            flops=6 * length * length * width,
            bytes_accessed=6 * length * length + 4 * length * width,
            transcendentals=0,
        ),
        name="x_pass",
    )(at, *args)
    return outs[:members], outs[members] if first else speed


def y_pass(field, at, operators, viscosity, own, others, speed, yb):
    groups, xb, width = own.shape
    members = len(others) + 1
    length = width * members
    blocks = length // yb
    first = field == V

    def kernel(at_ref, visc_ref, op_ref, *refs):
        sources, rest = refs[:members], refs[members:]
        if first:
            outs, lines = rest[:groups], rest[groups]
        else:
            speed_ref, outs, lines = rest[0], rest[1 : 1 + groups], rest[1 + groups]
        step = pl.program_id(0)
        q, m = at_ref[0], at_ref[1]

        @pl.when(step == 0)
        def _():
            for t in range(groups):
                for r in range(members):
                    columns = pl.ds(pl.multiple_of((m ^ r) * width, width), width)
                    lines[t * xb : (t + 1) * xb, columns] = sources[r][q ^ t]

        result = lax.dot_general(
            lines[...],
            op_ref[...].reshape(3 * yb, length),
            (((1,), (1,)), ((), ())),
            preferred_element_type=jnp.float32,
        )
        if first:
            v = lines[:, pl.ds(pl.multiple_of(step * yb, yb), yb)]
        else:
            v = speed_ref[...]
        value = result[:, 2 * yb :] + time_step * (
            -v.astype(jnp.float32) * result[:, :yb] + visc_ref[field] * result[:, yb : 2 * yb]
        )
        value = value.astype(jnp.bfloat16)
        for t in range(groups):
            outs[t][0] = value[t * xb : (t + 1) * xb]

    in_specs = [smem, pl.BlockSpec((3, yb, length), lambda i, at: (0, i, 0))]
    in_specs += [pl.BlockSpec((groups, xb, width), lambda i, at: (0, 0, 0))] * members
    args = [viscosity, operators, own, *others]
    out_specs = [pl.BlockSpec((1, xb, yb), lambda i, at: (i, 0, 0))] * groups
    out_shape = [jax.ShapeDtypeStruct((blocks, xb, yb), jnp.bfloat16)] * groups
    scratch = []
    if first:
        out_specs.append(pl.BlockSpec((groups * xb, length), lambda i, at: (0, 0)))
        out_shape.append(jax.ShapeDtypeStruct((groups * xb, length), jnp.bfloat16))
    else:
        in_specs.append(pl.BlockSpec((groups * xb, yb), lambda i, at: (0, i)))
        args.append(speed)
        scratch = [pltpu.VMEM((groups * xb, length), jnp.bfloat16)]
    outs = pl.pallas_call(
        kernel,
        grid_spec=pltpu.PrefetchScalarGridSpec(
            num_scalar_prefetch=1,
            grid=(blocks,),
            in_specs=in_specs,
            out_specs=out_specs,
            scratch_shapes=scratch,
        ),
        out_shape=out_shape,
        compiler_params=params(),
        cost_estimate=pl.CostEstimate(
            flops=6 * length * length * groups * xb,
            bytes_accessed=6 * length * length + 4 * length * groups * xb,
            transcendentals=0,
        ),
        name="y_pass",
    )(at, *args)
    return outs[:groups], outs[groups] if first else speed


def put(buffer, pieces, field, b, shape):
    count, groups = len(pieces), pieces[0].shape[0]

    def kernel(at, *refs):
        out, sems = refs[-2], refs[-1]
        copies = [
            pltpu.make_async_copy(
                refs[s], out.at[field, pl.ds((at[0] ^ s) * groups, groups)], sems.at[s]
            )
            for s in range(count)
        ]
        for copy in copies:
            copy.start()
        for copy in copies:
            copy.wait()

    extra = [] if buffer is None else [buffer]
    return pl.pallas_call(
        kernel,
        in_specs=[smem] + [anywhere] * (count + len(extra)),
        out_specs=anywhere,
        out_shape=jax.ShapeDtypeStruct(shape, pieces[0].dtype),
        scratch_shapes=[pltpu.SemaphoreType.DMA((count,))],
        input_output_aliases={} if buffer is None else {1 + count: 0},
        compiler_params=params(),
        name="put",
    )(b.reshape(1), *pieces, *extra)


def wall_lines(pieces, b, tile, slot, slots):
    groups, xb, yb = pieces[0].shape
    span = groups * xb
    count = tile.shape[0]

    def kernel(at, tile_ref, slot_ref, *refs):
        places = lax.broadcasted_iota(jnp.int32, (count, span), 1)
        lines = jnp.zeros((count, yb), jnp.float32)
        for s, piece in enumerate(refs[:-1]):
            chosen = tile_ref[...] == places + (at[0] ^ s) * span
            lines = lines + jnp.dot(
                chosen.astype(jnp.float32).astype(jnp.bfloat16),
                piece[...].reshape(span, yb),
                preferred_element_type=jnp.float32,
            )
        filled = slot_ref[...] == lax.broadcasted_iota(jnp.int32, (slots, count), 0)
        refs[-1][...] = jnp.dot(
            filled.astype(jnp.float32).astype(jnp.bfloat16),
            lines.astype(jnp.bfloat16),
            preferred_element_type=jnp.float32,
        ).astype(jnp.bfloat16)

    return pl.pallas_call(
        kernel,
        in_specs=[smem] + [vmem] * (2 + len(pieces)),
        out_specs=vmem,
        out_shape=jax.ShapeDtypeStruct((slots, yb), jnp.bfloat16),
        compiler_params=params(),
        name="wall_lines",
    )(b.reshape(1), tile.reshape(-1, 1), slot.reshape(1, -1), *pieces)


def conduct(temp, faces, heat, rows, columns, margin):
    def kernel(temp_ref, faces_ref, heat_ref, out_ref):
        t = temp_ref[...]
        high, wide = t.shape
        for _ in range(COND_STEPS):
            change = heat_ref[...]
            for n, (shift, dim) in enumerate(((high - 1, 0), (1, 0), (wide - 1, 1), (1, 1))):
                change = change + faces_ref[n] * (pltpu.roll(t, shift, dim) - t)
            t = t + change
        out_ref[...] = t[margin : margin + rows, margin : margin + columns]

    return pl.pallas_call(
        kernel,
        in_specs=[vmem] * 3,
        out_specs=vmem,
        out_shape=jax.ShapeDtypeStruct((rows, columns), jnp.float32),
        compiler_params=params(),
        name="conduct",
    )(temp, faces, heat)


def on_device(
    fields,
    x_operators,
    y_operators,
    viscosity,
    wall_tile,
    wall_owner,
    wall_row,
    solid_temp,
    conductivity,
):
    across_px, across_py = lax.axis_size("px"), lax.axis_size("py")
    devices = across_px * across_py
    layers, xb, yb = fields.shape[1:]
    members = devices // layers
    groups = across_px // members
    a, b = lax.axis_index("px"), lax.axis_index("py")
    q, m = a // members, a % members
    at = jnp.stack([q, m])

    def along_py(piece, s):
        return lax.ppermute(piece, "py", [(i, i ^ s) for i in range(across_py)])

    def along_groups(piece, t):
        return lax.ppermute(piece, "px", [(i, i ^ (t * members)) for i in range(across_px)])

    def along_members(piece, r):
        return lax.ppermute(piece, "px", [(i, i ^ r) for i in range(across_px)])

    margin = COND_STEPS
    sides = (("px", 0), ("py", 1))
    solid = with_halo(
        jnp.stack([solid_temp, conductivity]), (("px", 1), ("py", 2)), margin
    )
    rows, columns = solid_temp.shape
    high, wide = solid.shape[1:]
    lanes = -(-wide // 128) * 128
    solid = jnp.pad(solid, ((0, 0), (0, 0), (0, lanes - wide)))
    row_index = a * rows - margin + jnp.arange(high, dtype=jnp.int32)
    col_index = b * columns - margin + jnp.arange(lanes, dtype=jnp.int32)
    inside = ((row_index >= 0) & (row_index < across_px * rows))[:, None] & (
        (col_index >= 0) & (col_index < across_py * columns)
    )[None, :]
    kappa = solid[1]
    faces = jnp.stack(
        [
            jnp.where(inside, diffusion_rate * 0.5 * (kappa + jnp.roll(kappa, shift, dim)), 0.0)
            for shift, dim in ((-1, 0), (1, 0), (-1, 1), (1, 1))
        ]
    )

    count = wall_tile.shape[0]
    owner = wall_owner[:, 0]
    capacity = max(2, 4 * count // devices)
    slots = devices * capacity
    order = jnp.arange(count, dtype=jnp.int32)
    earlier = (owner[:, None] == owner[None, :]) & (order[None, :] < order[:, None])
    slot = owner * capacity + jnp.sum(earlier.astype(jnp.int32), axis=1)
    filled = slot[None, :] == jnp.arange(slots, dtype=jnp.int32)[:, None]
    labels = jnp.sum(jnp.where(filled, wall_row[None, :] + 1, 0), axis=1) - 1
    tags = lax.all_to_all(
        labels.reshape(devices, capacity), ("px", "py"), split_axis=0, concat_axis=0, tiled=True
    )

    part = across_py // members
    kept, speed = {}, None
    for f in FORWARD:
        pieces = [
            lax.dynamic_slice_in_dim(fields[f], (b ^ s) * groups, groups, axis=0)
            for s in range(across_py)
        ]
        pieces = [pieces[0]] + [along_py(pieces[s], s) for s in range(1, across_py)]
        sending = shuffle(pieces, b, q)
        own = [sending[0]] + [along_groups(sending[t], t) for t in range(1, groups)]
        others = [
            along_members(
                jnp.stack(
                    [lax.dynamic_slice_in_dim(o, (m ^ r) * part, part, axis=0) for o in own]
                ),
                r,
            )
            for r in range(1, members)
        ]
        half, speed = x_pass(f, at, x_operators, viscosity, own, others, speed)
        kept[f] = (half[0], [along_members(half[r], r) for r in range(1, members)])

    new_fields, speed = None, None
    for f in BACK:
        own, others = kept[f]
        sending, speed = y_pass(f, at, y_operators, viscosity, own, others, speed, yb)
        own = [sending[0]] + [along_groups(sending[t], t) for t in range(1, groups)]
        sending = shuffle(own, q, b)
        pieces = [sending[0]] + [along_py(sending[s], s) for s in range(1, across_py)]
        new_fields = put(new_fields, pieces, f, b, fields.shape)
        if f == THETA:
            flux = wall_lines(pieces, b, wall_tile, slot, slots)
            arrived = lax.all_to_all(
                flux.reshape(devices, capacity, yb),
                ("px", "py"),
                split_axis=0,
                concat_axis=0,
                tiled=True,
            ).reshape(slots, yb)
            selector = tags.reshape(-1)[None, :] == jnp.arange(rows, dtype=jnp.int32)[:, None]
            source = (wall_gain * source_gain) * jnp.dot(
                selector.astype(jnp.bfloat16), arrived, preferred_element_type=jnp.float32
            )
            heat = with_halo(source, sides, margin)
            heat = jnp.pad(heat, ((0, 0), (0, lanes - wide)))
            new_solid = conduct(solid[0], faces, heat, rows, columns, margin)
    return new_fields, new_solid


def solution(mesh):
    return jax.shard_map(
        on_device,
        mesh=mesh,
        in_specs=(
            P(None, None, "px", "py"),
            P(),
            P(),
            P(),
            P(("px", "py")),
            P(("px", "py"), None),
            P(("px", "py")),
            P("px", "py"),
            P("px", "py"),
        ),
        out_specs=(P(None, None, "px", "py"), P("px", "py")),
        check_vma=False,
    )
```

time: 493 us -> 334 us (0.68)
  blocking collectives: 105 us -> 0 us
  Pallas kernels: 0 us -> 61.8 us
  local copies, waits for them, and re-layouts: 88.6 us -> 33.6 us
  matrix products: 40 us -> 1.12 us
  starting transfers between devices: 53.1 us -> 91.4 us
  other arithmetic: 33.1 us -> 3.21 us
  waiting for transfers between devices: 167 us -> 141 us
    all_to_all x4 -> x2, waiting for transfers between devices: 160 us -> 1.86 us  [the longest x1 1.86 us: on_device(): lax.all_to_all(labels.reshape(devices, capacity), ('px', 'py'), split_axi...]
    ppermute x0 -> x56, waiting for transfers between devices: none -> 139 us  [the longest x24 99.9 us: along_py(): return lax.ppermute(piece, 'py', [(i, i ^ s) for i in range(across_py)])]
    all_to_all x2 -> x0, blocking collectives: 105 us -> none  [the longest x1 52.7 us: on_device(): lax.all_to_all(fields, 'px', split_axis=1, concat_axis=2, tiled=True)]
    pallas_call x0 -> x22, Pallas kernels: none -> 61.8 us  [the longest x4 25.2 us: x_pass(): pl.pallas_call(kernel, grid_spec=pltpu.PrefetchScalarGridSpec(num_scalar_...]
    ppermute x0 -> x56, starting transfers between devices: none -> 58.8 us  [the longest x24 29.4 us: along_py(): return lax.ppermute(piece, 'py', [(i, i ^ s) for i in range(across_py)])]
    all_to_all x11 -> x1, local copies, waits for them, and re-layouts: 44.8 us -> 0.51 us  [on_device(): lax.all_to_all(labels.reshape(devices, capacity), ('px', 'py'), split_axi...]
    dot_general x3 -> x1, matrix products: 40 us -> 1.12 us  [on_device(): jnp.dot(selector.astype(jnp.bfloat16), arrived, preferred_element_type=jn...]
    convert_element_type x5 -> x0, other arithmetic: 25.1 us -> none  [the longest x2 24.2 us: on_device(): (result[2] + time_step * (-speed * result[0] + rates * result[1])).astype...]
  transfers between devices with their start and end apart: 16 -> 66, of which waited for: 5 -> 26; matrix products, arithmetic and copies ran while one was open for 18% -> 4% of each run, Pallas kernels for 0% -> 18%
where the time goes in v1:
time: 334 us; the launch traced here: 333 us
  waiting for transfers between devices  141 us (42%)
  starting transfers between devices  91.4 us (27%)
  Pallas kernels  61.8 us (19%)
  local copies, waits for them, and re-layouts  33.6 us (10%)
    ppermute x24, waiting for transfers between devices, along_py(): return lax.ppermute(piece, 'py', [(i, i ^ s) for i in range(across_py)])  99.9 us
    ppermute x24, waiting for transfers between devices, along_groups(): lax.ppermute(piece, 'px', [(i, i ^ t * members) for i in range(across_px)])  38.9 us
    ppermute x24, starting transfers between devices, along_py(): return lax.ppermute(piece, 'py', [(i, i ^ s) for i in range(across_py)])  29.4 us
    ppermute x24, starting transfers between devices, along_groups(): lax.ppermute(piece, 'px', [(i, i ^ t * members) for i in range(across_px)])  27.6 us
    pallas_call x4, Pallas kernels, x_pass(): pl.pallas_call(kernel, grid_spec=pltpu.PrefetchScalarGridSpec(num_scalar_...  25.2 us
    pallas_call x4, Pallas kernels, y_pass(): pl.pallas_call(kernel, grid_spec=pltpu.PrefetchScalarGridSpec(num_scalar_...  23.6 us
    unnamed x52, local copies, waits for them, and re-layouts  19.7 us
    ppermute x4, starting transfers between devices, with_halo(): lax.ppermute(lax.slice_in_dim(block, block.shape[dim] - width, None, axis...  14 us
  transfers between devices with their start and end apart: 66, of which 26 were waited for; matrix products, arithmetic and copies ran while one was open for 4% of the time, Pallas kernels for 18%

profile of v1, /device:TPU:8, one launch (start us, length us, event | category | flops | bytes accessed | tf_op | source)
XLA Modules:
  0.0 333.3 jit_solution(7479834691316325251)
XLA Ops:
  14.4 6.9 %all-to-all-start = ((s32[32,1,16]{2,1,0:T(1,128)}), s32[32,1,16]{2,1,0:T(1,128)S(1)}, u32[]{:S(2)}, u32[]{:S(2)}) async-start(s32[32,1,16]{2,1,0:T(1,128)} %bitcast.46), calls=%async_computation | async-start | bytes 32768 | tf_op jit(solution)/shard_map/all_to_all | solution.py:376
  43.3 5.9 %collective-permute-done.7.refs_1_ = bf16[4,128,256]{2,1,0:T(8,128)(2,1)S(1)} collective-permute-done((bf16[4,128,256]{2,1,0:T(8,128)(2,1)}, bf16[4,128,256]{2,1,0:T(8,128)(2,1)S(1)}, u32[]{:S(2)}, u32[]{:S(2)}) %collective-permute-start.7) | collective-permute-done | bytes 262176 | tf_op jit(solution)/shard_map/ppermute | solution.py:337
  51.7 5.0 %collective-permute-done.8.refs_2_ = bf16[4,128,256]{2,1,0:T(8,128)(2,1)S(1)} collective-permute-done((bf16[4,128,256]{2,1,0:T(8,128)(2,1)}, bf16[4,128,256]{2,1,0:T(8,128)(2,1)S(1)}, u32[]{:S(2)}, u32[]{:S(2)}) %collective-permute-start.8) | collective-permute-done | bytes 262176 | tf_op jit(solution)/shard_map/ppermute | solution.py:337
  59.7 15.4 %collective-permute-done.9.refs_3_ = bf16[4,128,256]{2,1,0:T(8,128)(2,1)S(1)} collective-permute-done((bf16[4,128,256]{2,1,0:T(8,128)(2,1)}, bf16[4,128,256]{2,1,0:T(8,128)(2,1)S(1)}, u32[]{:S(2)}, u32[]{:S(2)}) %collective-permute-start.9) | collective-permute-done | bytes 262176 | tf_op jit(solution)/shard_map/ppermute | solution.py:337
  76.6 13.8 %collective-permute-done.16.refs_2_ = bf16[4,128,256]{2,1,0:T(8,128)(2,1)S(1)} collective-permute-done((bf16[4,128,256]{2,1,0:T(8,128)(2,1)}, bf16[4,128,256]{2,1,0:T(8,128)(2,1)S(1)}, u32[]{:S(2)}, u32[]{:S(2)}) %collective-permute-start.16) | collective-permute-done | bytes 262176 | tf_op jit(solution)/shard_map/ppermute | solution.py:337
  92.5 5.1 %collective-permute-done.17.refs_3_ = bf16[4,128,256]{2,1,0:T(8,128)(2,1)S(1)} collective-permute-done((bf16[4,128,256]{2,1,0:T(8,128)(2,1)}, bf16[4,128,256]{2,1,0:T(8,128)(2,1)S(1)}, u32[]{:S(2)}, u32[]{:S(2)}) %collective-permute-start.17) | collective-permute-done | bytes 262176 | tf_op jit(solution)/shard_map/ppermute | solution.py:337
  102.8 4.5 %collective-permute-done.38.refs_3_ = bf16[4,128,256]{2,1,0:T(8,128)(2,1)S(1)} collective-permute-done((bf16[4,128,256]{2,1,0:T(8,128)(2,1)}, bf16[4,128,256]{2,1,0:T(8,128)(2,1)S(1)}, u32[]{:S(2)}, u32[]{:S(2)}) %collective-permute-start.38) | collective-permute-done | bytes 262176 | tf_op jit(solution)/shard_map/ppermute | solution.py:337
  111.6 4.9 %collective-permute-done.10.refs_1_ = bf16[4,128,256]{2,1,0:T(8,128)(2,1)S(1)} collective-permute-done((bf16[4,128,256]{2,1,0:T(8,128)(2,1)S(1)}, bf16[4,128,256]{2,1,0:T(8,128)(2,1)S(1)}, u32[]{:S(2)}, u32[]{:S(2)}) %collective-permute-start.10) | collective-permute-done | bytes 262176 | tf_op jit(solution)/shard_map/ppermute | solution.py:340
  117.5 4.9 %collective-permute-done.20.refs_3_ = bf16[4,128,256]{2,1,0:T(8,128)(2,1)S(1)} collective-permute-done((bf16[4,128,256]{2,1,0:T(8,128)(2,1)S(1)}, bf16[4,128,256]{2,1,0:T(8,128)(2,1)S(1)}, u32[]{:S(2)}, u32[]{:S(2)}) %collective-permute-start.20) | collective-permute-done | bytes 262176 | tf_op jit(solution)/shard_map/ppermute | solution.py:340
  129.0 4.5 %collective-permute-done.18.refs_1_ = bf16[4,128,256]{2,1,0:T(8,128)(2,1)S(1)} collective-permute-done((bf16[4,128,256]{2,1,0:T(8,128)(2,1)S(1)}, bf16[4,128,256]{2,1,0:T(8,128)(2,1)S(1)}, u32[]{:S(2)}, u32[]{:S(2)}) %collective-permute-start.18) | collective-permute-done | bytes 262176 | tf_op jit(solution)/shard_map/ppermute | solution.py:340
  146.7 6.1 %x_pass.4 = (bf16[4,128,512]{2,1,0:T(8,128)(2,1)S(1)}, bf16[4,128,512]{2,1,0:T(8,128)(2,1)S(1)}, bf16[1024,512]{1,0:T(8,128)(2,1)S(1)}) custom-call(s32[2]{0:T(128)S(1)} %pad_add_fusion.1.at_ref, f32[4]{0:T(128)S(1)} %copy-done.12, bf16[3,4,2,128,1024]{4,3,2,1,0:T(8,128)(2,1)S(1)} %bitcast.94, bf16[4,128,256]{2,1,0:T(8,128)(2,1)S(1)} %get-tuple-element.64.refs_0_, ...), custom_call_target="tpu_custom_call" | custom-call | flops 3221225472 | bytes 8388608 | tf_op jit(solution)/shard_map/x_pass/pallas_call | solution.py:139
  152.8 6.1 %x_pass.6 = (bf16[4,128,512]{2,1,0:T(8,128)(2,1)S(1)}, bf16[4,128,512]{2,1,0:T(8,128)(2,1)S(1)}) custom-call(s32[2]{0:T(128)S(1)} %pad_add_fusion.1.at_ref, f32[4]{0:T(128)S(1)} %copy-done.12, bf16[3,4,2,128,1024]{4,3,2,1,0:T(8,128)(2,1)S(1)} %bitcast.97, bf16[4,128,256]{2,1,0:T(8,128)(2,1)S(1)} %get-tuple-element.71.refs_0_, ...), custom_call_target="tpu_custom_call" | custom-call | flops 3221225472 | bytes 8388608 | tf_op jit(solution)/shard_map/x_pass/pallas_call | solution.py:139
  159.0 6.1 %x_pass.7 = (bf16[4,128,512]{2,1,0:T(8,128)(2,1)S(1)}, bf16[4,128,512]{2,1,0:T(8,128)(2,1)S(1)}) custom-call(s32[2]{0:T(128)S(1)} %pad_add_fusion.1.at_ref, f32[4]{0:T(128)S(1)} %copy-done.12, bf16[3,4,2,128,1024]{4,3,2,1,0:T(8,128)(2,1)S(1)} %bitcast.98, bf16[4,128,256]{2,1,0:T(8,128)(2,1)S(1)} %get-tuple-element.96.refs_0_, ...), custom_call_target="tpu_custom_call" | custom-call | flops 3221225472 | bytes 8388608 | tf_op jit(solution)/shard_map/x_pass/pallas_call | solution.py:139
  169.2 5.7 %y_pass.4 = (bf16[4,128,256]{2,1,0:T(8,128)(2,1)S(1)}, bf16[4,128,256]{2,1,0:T(8,128)(2,1)S(1)}, bf16[4,128,256]{2,1,0:T(8,128)(2,1)S(1)}, bf16[4,128,256]{2,1,0:T(8,128)(2,1)S(1)}, bf16[512,1024]{1,0:T(8,128)(2,1)S(1)}) custom-call(s32[2]{0:T(128)S(1)} %pad_add_fusion.1.at_ref, f32[4]{0:T(128)S(1)} %copy-done.12, bf16[3,1024,1024]{2,1,0:T(8,128)(2,1)S(1)} %copy-done.1, ...), custom_call_target="tpu_custom_call" | custom-call | flops 3221225472 | bytes 8388608 | tf_op jit(solution)/shard_map/y_pass/pallas_call | solution.py:213
  178.4 5.8 %y_pass.7 = (bf16[4,128,256]{2,1,0:T(8,128)(2,1)S(1)}, bf16[4,128,256]{2,1,0:T(8,128)(2,1)S(1)}, bf16[4,128,256]{2,1,0:T(8,128)(2,1)S(1)}, bf16[4,128,256]{2,1,0:T(8,128)(2,1)S(1)}) custom-call(s32[2]{0:T(128)S(1)} %pad_add_fusion.1.at_ref, f32[4]{0:T(128)S(1)} %copy-done.12, bf16[3,1024,1024]{2,1,0:T(8,128)(2,1)S(1)} %copy-done.2, ...), custom_call_target="tpu_custom_call" | custom-call | flops 3221225472 | bytes 8388608 | tf_op jit(solution)/shard_map/y_pass/pallas_call | solution.py:213
  187.7 6.9 %x_pass.5 = (bf16[4,128,512]{2,1,0:T(8,128)(2,1)S(1)}, bf16[4,128,512]{2,1,0:T(8,128)(2,1)}) custom-call(s32[2]{0:T(128)S(1)} %pad_add_fusion.1.at_ref, f32[4]{0:T(128)S(1)} %copy-done.12, bf16[3,4,2,128,1024]{4,3,2,1,0:T(8,128)(2,1)S(1)} %bitcast.99, bf16[4,128,256]{2,1,0:T(8,128)(2,1)S(1)} %get-tuple-element.60.refs_0_, ...), custom_call_target="tpu_custom_call" | custom-call | flops 3221225472 | bytes 8388608 | tf_op jit(solution)/shard_map/x_pass/pallas_call | solution.py:139
  206.3 5.8 %y_pass.6 = (bf16[4,128,256]{2,1,0:T(8,128)(2,1)S(1)}, bf16[4,128,256]{2,1,0:T(8,128)(2,1)S(1)}, bf16[4,128,256]{2,1,0:T(8,128)(2,1)S(1)}, bf16[4,128,256]{2,1,0:T(8,128)(2,1)S(1)}) custom-call(s32[2]{0:T(128)S(1)} %pad_add_fusion.1.at_ref, f32[4]{0:T(128)S(1)} %copy-done.12, bf16[3,1024,1024]{2,1,0:T(8,128)(2,1)S(1)} %copy-done.3, ...), custom_call_target="tpu_custom_call" | custom-call | flops 3221225472 | bytes 8388608 | tf_op jit(solution)/shard_map/y_pass/pallas_call | solution.py:213
  213.9 6.9 %collective-permute-done.48.refs_2_ = bf16[4,128,256]{2,1,0:T(8,128)(2,1)S(1)} collective-permute-done((bf16[4,128,256]{2,1,0:T(8,128)(2,1)S(1)}, bf16[4,128,256]{2,1,0:T(8,128)(2,1)S(1)}, u32[]{:S(2)}, u32[]{:S(2)}) %collective-permute-start.48) | collective-permute-done | bytes 262176 | tf_op jit(solution)/shard_map/ppermute | solution.py:337
  220.8 5.0 %collective-permute-done.49.refs_3_ = bf16[4,128,256]{2,1,0:T(8,128)(2,1)S(1)} collective-permute-done((bf16[4,128,256]{2,1,0:T(8,128)(2,1)S(1)}, bf16[4,128,256]{2,1,0:T(8,128)(2,1)S(1)}, u32[]{:S(2)}, u32[]{:S(2)}) %collective-permute-start.49) | collective-permute-done | bytes 262176 | tf_op jit(solution)/shard_map/ppermute | solution.py:337
  242.3 6.4 %y_pass.5 = (bf16[4,128,256]{2,1,0:T(8,128)(2,1)S(1)}, bf16[4,128,256]{2,1,0:T(8,128)(2,1)}, bf16[4,128,256]{2,1,0:T(8,128)(2,1)}, bf16[4,128,256]{2,1,0:T(8,128)(2,1)}) custom-call(s32[2]{0:T(128)S(1)} %pad_add_fusion.1.at_ref, f32[4]{0:T(128)S(1)} %copy-done.12, bf16[3,1024,1024]{2,1,0:T(8,128)(2,1)S(1)} %copy-done.4, bf16[4,128,512]{2,1,0:T(8,128)(2,1)S(1)} %copy-done.16, ...), custom_call_target="tpu_custom_call" | custom-call | flops 3221225472 | bytes 8388608 | tf_op jit(solution)/shard_map/y_pass/pallas_call | solution.py:213
  254.4 4.8 %collective-permute-done.51.refs_2_ = bf16[4,128,256]{2,1,0:T(8,128)(2,1)S(1)} collective-permute-done((bf16[4,128,256]{2,1,0:T(8,128)(2,1)}, bf16[4,128,256]{2,1,0:T(8,128)(2,1)S(1)}, u32[]{:S(2)}, u32[]{:S(2)}) %collective-permute-start.51) | collective-permute-done | bytes 262176 | tf_op jit(solution)/shard_map/ppermute | solution.py:340
  281.5 15.8 %collective-permute-done.35.refs_3_ = bf16[4,128,256]{2,1,0:T(8,128)(2,1)S(1)} collective-permute-done((bf16[4,128,256]{2,1,0:T(8,128)(2,1)}, bf16[4,128,256]{2,1,0:T(8,128)(2,1)S(1)}, u32[]{:S(2)}, u32[]{:S(2)}) %collective-permute-start.35) | collective-permute-done | bytes 262176 | tf_op jit(solution)/shard_map/ppermute | solution.py:337
  299.7 14.4 %collective-permute-done.54.refs_2_ = bf16[4,128,256]{2,1,0:T(8,128)(2,1)S(1)} collective-permute-done((bf16[4,128,256]{2,1,0:T(8,128)(2,1)}, bf16[4,128,256]{2,1,0:T(8,128)(2,1)S(1)}, u32[]{:S(2)}, u32[]{:S(2)}) %collective-permute-start.54) | collective-permute-done | bytes 262176 | tf_op jit(solution)/shard_map/ppermute | solution.py:337
  319.7 4.3 %collective-permute-start.62 = (f32[80,8]{1,0:T(8,128)S(1)}, f32[80,8]{1,0:T(8,128)S(1)}, u32[]{:S(2)}, u32[]{:S(2)}) collective-permute-start(f32[80,8]{1,0:T(8,128)S(1)} %get-tuple-element.155), channel_id=1, source_target_pairs={{0,1},{1,2},{2,3},{4,5},{5,6},{6,7},{8,9},{9,10},{10,11},{12,13},{... | collective-permute-start | bytes 7688 | tf_op jit(solution)/shard_map/ppermute | solution.py:36
  (240 shorter events, 161.0 us)
Async XLA Ops:
  5.5 33.8 %collective-permute-start = (bf16[4,128,256]{2,1,0:T(8,128)(2,1)}, bf16[4,128,256]{2,1,0:T(8,128)(2,1)S(1)}, u32[]{:S(2)}, u32[]{:S(2)}) collective-permute-start(bf16[4,128,256]{2,1,0:T(8,128)(2,1)} %get-tuple-element.136), channel_id=1, source_target_pairs={{0,1},{1,0},{2,3},{3,2},{4,5},{5,4},{6,7},{7,6},{8,9},{9,8},{10,11... | collective-permute-start | bytes 786440 | tf_op jit(solution)/shard_map/ppermute | solution.py:337
  5.5 35.0 %collective-permute-start.1 = (bf16[4,128,256]{2,1,0:T(8,128)(2,1)}, bf16[4,128,256]{2,1,0:T(8,128)(2,1)S(1)}, u32[]{:S(2)}, u32[]{:S(2)}) collective-permute-start(bf16[4,128,256]{2,1,0:T(8,128)(2,1)} %get-tuple-element.135), channel_id=1, source_target_pairs={{0,2},{1,3},{2,0},{3,1},{4,6},{5,7},{6,4},{7,5},{8,10},{9,11},{10,... | collective-permute-start | bytes 786440 | tf_op jit(solution)/shard_map/ppermute | solution.py:337
  8.6 34.3 %collective-permute-start.2 = (bf16[4,128,256]{2,1,0:T(8,128)(2,1)}, bf16[4,128,256]{2,1,0:T(8,128)(2,1)S(1)}, u32[]{:S(2)}, u32[]{:S(2)}) collective-permute-start(bf16[4,128,256]{2,1,0:T(8,128)(2,1)} %get-tuple-element.134), channel_id=1, source_target_pairs={{0,3},{1,2},{2,1},{3,0},{4,7},{5,6},{6,5},{7,4},{8,11},{9,10},{10,... | collective-permute-start | bytes 786440 | tf_op jit(solution)/shard_map/ppermute | solution.py:337
  39.3 35.8 %collective-permute-start.9 = (bf16[4,128,256]{2,1,0:T(8,128)(2,1)}, bf16[4,128,256]{2,1,0:T(8,128)(2,1)S(1)}, u32[]{:S(2)}, u32[]{:S(2)}) collective-permute-start(bf16[4,128,256]{2,1,0:T(8,128)(2,1)} %get-tuple-element.130), channel_id=1, source_target_pairs={{0,3},{1,2},{2,1},{3,0},{4,7},{5,6},{6,5},{7,4},{8,11},{9,10},{10,... | collective-permute-start | bytes 786440 | tf_op jit(solution)/shard_map/ppermute | solution.py:337
  40.5 34.6 %collective-permute-start.15 = (bf16[4,128,256]{2,1,0:T(8,128)(2,1)}, bf16[4,128,256]{2,1,0:T(8,128)(2,1)S(1)}, u32[]{:S(2)}, u32[]{:S(2)}) collective-permute-start(bf16[4,128,256]{2,1,0:T(8,128)(2,1)} %get-tuple-element.128), channel_id=1, source_target_pairs={{0,1},{1,0},{2,3},{3,2},{4,5},{5,4},{6,7},{7,6},{8,9},{9,8},{10,11... | collective-permute-start | bytes 786440 | tf_op jit(solution)/shard_map/ppermute | solution.py:337
  42.8 47.6 %collective-permute-start.16 = (bf16[4,128,256]{2,1,0:T(8,128)(2,1)}, bf16[4,128,256]{2,1,0:T(8,128)(2,1)S(1)}, u32[]{:S(2)}, u32[]{:S(2)}) collective-permute-start(bf16[4,128,256]{2,1,0:T(8,128)(2,1)} %get-tuple-element.127), channel_id=1, source_target_pairs={{0,2},{1,3},{2,0},{3,1},{4,6},{5,7},{6,4},{7,5},{8,10},{9,11},{10,... | collective-permute-start | bytes 786440 | tf_op jit(solution)/shard_map/ppermute | solution.py:337
  49.1 48.5 %collective-permute-start.17 = (bf16[4,128,256]{2,1,0:T(8,128)(2,1)}, bf16[4,128,256]{2,1,0:T(8,128)(2,1)S(1)}, u32[]{:S(2)}, u32[]{:S(2)}) collective-permute-start(bf16[4,128,256]{2,1,0:T(8,128)(2,1)} %get-tuple-element.126), channel_id=1, source_target_pairs={{0,3},{1,2},{2,1},{3,0},{4,7},{5,6},{6,5},{7,4},{8,11},{9,10},{10,... | collective-permute-start | bytes 786440 | tf_op jit(solution)/shard_map/ppermute | solution.py:337
  56.7 42.1 %collective-permute-start.36 = (bf16[4,128,256]{2,1,0:T(8,128)(2,1)}, bf16[4,128,256]{2,1,0:T(8,128)(2,1)S(1)}, u32[]{:S(2)}, u32[]{:S(2)}) collective-permute-start(bf16[4,128,256]{2,1,0:T(8,128)(2,1)} %get-tuple-element.124), channel_id=1, source_target_pairs={{0,1},{1,0},{2,3},{3,2},{4,5},{5,4},{6,7},{7,6},{8,9},{9,8},{10,11... | collective-permute-start | bytes 786440 | tf_op jit(solution)/shard_map/ppermute | solution.py:337
  75.1 26.5 %collective-permute-start.37 = (bf16[4,128,256]{2,1,0:T(8,128)(2,1)}, bf16[4,128,256]{2,1,0:T(8,128)(2,1)S(1)}, u32[]{:S(2)}, u32[]{:S(2)}) collective-permute-start(bf16[4,128,256]{2,1,0:T(8,128)(2,1)} %get-tuple-element.123), channel_id=1, source_target_pairs={{0,2},{1,3},{2,0},{3,1},{4,6},{5,7},{6,4},{7,5},{8,10},{9,11},{10,... | collective-permute-start | bytes 786440 | tf_op jit(solution)/shard_map/ppermute | solution.py:337
  75.1 32.2 %collective-permute-start.38 = (bf16[4,128,256]{2,1,0:T(8,128)(2,1)}, bf16[4,128,256]{2,1,0:T(8,128)(2,1)S(1)}, u32[]{:S(2)}, u32[]{:S(2)}) collective-permute-start(bf16[4,128,256]{2,1,0:T(8,128)(2,1)} %get-tuple-element.122), channel_id=1, source_target_pairs={{0,3},{1,2},{2,1},{3,0},{4,7},{5,6},{6,5},{7,4},{8,11},{9,10},{10,... | collective-permute-start | bytes 786440 | tf_op jit(solution)/shard_map/ppermute | solution.py:337
  98.9 66.9 %collective-permute-start.3 = (bf16[4,128,256]{2,1,0:T(8,128)(2,1)S(1)}, bf16[4,128,256]{2,1,0:T(8,128)(2,1)S(1)}, u32[]{:S(2)}, u32[]{:S(2)}) collective-permute-start(bf16[4,128,256]{2,1,0:T(8,128)(2,1)S(1)} %get-tuple-element.61), channel_id=1, source_target_pairs={{0,8},{4,12},{8,0},{12,4},{16,24},{20,28},{24,16},{28,20},{1,9},{5... | collective-permute-start | bytes 786440 | tf_op jit(solution)/shard_map/ppermute | solution.py:340
  101.7 42.2 %collective-permute-start.4 = (bf16[4,128,256]{2,1,0:T(8,128)(2,1)S(1)}, bf16[4,128,256]{2,1,0:T(8,128)(2,1)S(1)}, u32[]{:S(2)}, u32[]{:S(2)}) collective-permute-start(bf16[4,128,256]{2,1,0:T(8,128)(2,1)S(1)} %get-tuple-element.62), channel_id=1, source_target_pairs={{0,16},{4,20},{8,24},{12,28},{16,0},{20,4},{24,8},{28,12},{1,17},{... | collective-permute-start | bytes 786440 | tf_op jit(solution)/shard_map/ppermute | solution.py:340
  116.6 26.7 %collective-permute-start.5 = (bf16[4,128,256]{2,1,0:T(8,128)(2,1)S(1)}, bf16[4,128,256]{2,1,0:T(8,128)(2,1)S(1)}, u32[]{:S(2)}, u32[]{:S(2)}) collective-permute-start(bf16[4,128,256]{2,1,0:T(8,128)(2,1)S(1)} %get-tuple-element.63), channel_id=1, source_target_pairs={{0,24},{4,28},{8,16},{12,20},{16,8},{20,12},{24,0},{28,4},{1,25},{... | collective-permute-start | bytes 786440 | tf_op jit(solution)/shard_map/ppermute | solution.py:340
  165.9 37.6 %collective-permute-start.29 = (bf16[4,128,512]{2,1,0:T(8,128)(2,1)S(1)}, bf16[4,128,512]{2,1,0:T(8,128)(2,1)S(1)}, u32[]{:S(2)}, u32[]{:S(2)}) collective-permute-start(bf16[4,128,512]{2,1,0:T(8,128)(2,1)S(1)} %get-tuple-element.87), channel_id=1, source_target_pairs={{0,4},{4,0},{8,12},{12,8},{16,20},{20,16},{24,28},{28,24},{1,5},{5... | collective-permute-start | bytes 1572872 | tf_op jit(solution)/shard_map/ppermute | solution.py:343
  194.6 39.8 %collective-permute-start.14 = (bf16[4,128,512]{2,1,0:T(8,128)(2,1)}, bf16[4,128,512]{2,1,0:T(8,128)(2,1)S(1)}, u32[]{:S(2)}, u32[]{:S(2)}) collective-permute-start(bf16[4,128,512]{2,1,0:T(8,128)(2,1)} %get-tuple-element.70), channel_id=1, source_target_pairs={{0,4},{4,0},{8,12},{12,8},{16,20},{20,16},{24,28},{28,24},{1,5},{5... | collective-permute-start | bytes 1572872 | tf_op jit(solution)/shard_map/ppermute | solution.py:343
  227.2 37.6 %all-to-all-start.1 = ((bf16[32,16,256]{2,1,0:T(8,128)(2,1)}), bf16[32,16,256]{2,1,0:T(8,128)(2,1)}, u32[]{:S(2)}, u32[]{:S(2)}) async-start(bf16[32,16,256]{2,1,0:T(8,128)(2,1)} %bitcast.50), calls=%async_computation.1 | async-start | bytes 524288 | tf_op jit(solution)/shard_map/all_to_all | solution.py:412
  234.3 24.8 %collective-permute-start.51 = (bf16[4,128,256]{2,1,0:T(8,128)(2,1)}, bf16[4,128,256]{2,1,0:T(8,128)(2,1)S(1)}, u32[]{:S(2)}, u32[]{:S(2)}) collective-permute-start(bf16[4,128,256]{2,1,0:T(8,128)(2,1)} %copy-done.6), channel_id=1, source_target_pairs={{0,16},{4,20},{8,24},{12,28},{16,0},{20,4},{24,8},{28,12},{1,17},{... | collective-permute-start | bytes 786440 | tf_op jit(solution)/shard_map/ppermute | solution.py:340
  265.9 31.4 %collective-permute-start.35 = (bf16[4,128,256]{2,1,0:T(8,128)(2,1)}, bf16[4,128,256]{2,1,0:T(8,128)(2,1)S(1)}, u32[]{:S(2)}, u32[]{:S(2)}) collective-permute-start(bf16[4,128,256]{2,1,0:T(8,128)(2,1)} %copy-done.8), channel_id=1, source_target_pairs={{0,3},{1,2},{2,1},{3,0},{4,7},{5,6},{6,5},{7,4},{8,11},{9,10},{10,... | collective-permute-start | bytes 786440 | tf_op jit(solution)/shard_map/ppermute | solution.py:337
  269.9 27.3 %collective-permute-start.53 = (bf16[4,128,256]{2,1,0:T(8,128)(2,1)}, bf16[4,128,256]{2,1,0:T(8,128)(2,1)S(1)}, u32[]{:S(2)}, u32[]{:S(2)}) collective-permute-start(bf16[4,128,256]{2,1,0:T(8,128)(2,1)} %copy-done.11), channel_id=1, source_target_pairs={{0,1},{1,0},{2,3},{3,2},{4,5},{5,4},{6,7},{7,6},{8,9},{9,8},{10,11... | collective-permute-start | bytes 786440 | tf_op jit(solution)/shard_map/ppermute | solution.py:337
  276.7 37.4 %collective-permute-start.54 = (bf16[4,128,256]{2,1,0:T(8,128)(2,1)}, bf16[4,128,256]{2,1,0:T(8,128)(2,1)S(1)}, u32[]{:S(2)}, u32[]{:S(2)}) collective-permute-start(bf16[4,128,256]{2,1,0:T(8,128)(2,1)} %copy-done.10), channel_id=1, source_target_pairs={{0,2},{1,3},{2,0},{3,1},{4,6},{5,7},{6,4},{7,5},{8,10},{9,11},{10,... | collective-permute-start | bytes 786440 | tf_op jit(solution)/shard_map/ppermute | solution.py:337
  279.2 40.5 %collective-permute-start.55 = (bf16[4,128,256]{2,1,0:T(8,128)(2,1)}, bf16[4,128,256]{2,1,0:T(8,128)(2,1)S(1)}, u32[]{:S(2)}, u32[]{:S(2)}) collective-permute-start(bf16[4,128,256]{2,1,0:T(8,128)(2,1)} %copy-done.9), channel_id=1, source_target_pairs={{0,3},{1,2},{2,1},{3,0},{4,7},{5,6},{6,5},{7,4},{8,11},{9,10},{10,... | collective-permute-start | bytes 786440 | tf_op jit(solution)/shard_map/ppermute | solution.py:337
  280.4 46.7 %collective-permute-start.26 = (bf16[4,128,256]{2,1,0:T(8,128)(2,1)S(1)}, bf16[4,128,256]{2,1,0:T(8,128)(2,1)S(1)}, u32[]{:S(2)}, u32[]{:S(2)}) collective-permute-start(bf16[4,128,256]{2,1,0:T(8,128)(2,1)S(1)} %get-tuple-element.83), channel_id=1, source_target_pairs={{0,1},{1,0},{2,3},{3,2},{4,5},{5,4},{6,7},{7,6},{8,9},{9,8},{10,11... | collective-permute-start | bytes 786440 | tf_op jit(solution)/shard_map/ppermute | solution.py:337
  297.3 29.8 %collective-permute-start.27 = (bf16[4,128,256]{2,1,0:T(8,128)(2,1)S(1)}, bf16[4,128,256]{2,1,0:T(8,128)(2,1)S(1)}, u32[]{:S(2)}, u32[]{:S(2)}) collective-permute-start(bf16[4,128,256]{2,1,0:T(8,128)(2,1)S(1)} %get-tuple-element.84), channel_id=1, source_target_pairs={{0,2},{1,3},{2,0},{3,1},{4,6},{5,7},{6,4},{7,5},{8,10},{9,11},{10,... | collective-permute-start | bytes 786440 | tf_op jit(solution)/shard_map/ppermute | solution.py:337
  297.3 33.0 %collective-permute-start.28 = (bf16[4,128,256]{2,1,0:T(8,128)(2,1)S(1)}, bf16[4,128,256]{2,1,0:T(8,128)(2,1)S(1)}, u32[]{:S(2)}, u32[]{:S(2)}) collective-permute-start(bf16[4,128,256]{2,1,0:T(8,128)(2,1)S(1)} %get-tuple-element.85), channel_id=1, source_target_pairs={{0,3},{1,2},{2,1},{3,0},{4,7},{5,6},{6,5},{7,4},{8,11},{9,10},{10,... | collective-permute-start | bytes 786440 | tf_op jit(solution)/shard_map/ppermute | solution.py:337
  (68 other events, 1180.1 us)

commit v2 on v0

v2 whole, which is shorter than its diff:
```python
import jax
import jax.numpy as jnp
from jax import lax
from jax.experimental import pallas as pl
from jax.experimental.pallas import tpu as pltpu
from jax.sharding import PartitionSpec as P

COND_STEPS = 8

time_step = 0.25
wall_gain = 0.5
diffusion_rate = 0.24
source_gain = 0.1

U, V, W, THETA = 0, 1, 2, 3
VMEM_BYTES = 20 * 1024 * 1024

smem = pl.BlockSpec(memory_space=pltpu.SMEM)
anywhere = pl.BlockSpec(memory_space=pl.ANY)


def with_halo(block, sides, width):
    for axis, dim in sides:
        count = lax.axis_size(axis)
        forward = [(i, i + 1) for i in range(count - 1)]
        backward = [(target, source) for source, target in forward]
        low = lax.ppermute(
            lax.slice_in_dim(block, block.shape[dim] - width, None, axis=dim), axis, forward
        )
        high = lax.ppermute(lax.slice_in_dim(block, 0, width, axis=dim), axis, backward)
        block = jnp.concatenate([low, block, high], axis=dim)
    return block


def in_order(part):
    return part % 128 == 0


class Chain:
    def __init__(self, at):
        self.at = at
        self.last = []

    def run(
        self, name, kernel, args, in_specs, out_specs, out_shape, grid=(1,), scratch=(), aliases=None, flops=0
    ):
        count = len(args)
        tokens = [x for x in self.last if not any(x is y for y in args)]

        def body(at_ref, *refs):
            kernel(at_ref, *refs[:count], *refs[count + len(tokens) :])

        moved = sum(x.size * x.dtype.itemsize for x in out_shape)
        outs = pl.pallas_call(
            body,
            grid_spec=pltpu.PrefetchScalarGridSpec(
                num_scalar_prefetch=1,
                grid=grid,
                in_specs=list(in_specs) + [anywhere] * len(tokens),
                out_specs=out_specs,
                scratch_shapes=list(scratch),
            ),
            out_shape=out_shape,
            input_output_aliases=aliases or {},
            compiler_params=pltpu.CompilerParams(vmem_limit_bytes=VMEM_BYTES),
            cost_estimate=pl.CostEstimate(flops=flops, bytes_accessed=2 * moved, transcendentals=0),
            name=name,
        )(self.at, *args, *tokens)
        self.last = [outs[0]]
        return outs


def whole(shape):
    return pl.BlockSpec(shape, lambda i, at: (0,) * len(shape))


def like(pieces):
    return [whole(piece.shape) for piece in pieces]


def cut(chain, fields, which, across_px, across_py):
    layers, xb, yb = fields.shape[1:]
    groups = layers // across_py
    members = across_px // groups
    part = yb // members

    def kernel(at, *refs):
        for n in range(len(which)):
            for g in range(groups):
                for k in range(members):
                    refs[-1][g * members + k, 0, n] = refs[n][0, g, :, k * part : (k + 1) * part]

    def field(f):
        return pl.BlockSpec((1, groups, xb, yb), lambda i, at: (f, i, 0, 0))

    shape = (across_px, across_py, len(which), xb, part)
    return chain.run(
        "cut",
        kernel,
        [fields] * len(which),
        [field(f) for f in which],
        [pl.BlockSpec((across_px, 1) + shape[2:], lambda i, at: (0, i, 0, 0, 0))],
        [jax.ShapeDtypeStruct(shape, fields.dtype)],
        grid=(across_py,),
    )[0]


def x_pass(chain, field, operators, viscosity, arrived, n, members, speed):
    across_px, across_py, _, xb, part = arrived.shape
    width = across_py * part
    length = across_px * xb
    rows = xb // members
    many = min(across_px, max(1, 256 // rows))
    steps = across_px // many
    first = field == U

    def kernel(at, visc_ref, op_ref, arrived_ref, *refs):
        if first:
            outs, lines = refs[:-1], refs[-1]
        else:
            speed_ref, outs, lines = refs[0], refs[1:-1], refs[-1]
        step = pl.program_id(0)
        turn, place = step // steps, step % steps

        @pl.when(step == 0)
        def _():
            for x in range(across_px):
                for y in range(across_py):
                    lines[x * xb : (x + 1) * xb, y * part : (y + 1) * part] = arrived_ref[x, y, 0]

        result = jnp.dot(
            op_ref[...].reshape(3 * many * rows, length), lines[...], preferred_element_type=jnp.float32
        ).reshape(3, many, rows, width)
        for c in range(many):
            if first:
                row = (place * many + c) * xb + (at[1] ^ turn) * rows
                u = lines[pl.ds(pl.multiple_of(row, rows), rows), :]
            else:
                u = speed_ref[c, 0]
            value = result[2, c] + time_step * (
                -u.astype(jnp.float32) * result[0, c] + visc_ref[field] * result[1, c]
            )
            value = value.astype(jnp.bfloat16)
            for r in range(members):

                @pl.when(turn == r)
                def _():
                    outs[r][c] = value

    def out_block(r):
        return pl.BlockSpec(
            (many, rows, width), lambda i, at: (jnp.clip(i - r * steps, 0, steps - 1), 0, 0)
        )

    def place_of(i, at):
        return i % steps, at[1] ^ (i // steps), 0, 0

    in_specs = [
        smem,
        pl.BlockSpec((3, many, 1, rows, length), lambda i, at: (0,) + place_of(i, at)),
        pl.BlockSpec((across_px, across_py, 1, xb, part), lambda i, at: (0, 0, n, 0, 0)),
    ]
    args = [viscosity, operators.reshape(3, across_px, members, rows, length), arrived]
    out_specs = [out_block(r) for r in range(members)]
    out_shape = [jax.ShapeDtypeStruct((across_px, rows, width), jnp.bfloat16)] * members
    scratch = []
    if first:
        out_specs.append(whole((length, width)))
        out_shape.append(jax.ShapeDtypeStruct((length, width), jnp.bfloat16))
    else:
        in_specs.append(pl.BlockSpec((many, 1, rows, width), place_of))
        args.append(speed.reshape(across_px, members, rows, width))
        scratch = [pltpu.VMEM((length, width), jnp.bfloat16)]
    outs = chain.run(
        "x_pass",
        kernel,
        args,
        in_specs,
        out_specs,
        out_shape,
        grid=(steps * members,),
        scratch=scratch,
        flops=6 * length * length * width,
    )
    return outs[:members], outs[members] if first else speed


def y_pass(chain, field, operators, viscosity, parts, speed, buffer, n, shape):
    across_px, rows, width = parts[0].shape
    members = len(parts)
    yb = shape[-1]
    part = yb // members
    length = width * members
    blocks = length // yb
    first = field == V
    extra = [] if buffer is None else [buffer]

    def kernel(at, visc_ref, op_ref, *refs):
        part_refs, rest = refs[:members], refs[members:]
        if first:
            out, speed_ref, lines = rest[-3:]
        else:
            speed_ref, out, lines = rest[0], rest[-2], rest[-1]
        step = pl.program_id(0)

        @pl.when(step == 0)
        def _():
            for r in range(members):
                values = part_refs[r][...].reshape(across_px * rows, width)
                if in_order(part):
                    for y in range(blocks):
                        start = pl.multiple_of(y * yb + (at[1] ^ r) * part, part)
                        lines[:, pl.ds(start, part)] = values[:, y * part : (y + 1) * part]
                else:
                    lines[:, pl.ds(pl.multiple_of((at[1] ^ r) * width, width), width)] = values
            if first:
                for y in range(blocks):
                    if in_order(part):
                        speed_ref[y] = lines[:, y * yb : (y + 1) * yb]
                    else:
                        for k in range(members):
                            start = k * width + y * part
                            speed_ref[y, :, k * part : (k + 1) * part] = lines[:, start : start + part]

        result = lax.dot_general(
            lines[...],
            op_ref[...].reshape(3 * yb, length),
            (((1,), (1,)), ((), ())),
            preferred_element_type=jnp.float32,
        )
        v = speed_ref[step if first else 0]
        value = result[:, 2 * yb :] + time_step * (
            -v.astype(jnp.float32) * result[:, :yb] + visc_ref[field] * result[:, yb : 2 * yb]
        )
        out[:, 0, 0] = value.astype(jnp.bfloat16).reshape(across_px, rows, yb)

    in_specs = [smem, pl.BlockSpec((3, yb, length), lambda i, at: (0, i, 0))] + like(parts)
    args = [viscosity, operators, *parts]
    out_specs = [pl.BlockSpec((across_px, 1, 1, rows, yb), lambda i, at: (0, i, n, 0, 0))]
    out_shape = [jax.ShapeDtypeStruct(shape, jnp.bfloat16)]
    if first:
        out_specs.append(whole((blocks, across_px * rows, yb)))
        out_shape.append(jax.ShapeDtypeStruct((blocks, across_px * rows, yb), jnp.bfloat16))
    else:
        in_specs.append(pl.BlockSpec((1, across_px * rows, yb), lambda i, at: (i, 0, 0)))
        args.append(speed)
    outs = chain.run(
        "y_pass",
        kernel,
        args + extra,
        in_specs + [anywhere] * len(extra),
        out_specs,
        out_shape,
        grid=(blocks,),
        scratch=[pltpu.VMEM((across_px * rows, length), jnp.bfloat16)],
        aliases={1 + len(args): 0} if extra else {},
        flops=6 * length * length * across_px * rows,
    )
    return outs[0], outs[1] if first else speed


def put(chain, buffer, arrived, which, shape):
    across_px, across_py, many, rows, yb = arrived.shape
    layers, xb = shape[1:3]
    groups = layers // across_py
    members = across_px // groups

    def kernel(at, arrived_ref, *refs):
        for g in range(groups):
            for k in range(members):
                refs[-1][0, g, k * rows : (k + 1) * rows] = arrived_ref[g * members + k, 0, 0]

    extra = [] if buffer is None else [buffer]
    first, stride = which[0], which[-1] - which[0]
    return chain.run(
        "put",
        kernel,
        [arrived, *extra],
        [pl.BlockSpec((across_px, 1, 1, rows, yb), lambda n, i, at: (0, i, n, 0, 0))]
        + [anywhere] * len(extra),
        [pl.BlockSpec((1, groups, xb, yb), lambda n, i, at: (first + n * stride, i, 0, 0))],
        [jax.ShapeDtypeStruct(shape, arrived.dtype)],
        grid=(many, across_py),
        aliases={2: 0} if extra else {},
    )[0]


def wall_lines(chain, arrived, n, line, slot, capacity):
    across_px, across_py, _, rows, yb = arrived.shape
    count, span = line.shape[0], across_px * across_py * rows
    slots = across_px * across_py * capacity

    def kernel(at, line_ref, slot_ref, arrived_ref, *refs):
        chosen = line_ref[...] == lax.broadcasted_iota(jnp.int32, (count, span), 1)
        flux = jnp.dot(
            chosen.astype(jnp.float32).astype(jnp.bfloat16),
            arrived_ref[...].reshape(span, yb),
            preferred_element_type=jnp.float32,
        )
        filled = slot_ref[...] == lax.broadcasted_iota(jnp.int32, (slots, count), 0)
        refs[-1][...] = jnp.dot(
            filled.astype(jnp.float32).astype(jnp.bfloat16),
            flux.astype(jnp.bfloat16),
            preferred_element_type=jnp.float32,
        ).reshape(across_px, across_py, capacity, yb)
        for s in range(across_px):
            refs[s][...] = refs[-1][at[7] ^ s].astype(jnp.bfloat16)

    args = [line.reshape(-1, 1), slot.reshape(1, -1)]
    shape = (across_py, capacity, yb)
    return chain.run(
        "wall_lines",
        kernel,
        args + [arrived],
        like(args)
        + [pl.BlockSpec((across_px, across_py, 1, rows, yb), lambda i, at: (0, 0, n, 0, 0))],
        [whole(shape)] * across_px,
        [jax.ShapeDtypeStruct(shape, jnp.bfloat16)] * across_px,
        scratch=[pltpu.VMEM((across_px,) + shape, jnp.float32)],
    )


def wall_columns(chain, pieces):
    across_px, (across_py, capacity, yb) = len(pieces), pieces[0].shape

    def kernel(at, *refs):
        for s in range(across_py):
            for t in range(across_px):
                refs[across_px + s][at[7] ^ t] = refs[t][at[2] ^ s]

    shape = (across_px, capacity, yb)
    return chain.run(
        "wall_columns",
        kernel,
        pieces,
        like(pieces),
        [whole(shape)] * across_py,
        [jax.ShapeDtypeStruct(shape, jnp.bfloat16)] * across_py,
    )


def add_flux(chain, tags, arrived, solid_temp, conductivity):
    rows, columns = solid_temp.shape
    across_py, (across_px, capacity, _) = len(arrived), arrived[0].shape

    def kernel(at, temp_ref, kappa_ref, *refs):
        tag_refs, flux_refs, out = refs[:across_py], refs[across_py:-1], refs[-1]
        out[0] = temp_ref[...]
        out[1] = kappa_ref[...]
        places = lax.broadcasted_iota(jnp.int32, (rows, capacity), 0)
        source = jnp.zeros((rows, columns), jnp.float32)
        for s in range(across_py):
            chosen = [tag_refs[s][at[7] ^ t] == places for t in range(across_px)]
            chosen = jnp.concatenate([c.astype(jnp.float32) for c in chosen], axis=1)
            source = source + jnp.dot(
                chosen.astype(jnp.bfloat16),
                flux_refs[s][...].reshape(across_px * capacity, columns),
                preferred_element_type=jnp.float32,
            )
        out[2] = (wall_gain * source_gain) * source

    args = [solid_temp, conductivity, *tags, *arrived]
    return chain.run(
        "add_flux",
        kernel,
        args,
        like(args),
        [whole((3, rows, columns))],
        [jax.ShapeDtypeStruct((3, rows, columns), jnp.float32)],
    )[0]


def conduct(chain, solid, rows, columns, margin):
    high, wide = solid.shape[1:]

    def kernel(at, solid_ref, out):
        t, kappa, heat = solid_ref[0], solid_ref[1], solid_ref[2]
        row = lax.broadcasted_iota(jnp.int32, (high, wide), 0) + at[3]
        col = lax.broadcasted_iota(jnp.int32, (high, wide), 1) + at[4]
        inside = (row >= 0) & (row < at[5]) & (col >= 0) & (col < at[6])
        moves = ((high - 1, 0), (1, 0), (wide - 1, 1), (1, 1))
        faces = [
            jnp.where(inside, diffusion_rate * 0.5 * (kappa + pltpu.roll(kappa, shift, dim)), 0.0)
            for shift, dim in moves
        ]
        for _ in range(COND_STEPS):
            change = heat
            for face, (shift, dim) in zip(faces, moves):
                change = change + face * (pltpu.roll(t, shift, dim) - t)
            t = t + change
        out[...] = t[margin : margin + rows, margin : margin + columns]

    return chain.run(
        "conduct",
        kernel,
        [solid],
        like([solid]),
        [whole((rows, columns))],
        [jax.ShapeDtypeStruct((rows, columns), jnp.float32)],
    )[0]


def on_device(
    fields,
    x_operators,
    y_operators,
    viscosity,
    wall_tile,
    wall_owner,
    wall_row,
    solid_temp,
    conductivity,
):
    across_px, across_py = lax.axis_size("px"), lax.axis_size("py")
    devices = across_px * across_py
    layers, xb, yb = fields.shape[1:]
    groups = layers // across_py
    members = across_px // groups
    a, b = lax.axis_index("px"), lax.axis_index("py")
    q, m = a // members, a % members
    rows, columns = solid_temp.shape
    margin = COND_STEPS
    at = jnp.stack(
        [
            q,
            m,
            b,
            a * rows - margin,
            b * columns - margin,
            across_px * rows,
            across_py * columns,
            a,
        ]
    ).astype(jnp.int32)
    chain = Chain(at)

    def along(axis, pieces):
        return [pieces[0]] + [
            lax.ppermute(piece, axis, [(i, i ^ s) for i in range(lax.axis_size(axis))])
            for s, piece in enumerate(pieces[1:], 1)
        ]

    def exchange(blocks):
        moved = lax.all_to_all(
            blocks.reshape((devices,) + blocks.shape[2:]),
            ("px", "py"),
            split_axis=0,
            concat_axis=0,
            tiled=True,
        )
        return moved.reshape(blocks.shape)

    lines, half, speeds = {}, {}, {}

    def forward(*which):
        moved = exchange(cut(chain, fields, which, across_px, across_py))
        for n, f in enumerate(which):
            lines[f] = moved, n

    def X(f):
        out, speeds[U] = x_pass(
            chain, f, x_operators, viscosity, *lines[f], members, speeds.get(U)
        )
        half[f] = along("px", out)

    y_columns = y_operators
    if not in_order(yb // members):
        y_columns = y_columns.reshape(3, -1, across_py, members, yb // members)
        y_columns = y_columns.swapaxes(2, 3).reshape(y_operators.shape)

    def Y(f, buffer, n, many):
        shape = (across_px, across_py, many, xb // members, yb)
        buffer, speeds[V] = y_pass(
            chain, f, y_columns, viscosity, half[f], speeds.get(V), buffer, n, shape
        )
        return buffer

    forward(U, V, THETA)
    forward(W)

    count = wall_tile.shape[0]
    owner = wall_owner[:, 0]
    capacity = max(2, 4 * count // devices)
    slots = devices * capacity
    order = jnp.arange(count, dtype=jnp.int32)
    earlier = (owner[:, None] == owner[None, :]) & (order[None, :] < order[:, None])
    slot = owner * capacity + jnp.sum(earlier.astype(jnp.int32), axis=1)
    layer, x = wall_tile // xb, wall_tile % xb
    source = (layer % groups * members + x // (xb // members)) * across_py + layer // groups
    line = source * (xb // members) + x % (xb // members)
    filled = slot[None, :] == jnp.arange(slots, dtype=jnp.int32)[:, None]
    labels = jnp.sum(jnp.where(filled, wall_row[None, :] + 1, 0), axis=1) - 1
    labels = labels.reshape(across_px, across_py, capacity)
    tags = along(
        "px",
        [lax.dynamic_index_in_dim(labels, a ^ s, 0, keepdims=False) for s in range(across_px)],
    )
    tags = along(
        "py",
        [
            jnp.stack([lax.dynamic_index_in_dim(tag, b ^ s, 0) for tag in tags])
            for s in range(across_py)
        ],
    )

    chain.last += tags
    X(U), X(V)
    back = Y(V, None, 0, 2)
    X(THETA)
    back = exchange(Y(THETA, back, 1, 2))
    other = Y(U, None, 0, 2)
    X(W)
    other = exchange(Y(W, other, 1, 2))
    flux = along("px", wall_lines(chain, back, 1, line, slot, capacity))
    new_fields = put(chain, None, back, (V, THETA), fields.shape)
    flux = along("py", wall_columns(chain, flux))
    solid = add_flux(chain, tags, flux, solid_temp, conductivity)
    solid = with_halo(solid, (("px", 1), ("py", 2)), margin)
    solid = jnp.pad(solid, ((0, 0), (0, 0), (0, -solid.shape[2] % 128)))
    new_solid = conduct(chain, solid, rows, columns, margin)
    new_fields = put(chain, new_fields, other, (U, W), fields.shape)
    return new_fields, new_solid


def solution(mesh):
    return jax.shard_map(
        on_device,
        mesh=mesh,
        in_specs=(
            P(None, None, "px", "py"),
            P(),
            P(),
            P(),
            P(("px", "py")),
            P(("px", "py"), None),
            P(("px", "py")),
            P("px", "py"),
            P("px", "py"),
        ),
        out_specs=(P(None, None, "px", "py"), P("px", "py")),
        check_vma=False,
    )
```

time: 493 us -> 270 us (0.55)
  blocking collectives: 105 us -> 0 us
  Pallas kernels: 0 us -> 71 us
  local copies, waits for them, and re-layouts: 88.6 us -> 23.2 us
  waiting for transfers between devices: 167 us -> 110 us
  matrix products: 40 us -> 0 us
  other arithmetic: 33.1 us -> 0.57 us
  starting transfers between devices: 53.1 us -> 59 us
    all_to_all x4, waiting for transfers between devices: 160 us -> 50.5 us  [exchange(): lax.all_to_all(blocks.reshape((devices,) + blocks.shape[2:]), ('px', 'py'...]
    all_to_all x2 -> x0, blocking collectives: 105 us -> none  [the longest x1 52.7 us: on_device(): lax.all_to_all(fields, 'px', split_axis=1, concat_axis=2, tiled=True)]
    pallas_call x0 -> x16, Pallas kernels: none -> 71 us  [run(): pl.pallas_call(body, grid_spec=pltpu.PrefetchScalarGridSpec(num_scalar_pr...]
    ppermute x0 -> x24, waiting for transfers between devices: none -> 53.4 us  [along(): lax.ppermute(piece, axis, [(i, i ^ s) for i in range(lax.axis_size(axis))])]
    all_to_all x11 -> x0, local copies, waits for them, and re-layouts: 44.8 us -> none  [the longest x3 18 us: on_device(): lax.all_to_all(half_step, 'py', split_axis=1, concat_axis=3, tiled=True)]
    dot_general x3 -> x0, matrix products: 40 us -> none  [the longest x1 20 us: on_device(): jnp.einsum('oij,fzjy->ofziy', x_operators, x_rows, preferred_element_type...]
    ppermute x0 -> x24, starting transfers between devices: none -> 31.6 us  [along(): lax.ppermute(piece, axis, [(i, i ^ s) for i in range(lax.axis_size(axis))])]
    convert_element_type x5 -> x0, other arithmetic: 25.1 us -> none  [the longest x2 24.2 us: on_device(): (result[2] + time_step * (-speed * result[0] + rates * result[1])).astype...]
  transfers between devices with their start and end apart: 16 -> 32, of which waited for: 5 -> 17; matrix products, arithmetic and copies ran while one was open for 18% -> 0% of each run, Pallas kernels for 0% -> 23%
where the time goes in v2:
time: 270 us; the launch traced here: 265 us
  waiting for transfers between devices  110 us (41%)
  Pallas kernels  71 us (26%)
  starting transfers between devices  59 us (22%)
  local copies, waits for them, and re-layouts  23.2 us (9%)
    pallas_call x16, Pallas kernels, run(): pl.pallas_call(body, grid_spec=pltpu.PrefetchScalarGridSpec(num_scalar_pr...  71 us
    ppermute x24, waiting for transfers between devices, along(): lax.ppermute(piece, axis, [(i, i ^ s) for i in range(lax.axis_size(axis))])  53.4 us
    all_to_all x4, waiting for transfers between devices, exchange(): lax.all_to_all(blocks.reshape((devices,) + blocks.shape[2:]), ('px', 'py'...  50.5 us
    ppermute x24, starting transfers between devices, along(): lax.ppermute(piece, axis, [(i, i ^ s) for i in range(lax.axis_size(axis))])  31.6 us
    unnamed x61, local copies, waits for them, and re-layouts  22.8 us
    all_to_all x4, starting transfers between devices, exchange(): lax.all_to_all(blocks.reshape((devices,) + blocks.shape[2:]), ('px', 'py'...  18.7 us
  transfers between devices with their start and end apart: 32, of which 17 were waited for; matrix products, arithmetic and copies ran while one was open for 0% of the time, Pallas kernels for 23%

profile of v2, /device:TPU:8, one launch (start us, length us, event | category | flops | bytes accessed | tf_op | source)
XLA Modules:
  0.0 264.8 jit_solution(7543285690789663313)
XLA Ops:
  5.8 6.0 %all-to-all-start.1 = ((bf16[32,3,128,128]{3,2,1,0:T(8,128)(2,1)}), bf16[32,3,128,128]{3,2,1,0:T(8,128)(2,1)S(1)}, u32[]{:S(2)}, u32[]{:S(2)}) async-start(bf16[32,3,128,128]{3,2,1,0:T(8,128)(2,1)} %bitcast.10), calls=%async_computation.1 | async-start | bytes 6291456 | tf_op jit(solution)/shard_map/all_to_all | solution.py:444
  18.5 9.9 %collective-permute-done.1 = s32[4,16]{1,0:T(4,128)S(1)} collective-permute-done((s32[4,16]{1,0:T(4,128)S(1)}, s32[4,16]{1,0:T(4,128)S(1)}, u32[]{:S(2)}, u32[]{:S(2)}) %collective-permute-start.1) | collective-permute-done | bytes 288 | tf_op jit(solution)/shard_map/ppermute | solution.py:439
  32.9 4.7 %collective-permute-start.7 = (s32[8,1,16]{2,1,0:T(1,128)S(1)}, s32[8,1,16]{2,1,0:T(1,128)S(1)}, u32[]{:S(2)}, u32[]{:S(2)}) collective-permute-start(s32[8,1,16]{2,1,0:T(1,128)S(1)} %get-tuple-element.65), channel_id=1, source_target_pairs={{0,1},{1,0},{2,3},{3,2},{4,5},{5,4},{6,7},{7,6},{8,9},{9,8},{10,11... | collective-permute-start | bytes 1544 | tf_op jit(solution)/shard_map/ppermute | solution.py:439
  37.5 6.0 %collective-permute-start.8 = (s32[8,1,16]{2,1,0:T(1,128)S(1)}, s32[8,1,16]{2,1,0:T(1,128)S(1)}, u32[]{:S(2)}, u32[]{:S(2)}) collective-permute-start(s32[8,1,16]{2,1,0:T(1,128)S(1)} %get-tuple-element.64), channel_id=1, source_target_pairs={{0,2},{1,3},{2,0},{3,1},{4,6},{5,7},{6,4},{7,5},{8,10},{9,11},{10,... | collective-permute-start | bytes 1544 | tf_op jit(solution)/shard_map/ppermute | solution.py:439
  48.1 35.4 %all-to-all-done.1 = bf16[32,3,128,128]{3,2,1,0:T(8,128)(2,1)S(1)} async-done(((bf16[32,3,128,128]{3,2,1,0:T(8,128)(2,1)}), bf16[32,3,128,128]{3,2,1,0:T(8,128)(2,1)S(1)}, u32[]{:S(2)}, u32[]{:S(2)}) %all-to-all-start.1) | async-done | bytes 3145760 | tf_op jit(solution)/shard_map/all_to_all | solution.py:444
  83.5 3.6 %all-to-all-start = ((bf16[32,1,128,128]{3,2,1,0:T(8,128)(2,1)}), bf16[32,1,128,128]{3,2,1,0:T(8,128)(2,1)}, u32[]{:S(2)}, u32[]{:S(2)}) async-start(bf16[32,1,128,128]{3,2,1,0:T(8,128)(2,1)} %bitcast.165), calls=%async_computation | async-start | bytes 2097152 | tf_op jit(solution)/shard_map/all_to_all | solution.py:444
  91.2 6.3 %x_pass.4 = (bf16[8,64,512]{2,1,0:T(8,128)(2,1)S(1)}, bf16[8,64,512]{2,1,0:T(8,128)(2,1)S(1)}, bf16[1024,512]{1,0:T(8,128)(2,1)S(1)}) custom-call(s32[8]{0:T(128)S(1)} %stack.127.at_ref, f32[4]{0:T(128)S(1)} %copy-done.18, bf16[3,8,2,64,1024]{4,3,2,1,0:T(8,128)(2,1)S(1)} %bitcast.159, bf16[8,4,3,128,128]{4,3,2,1,0:T(8,128)(2,1)S(1)} %bitcast.156, ...), custom_call_target="tpu_custom_call" | custom-call | flops 3221225472 | bytes 4194304 | tf_op jit(solution)/shard_map/x_pass/pallas_call | solution.py:54
  98.3 6.3 %x_pass.5 = (bf16[8,64,512]{2,1,0:T(8,128)(2,1)S(1)}, bf16[8,64,512]{2,1,0:T(8,128)(2,1)S(1)}) custom-call(s32[8]{0:T(128)S(1)} %stack.127.at_ref, f32[4]{0:T(128)S(1)} %copy-done.18, bf16[3,8,2,64,1024]{4,3,2,1,0:T(8,128)(2,1)S(1)} %bitcast.160, bf16[8,4,3,128,128]{4,3,2,1,0:T(8,128)(2,1)S(1)} %bitcast.157, bf16[8,2,64,512]{3,2,1,0:T(8,128)(2,1)S(1)} %bitcast.166, ...), custom_call_target="tpu_custom_call" | custom-call | flops 3221225472 | bytes 2097152 | tf_op jit(solution)/shard_map/x_pass/pallas_call | solution.py:54
  106.6 6.7 %y_pass.4 = (bf16[8,4,2,64,256]{4,3,2,1,0:T(8,128)(2,1)}, bf16[4,512,256]{2,1,0:T(8,128)(2,1)S(1)}) custom-call(s32[8]{0:T(128)S(1)} %stack.127.at_ref, f32[4]{0:T(128)S(1)} %copy-done.18, bf16[3,1024,1024]{2,1,0:T(8,128)(2,1)S(1)} %bitcast.153, bf16[8,64,512]{2,1,0:T(8,128)(2,1)S(1)} %get-tuple-element.28.refs_2_, ...), custom_call_target="tpu_custom_call" | custom-call | flops 3221225472 | bytes 6291456 | tf_op jit(solution)/shard_map/y_pass/pallas_call | solution.py:54
  113.3 6.3 %x_pass.6 = (bf16[8,64,512]{2,1,0:T(8,128)(2,1)S(1)}, bf16[8,64,512]{2,1,0:T(8,128)(2,1)S(1)}) custom-call(s32[8]{0:T(128)S(1)} %stack.127.at_ref, f32[4]{0:T(128)S(1)} %copy-done.18, bf16[3,8,2,64,1024]{4,3,2,1,0:T(8,128)(2,1)S(1)} %bitcast.163, bf16[8,4,3,128,128]{4,3,2,1,0:T(8,128)(2,1)S(1)} %bitcast.158, bf16[8,2,64,512]{3,2,1,0:T(8,128)(2,1)S(1)} %bitcast.167, ...), custom_call_target="tpu_custom_call" | custom-call | flops 3221225472 | bytes 2097152 | tf_op jit(solution)/shard_map/x_pass/pallas_call | solution.py:54
  121.6 6.6 %y_pass.5.refs_5_ = bf16[8,4,2,64,256]{4,3,2,1,0:T(8,128)(2,1)} custom-call(s32[8]{0:T(128)S(1)} %stack.127.at_ref, f32[4]{0:T(128)S(1)} %copy-done.18, bf16[3,1024,1024]{2,1,0:T(8,128)(2,1)S(1)} %bitcast.153, bf16[8,64,512]{2,1,0:T(8,128)(2,1)S(1)} %get-tuple-element.32.refs_2_, ...), custom_call_target="tpu_custom_call", output_to_operand_aliasing={{}: (6, {})} | custom-call | flops 3221225472 | bytes 4194304 | tf_op jit(solution)/shard_map/y_pass/pallas_call | solution.py:54
  128.2 5.8 %all-to-all-start.3 = ((bf16[32,2,64,256]{3,2,1,0:T(8,128)(2,1)}), bf16[32,2,64,256]{3,2,1,0:T(8,128)(2,1)S(1)}, u32[]{:S(2)}, u32[]{:S(2)}) async-start(bf16[32,2,64,256]{3,2,1,0:T(8,128)(2,1)} %bitcast.51), calls=%async_computation.3 | async-start | bytes 4194304 | tf_op jit(solution)/shard_map/all_to_all | solution.py:444
  140.0 6.6 %y_pass.6.refs_4_.refs_5_ = bf16[8,4,2,64,256]{4,3,2,1,0:T(8,128)(2,1)} custom-call(s32[8]{0:T(128)S(1)} %stack.127.at_ref, f32[4]{0:T(128)S(1)} %copy-done.18, bf16[3,1024,1024]{2,1,0:T(8,128)(2,1)S(1)} %copy-done.2, bf16[8,64,512]{2,1,0:T(8,128)(2,1)S(1)} %copy-done.14, bf16[8,64,512]{2,1,0:T(8,128)(2,1)S(1)} %collective-permute-done.10.refs_3_, ...), custom_call_target="tpu_custom_call" | custom-call | flops 3221225472 | bytes 4194304 | tf_op jit(solution)/shard_map/y_pass/pallas_call | solution.py:54
  149.4 7.0 %x_pass.7 = (bf16[8,64,512]{2,1,0:T(8,128)(2,1)S(1)}, bf16[8,64,512]{2,1,0:T(8,128)(2,1)S(1)}) custom-call(s32[8]{0:T(128)S(1)} %stack.127.at_ref, f32[4]{0:T(128)S(1)} %copy-done.18, bf16[3,8,2,64,1024]{4,3,2,1,0:T(8,128)(2,1)S(1)} %bitcast.164, bf16[8,4,1,128,128]{4,3,2,1,0:T(8,128)(2,1)} %bitcast.9.refs_2_, bf16[8,2,64,512]{3,2,1,0:T(8,128)(2,1)S(1)} %bitcast.168, ...), custom_call_target="tpu_custom_call" | custom-call | flops 3221225472 | bytes 2097152 | tf_op jit(solution)/shard_map/x_pass/pallas_call | solution.py:54
  161.2 6.6 %y_pass.7.refs_3_ = bf16[8,4,2,64,256]{4,3,2,1,0:T(8,128)(2,1)} custom-call(s32[8]{0:T(128)S(1)} %stack.127.at_ref, f32[4]{0:T(128)S(1)} %copy-done.18, bf16[3,1024,1024]{2,1,0:T(8,128)(2,1)S(1)} %copy-done.3, bf16[8,64,512]{2,1,0:T(8,128)(2,1)S(1)} %get-tuple-element.34.refs_2_, ...), custom_call_target="tpu_custom_call", output_to_operand_aliasing={{}: (6, {})} | custom-call | flops 3221225472 | bytes 4194304 | tf_op jit(solution)/shard_map/y_pass/pallas_call | solution.py:54
  167.8 15.0 %all-to-all-done.3 = bf16[32,2,64,256]{3,2,1,0:T(8,128)(2,1)S(1)} async-done(((bf16[32,2,64,256]{3,2,1,0:T(8,128)(2,1)}), bf16[32,2,64,256]{3,2,1,0:T(8,128)(2,1)S(1)}, u32[]{:S(2)}, u32[]{:S(2)}) %all-to-all-start.3) | async-done | bytes 2097184 | tf_op jit(solution)/shard_map/all_to_all | solution.py:444
  182.9 3.2 %all-to-all-start.2 = ((bf16[32,2,64,256]{3,2,1,0:T(8,128)(2,1)}), bf16[32,2,64,256]{3,2,1,0:T(8,128)(2,1)}, u32[]{:S(2)}, u32[]{:S(2)}) async-start(bf16[32,2,64,256]{3,2,1,0:T(8,128)(2,1)} %bitcast.49), calls=%async_computation.2 | async-start | bytes 4194304 | tf_op jit(solution)/shard_map/all_to_all | solution.py:444
  193.3 7.2 %collective-permute-done.15.refs_2_ = bf16[4,16,256]{2,1,0:T(8,128)(2,1)S(1)} collective-permute-done((bf16[4,16,256]{2,1,0:T(8,128)(2,1)S(1)}, bf16[4,16,256]{2,1,0:T(8,128)(2,1)S(1)}, u32[]{:S(2)}, u32[]{:S(2)}) %collective-permute-start.15) | collective-permute-done | bytes 32800 | tf_op jit(solution)/shard_map/ppermute | solution.py:439
  200.5 3.6 %put.2.refs_8_.refs_1_ = bf16[4,16,128,256]{3,2,1,0:T(8,128)(2,1)} custom-call(s32[8]{0:T(128)S(1)} %stack.127.at_ref, bf16[8,4,2,64,256]{4,3,2,1,0:T(8,128)(2,1)S(1)} %bitcast.155, bf16[4,16,256]{2,1,0:T(8,128)(2,1)S(1)} %get-tuple-element.36.refs_1_.refs_0_), custom_call_target="tpu_custom_call" | custom-call | bytes 8388608 | tf_op jit(solution)/shard_map/put/pallas_call | solution.py:54
  209.9 4.4 %collective-permute-start.22 = (bf16[8,16,256]{2,1,0:T(8,128)(2,1)S(1)}, bf16[8,16,256]{2,1,0:T(8,128)(2,1)S(1)}, u32[]{:S(2)}, u32[]{:S(2)}) collective-permute-start(bf16[8,16,256]{2,1,0:T(8,128)(2,1)S(1)} %get-tuple-element.46), channel_id=1, source_target_pairs={{0,2},{1,3},{2,0},{3,1},{4,6},{5,7},{6,4},{7,5},{8,10},{9,11},{10,... | collective-permute-start | bytes 196616 | tf_op jit(solution)/shard_map/ppermute | solution.py:439
  214.8 8.2 %collective-permute-done.21.refs_7_ = bf16[8,16,256]{2,1,0:T(8,128)(2,1)S(1)} collective-permute-done((bf16[8,16,256]{2,1,0:T(8,128)(2,1)S(1)}, bf16[8,16,256]{2,1,0:T(8,128)(2,1)S(1)}, u32[]{:S(2)}, u32[]{:S(2)}) %collective-permute-start.21) | collective-permute-done | bytes 65568 | tf_op jit(solution)/shard_map/ppermute | solution.py:439
  223.0 13.2 %collective-permute-done.22.refs_8_ = bf16[8,16,256]{2,1,0:T(8,128)(2,1)S(1)} collective-permute-done((bf16[8,16,256]{2,1,0:T(8,128)(2,1)S(1)}, bf16[8,16,256]{2,1,0:T(8,128)(2,1)S(1)}, u32[]{:S(2)}, u32[]{:S(2)}) %collective-permute-start.22) | collective-permute-done | bytes 65568 | tf_op jit(solution)/shard_map/ppermute | solution.py:439
  248.4 3.4 %collective-permute-start.27 = (f32[3,80,8]{2,1,0:T(8,128)S(1)}, f32[3,80,8]{2,1,0:T(8,128)S(1)}, u32[]{:S(2)}, u32[]{:S(2)}) collective-permute-start(f32[3,80,8]{2,1,0:T(8,128)S(1)} %get-tuple-element.49), channel_id=1, source_target_pairs={{1,0},{2,1},{3,2},{5,4},{6,5},{7,6},{9,8},{10,9},{11,10},{13,12},{... | collective-permute-start | bytes 23048 | tf_op jit(solution)/shard_map/ppermute | solution.py:30
  258.6 6.2 %put.3 = bf16[4,16,128,256]{3,2,1,0:T(8,128)(2,1)} custom-call(s32[8]{0:T(128)S(1)} %stack.127.at_ref, bf16[8,4,2,64,256]{4,3,2,1,0:T(8,128)(2,1)} %bitcast.50.refs_0_, bf16[4,16,128,256]{3,2,1,0:T(8,128)(2,1)} %put.2.refs_8_.refs_1_, f32[64,256]{1,0:T(8,128)S(1)} %copy-done.15), custom_call_target="tpu_custom_call", output_to_operand_aliasing={{}: (2, {})} | custom-call | bytes 8388608 | tf_op jit(solution)/shard_map/put/pallas_call | solution.py:54
  (134 shorter events, 75.5 us)
Async XLA Ops:
  5.8 77.7 %all-to-all-start.1 = ((bf16[32,3,128,128]{3,2,1,0:T(8,128)(2,1)}), bf16[32,3,128,128]{3,2,1,0:T(8,128)(2,1)S(1)}, u32[]{:S(2)}, u32[]{:S(2)}) async-start(bf16[32,3,128,128]{3,2,1,0:T(8,128)(2,1)} %bitcast.10), calls=%async_computation.1 | async-start | bytes 6291456 | tf_op jit(solution)/shard_map/all_to_all | solution.py:444
  12.6 15.8 %collective-permute-start.1 = (s32[4,16]{1,0:T(4,128)S(1)}, s32[4,16]{1,0:T(4,128)S(1)}, u32[]{:S(2)}, u32[]{:S(2)}) collective-permute-start(s32[4,16]{1,0:T(4,128)S(1)} %get-tuple-element.61), channel_id=1, source_target_pairs={{0,8},{4,12},{8,0},{12,4},{16,24},{20,28},{24,16},{28,20},{1,9},{5... | collective-permute-start | bytes 776 | tf_op jit(solution)/shard_map/ppermute | solution.py:439
  14.0 15.2 %collective-permute-start.2 = (s32[4,16]{1,0:T(4,128)S(1)}, s32[4,16]{1,0:T(4,128)S(1)}, u32[]{:S(2)}, u32[]{:S(2)}) collective-permute-start(s32[4,16]{1,0:T(4,128)S(1)} %get-tuple-element.60), channel_id=1, source_target_pairs={{0,12},{4,8},{8,4},{12,0},{16,28},{20,24},{24,20},{28,16},{1,13},{... | collective-permute-start | bytes 776 | tf_op jit(solution)/shard_map/ppermute | solution.py:439
  14.3 15.0 %collective-permute-start.3 = (s32[4,16]{1,0:T(4,128)S(1)}, s32[4,16]{1,0:T(4,128)S(1)}, u32[]{:S(2)}, u32[]{:S(2)}) collective-permute-start(s32[4,16]{1,0:T(4,128)S(1)} %get-tuple-element.59), channel_id=1, source_target_pairs={{0,16},{4,20},{8,24},{12,28},{16,0},{20,4},{24,8},{28,12},{1,17},{... | collective-permute-start | bytes 776 | tf_op jit(solution)/shard_map/ppermute | solution.py:439
  15.7 13.6 %collective-permute-start.4 = (s32[4,16]{1,0:T(4,128)S(1)}, s32[4,16]{1,0:T(4,128)S(1)}, u32[]{:S(2)}, u32[]{:S(2)}) collective-permute-start(s32[4,16]{1,0:T(4,128)S(1)} %get-tuple-element.58), channel_id=1, source_target_pairs={{0,20},{4,16},{8,28},{12,24},{16,4},{20,0},{24,12},{28,8},{1,21},{... | collective-permute-start | bytes 776 | tf_op jit(solution)/shard_map/ppermute | solution.py:439
  16.1 14.3 %collective-permute-start.5 = (s32[4,16]{1,0:T(4,128)S(1)}, s32[4,16]{1,0:T(4,128)S(1)}, u32[]{:S(2)}, u32[]{:S(2)}) collective-permute-start(s32[4,16]{1,0:T(4,128)S(1)} %get-tuple-element.57), channel_id=1, source_target_pairs={{0,24},{4,28},{8,16},{12,20},{16,8},{20,12},{24,0},{28,4},{1,25},{... | collective-permute-start | bytes 776 | tf_op jit(solution)/shard_map/ppermute | solution.py:439
  28.4 4.5 %collective-permute-start.6 = (s32[4,16]{1,0:T(4,128)S(1)}, s32[4,16]{1,0:T(4,128)S(1)}, u32[]{:S(2)}, u32[]{:S(2)}) collective-permute-start(s32[4,16]{1,0:T(4,128)S(1)} %get-tuple-element.56), channel_id=1, source_target_pairs={{0,28},{4,24},{8,20},{12,16},{16,12},{20,8},{24,4},{28,0},{1,29},{... | collective-permute-start | bytes 776 | tf_op jit(solution)/shard_map/ppermute | solution.py:439
  32.9 54.2 %collective-permute-start.7 = (s32[8,1,16]{2,1,0:T(1,128)S(1)}, s32[8,1,16]{2,1,0:T(1,128)S(1)}, u32[]{:S(2)}, u32[]{:S(2)}) collective-permute-start(s32[8,1,16]{2,1,0:T(1,128)S(1)} %get-tuple-element.65), channel_id=1, source_target_pairs={{0,1},{1,0},{2,3},{3,2},{4,5},{5,4},{6,7},{7,6},{8,9},{9,8},{10,11... | collective-permute-start | bytes 1544 | tf_op jit(solution)/shard_map/ppermute | solution.py:439
  37.5 49.6 %collective-permute-start.8 = (s32[8,1,16]{2,1,0:T(1,128)S(1)}, s32[8,1,16]{2,1,0:T(1,128)S(1)}, u32[]{:S(2)}, u32[]{:S(2)}) collective-permute-start(s32[8,1,16]{2,1,0:T(1,128)S(1)} %get-tuple-element.64), channel_id=1, source_target_pairs={{0,2},{1,3},{2,0},{3,1},{4,6},{5,7},{6,4},{7,5},{8,10},{9,11},{10,... | collective-permute-start | bytes 1544 | tf_op jit(solution)/shard_map/ppermute | solution.py:439
  43.5 43.6 %collective-permute-start.9 = (s32[8,1,16]{2,1,0:T(1,128)S(1)}, s32[8,1,16]{2,1,0:T(1,128)S(1)}, u32[]{:S(2)}, u32[]{:S(2)}) collective-permute-start(s32[8,1,16]{2,1,0:T(1,128)S(1)} %get-tuple-element.63), channel_id=1, source_target_pairs={{0,3},{1,2},{2,1},{3,0},{4,7},{5,6},{6,5},{7,4},{8,11},{9,10},{10,... | collective-permute-start | bytes 1544 | tf_op jit(solution)/shard_map/ppermute | solution.py:439
  83.5 44.7 %all-to-all-start = ((bf16[32,1,128,128]{3,2,1,0:T(8,128)(2,1)}), bf16[32,1,128,128]{3,2,1,0:T(8,128)(2,1)}, u32[]{:S(2)}, u32[]{:S(2)}) async-start(bf16[32,1,128,128]{3,2,1,0:T(8,128)(2,1)} %bitcast.165), calls=%async_computation | async-start | bytes 2097152 | tf_op jit(solution)/shard_map/all_to_all | solution.py:444
  128.2 54.7 %all-to-all-start.3 = ((bf16[32,2,64,256]{3,2,1,0:T(8,128)(2,1)}), bf16[32,2,64,256]{3,2,1,0:T(8,128)(2,1)S(1)}, u32[]{:S(2)}, u32[]{:S(2)}) async-start(bf16[32,2,64,256]{3,2,1,0:T(8,128)(2,1)} %bitcast.51), calls=%async_computation.3 | async-start | bytes 4194304 | tf_op jit(solution)/shard_map/all_to_all | solution.py:444
  182.9 74.9 %all-to-all-start.2 = ((bf16[32,2,64,256]{3,2,1,0:T(8,128)(2,1)}), bf16[32,2,64,256]{3,2,1,0:T(8,128)(2,1)}, u32[]{:S(2)}, u32[]{:S(2)}) async-start(bf16[32,2,64,256]{3,2,1,0:T(8,128)(2,1)} %bitcast.49), calls=%async_computation.2 | async-start | bytes 4194304 | tf_op jit(solution)/shard_map/all_to_all | solution.py:444
  187.6 12.9 %collective-permute-start.15 = (bf16[4,16,256]{2,1,0:T(8,128)(2,1)S(1)}, bf16[4,16,256]{2,1,0:T(8,128)(2,1)S(1)}, u32[]{:S(2)}, u32[]{:S(2)}) collective-permute-start(bf16[4,16,256]{2,1,0:T(8,128)(2,1)S(1)} %get-tuple-element.38), channel_id=1, source_target_pairs={{0,8},{4,12},{8,0},{12,4},{16,24},{20,28},{24,16},{28,20},{1,9},{5... | collective-permute-start | bytes 98312 | tf_op jit(solution)/shard_map/ppermute | solution.py:439
  188.9 15.3 %collective-permute-start.16 = (bf16[4,16,256]{2,1,0:T(8,128)(2,1)S(1)}, bf16[4,16,256]{2,1,0:T(8,128)(2,1)S(1)}, u32[]{:S(2)}, u32[]{:S(2)}) collective-permute-start(bf16[4,16,256]{2,1,0:T(8,128)(2,1)S(1)} %get-tuple-element.39), channel_id=1, source_target_pairs={{0,12},{4,8},{8,4},{12,0},{16,28},{20,24},{24,20},{28,16},{1,13},{... | collective-permute-start | bytes 98312 | tf_op jit(solution)/shard_map/ppermute | solution.py:439
  189.5 14.7 %collective-permute-start.17 = (bf16[4,16,256]{2,1,0:T(8,128)(2,1)S(1)}, bf16[4,16,256]{2,1,0:T(8,128)(2,1)S(1)}, u32[]{:S(2)}, u32[]{:S(2)}) collective-permute-start(bf16[4,16,256]{2,1,0:T(8,128)(2,1)S(1)} %get-tuple-element.40), channel_id=1, source_target_pairs={{0,16},{4,20},{8,24},{12,28},{16,0},{20,4},{24,8},{28,12},{1,17},{... | collective-permute-start | bytes 98312 | tf_op jit(solution)/shard_map/ppermute | solution.py:439
  190.6 13.6 %collective-permute-start.18 = (bf16[4,16,256]{2,1,0:T(8,128)(2,1)S(1)}, bf16[4,16,256]{2,1,0:T(8,128)(2,1)S(1)}, u32[]{:S(2)}, u32[]{:S(2)}) collective-permute-start(bf16[4,16,256]{2,1,0:T(8,128)(2,1)S(1)} %get-tuple-element.41), channel_id=1, source_target_pairs={{0,20},{4,16},{8,28},{12,24},{16,4},{20,0},{24,12},{28,8},{1,21},{... | collective-permute-start | bytes 98312 | tf_op jit(solution)/shard_map/ppermute | solution.py:439
  191.2 13.0 %collective-permute-start.19 = (bf16[4,16,256]{2,1,0:T(8,128)(2,1)S(1)}, bf16[4,16,256]{2,1,0:T(8,128)(2,1)S(1)}, u32[]{:S(2)}, u32[]{:S(2)}) collective-permute-start(bf16[4,16,256]{2,1,0:T(8,128)(2,1)S(1)} %get-tuple-element.42), channel_id=1, source_target_pairs={{0,24},{4,28},{8,16},{12,20},{16,8},{20,12},{24,0},{28,4},{1,25},{... | collective-permute-start | bytes 98312 | tf_op jit(solution)/shard_map/ppermute | solution.py:439
  200.5 4.6 %collective-permute-start.20 = (bf16[4,16,256]{2,1,0:T(8,128)(2,1)S(1)}, bf16[4,16,256]{2,1,0:T(8,128)(2,1)S(1)}, u32[]{:S(2)}, u32[]{:S(2)}) collective-permute-start(bf16[4,16,256]{2,1,0:T(8,128)(2,1)S(1)} %get-tuple-element.43), channel_id=1, source_target_pairs={{0,28},{4,24},{8,20},{12,16},{16,12},{20,8},{24,4},{28,0},{1,29},{... | collective-permute-start | bytes 98312 | tf_op jit(solution)/shard_map/ppermute | solution.py:439
  207.8 15.1 %collective-permute-start.21 = (bf16[8,16,256]{2,1,0:T(8,128)(2,1)S(1)}, bf16[8,16,256]{2,1,0:T(8,128)(2,1)S(1)}, u32[]{:S(2)}, u32[]{:S(2)}) collective-permute-start(bf16[8,16,256]{2,1,0:T(8,128)(2,1)S(1)} %get-tuple-element.45), channel_id=1, source_target_pairs={{0,1},{1,0},{2,3},{3,2},{4,5},{5,4},{6,7},{7,6},{8,9},{9,8},{10,11... | collective-permute-start | bytes 196616 | tf_op jit(solution)/shard_map/ppermute | solution.py:439
  209.9 26.2 %collective-permute-start.22 = (bf16[8,16,256]{2,1,0:T(8,128)(2,1)S(1)}, bf16[8,16,256]{2,1,0:T(8,128)(2,1)S(1)}, u32[]{:S(2)}, u32[]{:S(2)}) collective-permute-start(bf16[8,16,256]{2,1,0:T(8,128)(2,1)S(1)} %get-tuple-element.46), channel_id=1, source_target_pairs={{0,2},{1,3},{2,0},{3,1},{4,6},{5,7},{6,4},{7,5},{8,10},{9,11},{10,... | collective-permute-start | bytes 196616 | tf_op jit(solution)/shard_map/ppermute | solution.py:439
  214.3 25.0 %collective-permute-start.23 = (bf16[8,16,256]{2,1,0:T(8,128)(2,1)S(1)}, bf16[8,16,256]{2,1,0:T(8,128)(2,1)S(1)}, u32[]{:S(2)}, u32[]{:S(2)}) collective-permute-start(bf16[8,16,256]{2,1,0:T(8,128)(2,1)S(1)} %get-tuple-element.47), channel_id=1, source_target_pairs={{0,3},{1,2},{2,1},{3,0},{4,7},{5,6},{6,5},{7,4},{8,11},{9,10},{10,... | collective-permute-start | bytes 196616 | tf_op jit(solution)/shard_map/ppermute | solution.py:439
  245.9 6.8 %collective-permute-start.26 = (f32[3,80,8]{2,1,0:T(8,128)S(1)}, f32[3,80,8]{2,1,0:T(8,128)S(1)}, u32[]{:S(2)}, u32[]{:S(2)}) collective-permute-start(f32[3,80,8]{2,1,0:T(8,128)S(1)} %get-tuple-element.48), channel_id=1, source_target_pairs={{0,1},{1,2},{2,3},{4,5},{5,6},{6,7},{8,9},{9,10},{10,11},{12,13},{... | collective-permute-start | bytes 23048 | tf_op jit(solution)/shard_map/ppermute | solution.py:27
  248.4 6.8 %collective-permute-start.27 = (f32[3,80,8]{2,1,0:T(8,128)S(1)}, f32[3,80,8]{2,1,0:T(8,128)S(1)}, u32[]{:S(2)}, u32[]{:S(2)}) collective-permute-start(f32[3,80,8]{2,1,0:T(8,128)S(1)} %get-tuple-element.49), channel_id=1, source_target_pairs={{1,0},{2,1},{3,2},{5,4},{6,5},{7,6},{9,8},{10,9},{11,10},{13,12},{... | collective-permute-start | bytes 23048 | tf_op jit(solution)/shard_map/ppermute | solution.py:30
  (35 other events, 285.9 us)

commit v3 on v2

v3 whole, which is shorter than its diff:
```python
import jax
import jax.numpy as jnp
from jax import lax
from jax.experimental import pallas as pl
from jax.experimental.pallas import tpu as pltpu
from jax.sharding import PartitionSpec as P

COND_STEPS = 8

time_step = 0.25
wall_gain = 0.5
diffusion_rate = 0.24
source_gain = 0.1

U, V, W, THETA = 0, 1, 2, 3
SMALL_VMEM_BYTES = 16 * 1024 * 1024
MOST_VMEM_BYTES = 56 * 1024 * 1024

smem = pl.BlockSpec(memory_space=pltpu.SMEM)
anywhere = pl.BlockSpec(memory_space=pl.ANY)


def margins(block, axis, dim, width):
    count = lax.axis_size(axis)
    forward = [(i, i + 1) for i in range(count - 1)]
    backward = [(target, source) for source, target in forward]
    low = lax.ppermute(
        lax.slice_in_dim(block, block.shape[dim] - width, None, axis=dim), axis, forward
    )
    high = lax.ppermute(lax.slice_in_dim(block, 0, width, axis=dim), axis, backward)
    return low, high


def in_order(part):
    return part % 128 == 0


class Chain:
    def __init__(self, at):
        self.at = at
        self.last = []

    def run(
        self,
        name,
        kernel,
        args,
        in_specs,
        out_specs,
        out_shape,
        grid=(1,),
        scratch=(),
        aliases=None,
        flops=0,
        limit=MOST_VMEM_BYTES,
        free=False,
    ):
        count = len(args)
        tokens = [] if free else [x for x in self.last if not any(x is y for y in args)]

        def body(at_ref, *refs):
            kernel(at_ref, *refs[:count], *refs[count + len(tokens) :])

        moved = sum(x.size * x.dtype.itemsize for x in out_shape)
        outs = pl.pallas_call(
            body,
            grid_spec=pltpu.PrefetchScalarGridSpec(
                num_scalar_prefetch=1,
                grid=grid,
                in_specs=list(in_specs) + [anywhere] * len(tokens),
                out_specs=out_specs,
                scratch_shapes=list(scratch),
            ),
            out_shape=out_shape,
            input_output_aliases=aliases or {},
            compiler_params=pltpu.CompilerParams(vmem_limit_bytes=limit),
            cost_estimate=pl.CostEstimate(flops=flops, bytes_accessed=2 * moved, transcendentals=0),
            name=name,
        )(self.at, *args, *tokens)
        if not free:
            self.last = [min(outs, key=lambda x: x.size)]
        return outs


def whole(shape):
    return pl.BlockSpec(shape, lambda i, at: (0,) * len(shape))


def like(pieces):
    return [whole(piece.shape) for piece in pieces]


def cut(chain, fields, which, across_px, across_py):
    layers, xb, yb = fields.shape[1:]
    groups = layers // across_py
    members = across_px // groups
    part = yb // members

    def kernel(at, *refs):
        for n in range(len(which)):
            for g in range(groups):
                for k in range(members):
                    refs[-1][0, g * members + k, n] = refs[n][0, g, :, k * part : (k + 1) * part]

    def field(f):
        return pl.BlockSpec((1, groups, xb, yb), lambda i, at: (f, i, 0, 0))

    shape = (across_py, across_px, len(which), xb, part)
    return chain.run(
        "cut",
        kernel,
        [fields] * len(which),
        [field(f) for f in which],
        [pl.BlockSpec((1,) + shape[1:], lambda i, at: (i, 0, 0, 0, 0))],
        [jax.ShapeDtypeStruct(shape, fields.dtype)],
        grid=(across_py,),
        limit=MOST_VMEM_BYTES,
    )[0]


def x_pass(chain, which, operators, viscosity, arrived, members, speed):
    across_py, across_px, fields, xb, part = arrived.shape
    width = across_py * part
    length = across_px * xb
    rows = xb // members
    many = min(across_px, max(1, 256 // rows))
    steps = across_px // many
    first = which[0] == U

    def kernel(at, visc_ref, op_ref, arrived_ref, *refs):
        speed_ref, outs, lines = refs[0], refs[1:-1], refs[-1]
        if first:
            speed_ref, outs = refs[-2], refs[:-2]
        step = pl.program_id(0)
        turn, place = step // steps, step % steps

        @pl.when(step == 0)
        def _():
            for n in range(fields):
                for x in range(across_px):
                    for y in range(across_py):
                        start = n * width + y * part
                        lines[x * xb : (x + 1) * xb, start : start + part] = arrived_ref[y, x, n]
            if first:
                speed_ref[...] = lines[:, :width]

        block = op_ref[...].reshape(3 * many * rows, length)
        whole_result = jnp.dot(block, lines[...], preferred_element_type=jnp.float32)
        for n, field in enumerate(which):
            result = whole_result[:, n * width : (n + 1) * width].reshape(3, many, rows, width)
            for c in range(many):
                if first:
                    row = (place * many + c) * xb + (at[1] ^ turn) * rows
                    u = speed_ref[pl.ds(pl.multiple_of(row, rows), rows), :]
                else:
                    u = speed_ref[c, 0]
                value = result[2, c] + time_step * (
                    -u.astype(jnp.float32) * result[0, c] + visc_ref[field] * result[1, c]
                )
                value = value.astype(jnp.bfloat16)
                for r in range(members):

                    @pl.when(turn == r)
                    def _():
                        outs[n * members + r][c] = value

    def out_block(r):
        return pl.BlockSpec(
            (many, rows, width), lambda i, at: (jnp.clip(i - r * steps, 0, steps - 1), 0, 0)
        )

    def place_of(i, at):
        return i % steps, at[1] ^ (i // steps), 0, 0

    in_specs = [
        smem,
        pl.BlockSpec((3, many, 1, rows, length), lambda i, at: (0,) + place_of(i, at)),
        whole(arrived.shape),
    ]
    args = [viscosity, operators.reshape(3, across_px, members, rows, length), arrived]
    out_specs = [out_block(r) for _ in which for r in range(members)]
    out_shape = [jax.ShapeDtypeStruct((across_px, rows, width), jnp.bfloat16)] * len(out_specs)
    if first:
        out_specs.append(whole((length, width)))
        out_shape.append(jax.ShapeDtypeStruct((length, width), jnp.bfloat16))
    else:
        in_specs.append(pl.BlockSpec((many, 1, rows, width), place_of))
        args.append(speed.reshape(across_px, members, rows, width))
    outs = chain.run(
        "x_pass",
        kernel,
        args,
        in_specs,
        out_specs,
        out_shape,
        grid=(steps * members,),
        scratch=[pltpu.VMEM((length, fields * width), jnp.bfloat16)],
        flops=6 * length * length * width * fields,
        limit=MOST_VMEM_BYTES,
    )
    return [outs[n * members : (n + 1) * members] for n in range(fields)], outs[-1] if first else speed


def y_pass(chain, which, operators, viscosity, parts, speed, yb, shape, block):
    across_px, rows, width = parts[0][0].shape
    fields, members = len(parts), len(parts[0])
    part = yb // members
    length = width * members
    blocks = length // yb
    height = across_px * rows
    first = which[0] == V

    def kernel(at, visc_ref, op_ref, *refs):
        part_refs, rest = refs[: fields * members], refs[fields * members :]
        if first:
            out, speed_ref, lines = rest
        else:
            speed_ref, out, lines = rest
        step = pl.program_id(0)

        @pl.when(step == 0)
        def _():
            for n in range(fields):
                for r in range(members):
                    values = part_refs[n * members + r][...].reshape(height, width)
                    if in_order(part):
                        for y in range(blocks):
                            start = pl.multiple_of(y * yb + (at[1] ^ r) * part, part)
                            lines[n, :, pl.ds(start, part)] = values[:, y * part : (y + 1) * part]
                    else:
                        start = pl.multiple_of((at[1] ^ r) * width, width)
                        lines[n, :, pl.ds(start, width)] = values
            if first:
                for y in range(blocks):
                    if in_order(part):
                        speed_ref[y] = lines[0, :, y * yb : (y + 1) * yb]
                    else:
                        for k in range(members):
                            start = k * width + y * part
                            speed_ref[y, :, k * part : (k + 1) * part] = lines[0, :, start : start + part]

        v = speed_ref[step if first else 0].astype(jnp.float32)
        for n, field in enumerate(which):
            result = lax.dot_general(
                lines[n],
                op_ref[...].reshape(3 * yb, length),
                (((1,), (1,)), ((), ())),
                preferred_element_type=jnp.float32,
            )
            value = result[:, 2 * yb :] + time_step * (
                -v * result[:, :yb] + visc_ref[field] * result[:, yb : 2 * yb]
            )
            value = value.astype(jnp.bfloat16)
            if len(which) == 1:
                out[...] = value.reshape(block)
            else:
                out[0, :, n] = value.reshape(across_px, rows, yb)

    flat = [part for field_parts in parts for part in field_parts]
    in_specs = [smem, pl.BlockSpec((3, yb, length), lambda i, at: (0, i, 0))] + like(flat)
    args = [viscosity, operators, *flat]
    out_specs = [pl.BlockSpec(block, lambda i, at: (i,) + (0,) * (len(block) - 1))]
    out_shape = [jax.ShapeDtypeStruct(shape, jnp.bfloat16)]
    if first:
        out_specs.append(whole((blocks, height, yb)))
        out_shape.append(jax.ShapeDtypeStruct((blocks, height, yb), jnp.bfloat16))
    else:
        in_specs.append(pl.BlockSpec((1, height, yb), lambda i, at: (i, 0, 0)))
        args.append(speed)
    outs = chain.run(
        "y_pass",
        kernel,
        args,
        in_specs,
        out_specs,
        out_shape,
        grid=(blocks,),
        scratch=[pltpu.VMEM((fields, height, length), jnp.bfloat16)],
        flops=6 * length * length * height * fields,
        limit=MOST_VMEM_BYTES,
    )
    return outs[0], outs[1] if first else speed


def put(chain, buffer, arrived, which, block, shape):
    across_py, across_px = arrived.shape[:2]
    extra = [] if buffer is None else [buffer]
    many = len(which)
    first, stride = which[0], which[1] - which[0] if many > 1 else 0

    def kernel(at, arrived_ref, *refs):
        refs[-1][...] = arrived_ref[...].reshape(refs[-1].shape)

    return chain.run(
        "put",
        kernel,
        [arrived, *extra],
        [pl.BlockSpec((across_py, across_px, block) + arrived.shape[3:], lambda n, at: (0, 0, n, 0, 0))]
        + [anywhere] * len(extra),
        [pl.BlockSpec((1,) + shape[1:], lambda n, at: (first + n * stride, 0, 0, 0))],
        [jax.ShapeDtypeStruct(shape, arrived.dtype)],
        grid=(many,),
        aliases={2: 0} if extra else {},
        limit=SMALL_VMEM_BYTES,
        free=True,
    )[0]


def wall_lines(chain, arrived, n, tile, slot, buffer):
    across_py, across_px, _, rows, yb = arrived.shape
    count, span = tile.shape[0], across_px * across_py * rows
    devices = across_px * across_py
    units, unit = buffer.shape[2:4]

    def kernel(at, tile_ref, slot_ref, arrived_ref, buffer_ref, out):
        chosen = tile_ref[...] == lax.broadcasted_iota(jnp.int32, (count, span), 1)
        flux = jnp.dot(
            chosen.astype(jnp.float32).astype(jnp.bfloat16),
            arrived_ref[...].reshape(span, yb),
            preferred_element_type=jnp.float32,
        )
        filled = slot_ref[...] == lax.broadcasted_iota(jnp.int32, (devices * unit, count), 0)
        out[...] = (
            jnp.dot(
                filled.astype(jnp.float32).astype(jnp.bfloat16),
                flux.astype(jnp.bfloat16),
                preferred_element_type=jnp.float32,
            )
            .astype(jnp.bfloat16)
            .reshape(across_py, across_px, 1, unit, yb)
        )

    args = [tile.reshape(-1, 1), slot.reshape(1, -1)]
    return chain.run(
        "wall_lines",
        kernel,
        args + [arrived, buffer],
        like(args)
        + [pl.BlockSpec((across_py, across_px, 1, rows, yb), lambda i, at: (0, 0, n, 0, 0)), anywhere],
        [pl.BlockSpec((across_py, across_px, 1, unit, yb), lambda i, at: (0, 0, units - 1, 0, 0))],
        [jax.ShapeDtypeStruct(buffer.shape, buffer.dtype)],
        aliases={4: 0},
        limit=SMALL_VMEM_BYTES,
    )[0]


def add_flux(chain, tags, arrived, solid_temp, conductivity):
    rows, columns = solid_temp.shape
    across_py, across_px, units, unit, _ = arrived.shape

    def kernel(at, temp_ref, kappa_ref, arrived_ref, *refs):
        tag_refs, out = refs[:-1], refs[-1]
        out[0] = temp_ref[...]
        out[1] = kappa_ref[...]
        places = lax.broadcasted_iota(jnp.int32, (rows, unit), 0)
        source = jnp.zeros((rows, columns), jnp.float32)
        for s in range(across_py):
            chosen = [tag_refs[s][at[7] ^ t] == places for t in range(across_px)]
            chosen = jnp.concatenate([c.astype(jnp.float32) for c in chosen], axis=1)
            source = source + jnp.dot(
                chosen.astype(jnp.bfloat16),
                arrived_ref[at[2] ^ s].reshape(across_px * unit, columns),
                preferred_element_type=jnp.float32,
            )
        out[2] = (wall_gain * source_gain) * source

    args = [solid_temp, conductivity]
    lines = pl.BlockSpec(
        (across_py, across_px, 1, unit, columns), lambda i, at: (0, 0, units - 1, 0, 0)
    )
    return chain.run(
        "add_flux",
        kernel,
        args + [arrived, *tags],
        like(args) + [lines] + like(tags),
        [whole((3, rows, columns))],
        [jax.ShapeDtypeStruct((3, rows, columns), jnp.float32)],
    )[0]


def conduct_and_put(chain, solid, low, high, margin, buffer, arrived, field):
    across_py, across_px, _, x_rows, _ = arrived.shape
    members = buffer.shape[2] // x_rows
    groups = across_px // members
    kinds, height, columns = solid.shape
    rows = height - 2 * margin
    wide = columns + -(-2 * margin // 128) * 128

    def kernel(at, solid_ref, low_ref, high_ref, arrived_ref, buffer_ref, out, fields_ref, ext, sems):
        copies = [
            pltpu.make_async_copy(
                arrived_ref.at[k, a, 0],
                fields_ref.at[field, k * groups + a // members, pl.ds(a % members * x_rows, x_rows)],
                sems.at[k, a],
            )
            for k in range(across_py)
            for a in range(across_px)
        ]
        for copy in copies:
            copy.start()
        ext[:, :, columns:] = jnp.zeros((kinds, height, wide - columns), jnp.float32)
        ext[:, :, :columns] = solid_ref[...]
        ext[:, :, columns : columns + margin] = high_ref[...]
        ext[:, :, wide - margin :] = low_ref[...]
        t, kappa, heat = ext[0], ext[1], ext[2]
        row = lax.broadcasted_iota(jnp.int32, (height, wide), 0) + at[3]
        col = lax.broadcasted_iota(jnp.int32, (height, wide), 1)
        col = jnp.where(col < wide - margin, col, col - wide) + at[4]
        inside = (row >= 0) & (row < at[5]) & (col >= 0) & (col < at[6])
        moves = ((height - 1, 0), (1, 0), (wide - 1, 1), (1, 1))
        faces = [
            jnp.where(inside, diffusion_rate * 0.5 * (kappa + pltpu.roll(kappa, shift, dim)), 0.0)
            for shift, dim in moves
        ]
        for _ in range(COND_STEPS):
            change = heat
            for face, (shift, dim) in zip(faces, moves):
                change = change + face * (pltpu.roll(t, shift, dim) - t)
            t = t + change
        out[...] = t[margin : margin + rows, :columns]
        for copy in copies:
            copy.wait()

    args = [solid, low, high, arrived]
    return chain.run(
        "conduct_and_put",
        kernel,
        args + [buffer],
        like(args) + [anywhere],
        [whole((rows, columns)), anywhere],
        [
            jax.ShapeDtypeStruct((rows, columns), jnp.float32),
            jax.ShapeDtypeStruct(buffer.shape, buffer.dtype),
        ],
        scratch=[
            pltpu.VMEM((kinds, height, wide), jnp.float32),
            pltpu.SemaphoreType.DMA((across_py, across_px)),
        ],
        aliases={5: 1},
        limit=SMALL_VMEM_BYTES,
    )


def on_device(
    fields,
    x_operators,
    y_operators,
    viscosity,
    wall_tile,
    wall_owner,
    wall_row,
    solid_temp,
    conductivity,
):
    across_px, across_py = lax.axis_size("px"), lax.axis_size("py")
    devices = across_px * across_py
    layers, xb, yb = fields.shape[1:]
    groups = layers // across_py
    members = across_px // groups
    a, b = lax.axis_index("px"), lax.axis_index("py")
    q, m = a // members, a % members
    rows, columns = solid_temp.shape
    margin = COND_STEPS
    at = jnp.stack(
        [
            q,
            m,
            b,
            a * rows - margin,
            b * columns,
            across_px * rows,
            across_py * columns,
            a,
        ]
    ).astype(jnp.int32)
    chain = Chain(at)

    def along(axis, pieces):
        return [pieces[0]] + [
            lax.ppermute(piece, axis, [(i, i ^ s) for i in range(lax.axis_size(axis))])
            for s, piece in enumerate(pieces[1:], 1)
        ]

    def exchange(blocks):
        moved = lax.all_to_all(
            blocks.reshape((devices,) + blocks.shape[2:]),
            ("py", "px"),
            split_axis=0,
            concat_axis=0,
            tiled=True,
        )
        return moved.reshape(blocks.shape)

    half, speeds = {}, {}

    def forward(*which):
        return exchange(cut(chain, fields, which, across_px, across_py))

    def X(arrived, *which):
        outs, speeds[U] = x_pass(
            chain, which, x_operators, viscosity, arrived, members, speeds.get(U)
        )
        for f, out in zip(which, outs):
            half[f] = along("px", out)

    y_columns = y_operators
    if not in_order(yb // members):
        y_columns = y_columns.reshape(3, -1, across_py, members, yb // members)
        y_columns = y_columns.swapaxes(2, 3).reshape(y_operators.shape)

    x_rows = xb // members
    unit = min(16, x_rows)

    def Y(*which, slots=False):
        shape = (across_py, across_px, len(which), x_rows, yb)
        block = (1,) + shape[1:]
        if slots:
            shape = (across_py, across_px, x_rows // unit + 1, unit, yb)
            block = (1, across_px, x_rows // unit, unit, yb)
        out, speeds[V] = y_pass(
            chain,
            which,
            y_columns,
            viscosity,
            [half[f] for f in which],
            speeds.get(V),
            yb,
            shape,
            block,
        )
        return out

    most = forward(U, V, THETA)

    count = wall_tile.shape[0]
    owner = wall_owner[:, 0]
    capacity = max(2, 4 * count // devices)
    assert capacity <= unit
    order = jnp.arange(count, dtype=jnp.int32)
    earlier = (owner[:, None] == owner[None, :]) & (order[None, :] < order[:, None])
    position = jnp.sum(earlier.astype(jnp.int32), axis=1)
    label = owner * unit + position
    filled = label[None, :] == jnp.arange(devices * unit, dtype=jnp.int32)[:, None]
    labels = jnp.sum(jnp.where(filled, wall_row[None, :] + 1, 0), axis=1) - 1
    labels = labels.reshape(across_px, across_py, unit)
    slot = (owner % across_py * across_px + owner // across_py) * unit + position
    tags = along(
        "px",
        [lax.dynamic_index_in_dim(labels, a ^ s, 0, keepdims=False) for s in range(across_px)],
    )
    chain.last += tags
    last = forward(W)
    tags = along(
        "py",
        [
            jnp.stack([lax.dynamic_index_in_dim(tag, b ^ s, 0) for tag in tags])
            for s in range(across_py)
        ],
    )

    chain.last += tags
    X(most, U, V, THETA)
    first = exchange(Y(V, THETA))
    second = Y(U, slots=True)
    X(last, W)
    third = Y(W)
    second = exchange(wall_lines(chain, first, 1, wall_tile, slot, second))
    third = exchange(third)
    new_fields = put(chain, None, first, (V, THETA), 1, fields.shape)
    solid = add_flux(chain, tags, second, solid_temp, conductivity)
    low, high = margins(solid, "px", 1, margin)
    solid = jnp.concatenate([low, solid, high], axis=1)
    new_fields = put(chain, new_fields, second, (U,), x_rows // unit, fields.shape)
    low, high = margins(solid, "py", 2, margin)
    new_solid, new_fields = conduct_and_put(
        chain, solid, low, high, margin, new_fields, third, W
    )
    return new_fields, new_solid


def solution(mesh):
    return jax.shard_map(
        on_device,
        mesh=mesh,
        in_specs=(
            P(None, None, "px", "py"),
            P(),
            P(),
            P(),
            P(("px", "py")),
            P(("px", "py"), None),
            P(("px", "py")),
            P("px", "py"),
            P("px", "py"),
        ),
        out_specs=(P(None, None, "px", "py"), P("px", "py")),
        check_vma=False,
    )
```

time: 270 us -> 254 us (0.941); the launches traced: 265 us -> 252 us
  blocking collectives: 0 us -> 38.4 us
  waiting for transfers between devices: 110 us -> 82.7 us
  local copies, waits for them, and re-layouts: 23.2 us -> 6.8 us
  starting transfers between devices: 59 us -> 45.7 us
  Pallas kernels: 71 us -> 75.9 us
    all_to_all x0 -> x1, blocking collectives: none -> 38.4 us  [exchange(): lax.all_to_all(blocks.reshape((devices,) + blocks.shape[2:]), ('py', 'px'...]
    ppermute x24 -> x14, waiting for transfers between devices: 53.4 us -> 20.9 us  [along(): lax.ppermute(piece, axis, [(i, i ^ s) for i in range(lax.axis_size(axis))])]
    unnamed x61, local copies, waits for them, and re-layouts: 22.8 us -> 4.44 us
    ppermute x24 -> x14, starting transfers between devices: 31.6 us -> 13.6 us  [along(): lax.ppermute(piece, axis, [(i, i ^ s) for i in range(lax.axis_size(axis))])]
    all_to_all x4, waiting for transfers between devices: 50.5 us -> 56.8 us  [exchange(): lax.all_to_all(blocks.reshape((devices,) + blocks.shape[2:]), ('py', 'px'...]
    pallas_call x16 -> x12, Pallas kernels: 71 us -> 75.9 us  [run(): pl.pallas_call(body, grid_spec=pltpu.PrefetchScalarGridSpec(num_scalar_pr...]
    all_to_all x4, starting transfers between devices: 18.7 us -> 22.8 us  [exchange(): lax.all_to_all(blocks.reshape((devices,) + blocks.shape[2:]), ('py', 'px'...]
  transfers between devices with their start and end apart: 32 -> 22, of which waited for: 17 -> 12; matrix products, arithmetic and copies ran while one was open for 0% -> 1% of each run, Pallas kernels for 23% -> 26%
where the time goes in v3:
time: 254 us; the launch traced here: 252 us
  waiting for transfers between devices  82.7 us (33%)
  Pallas kernels  75.9 us (30%)
  starting transfers between devices  45.7 us (18%)
  blocking collectives  38.4 us (15%)
  local copies, waits for them, and re-layouts  6.8 us (3%)
    pallas_call x12, Pallas kernels, run(): pl.pallas_call(body, grid_spec=pltpu.PrefetchScalarGridSpec(num_scalar_pr...  75.9 us
    all_to_all x4, waiting for transfers between devices, exchange(): lax.all_to_all(blocks.reshape((devices,) + blocks.shape[2:]), ('py', 'px'...  56.8 us
    all_to_all x1, blocking collectives, exchange(): lax.all_to_all(blocks.reshape((devices,) + blocks.shape[2:]), ('py', 'px'...  38.4 us
    all_to_all x4, starting transfers between devices, exchange(): lax.all_to_all(blocks.reshape((devices,) + blocks.shape[2:]), ('py', 'px'...  22.8 us
    ppermute x14, waiting for transfers between devices, along(): lax.ppermute(piece, axis, [(i, i ^ s) for i in range(lax.axis_size(axis))])  20.9 us
    ppermute x14, starting transfers between devices, along(): lax.ppermute(piece, axis, [(i, i ^ s) for i in range(lax.axis_size(axis))])  13.6 us
    ppermute x2, starting transfers between devices, margins(): lax.ppermute(lax.slice_in_dim(block, block.shape[dim] - width, None, axis...  5.61 us
  transfers between devices with their start and end apart: 22, of which 12 were waited for; matrix products, arithmetic and copies ran while one was open for 1% of the time, Pallas kernels for 26%

profile of v3, /device:TPU:8, one launch (start us, length us, event | category | flops | bytes accessed | tf_op | source)
XLA Modules:
  0.0 251.9 jit_solution(4076968527232446552)
XLA Ops:
  1.3 5.0 %cut.2.refs_1_ = bf16[4,8,3,128,128]{4,3,2,1,0:T(8,128)(2,1)} custom-call(s32[8]{0:T(128)} %stack.127.at_ref, bf16[4,16,128,256]{3,2,1,0:T(8,128)(2,1)} %refs_0_.9, bf16[4,16,128,256]{3,2,1,0:T(8,128)(2,1)} %refs_0_.9, bf16[4,16,128,256]{3,2,1,0:T(8,128)(2,1)} %refs_0_.9), custom_call_target="tpu_custom_call" | custom-call | bytes 6291456 | tf_op jit(solution)/shard_map/cut/pallas_call | solution.py:65
  6.3 6.0 %all-to-all-start = ((bf16[32,3,128,128]{3,2,1,0:T(8,128)(2,1)}), bf16[32,3,128,128]{3,2,1,0:T(8,128)(2,1)S(1)}, u32[]{:S(2)}, u32[]{:S(2)}) async-start(bf16[32,3,128,128]{3,2,1,0:T(8,128)(2,1)} %bitcast.176), calls=%async_computation | async-start | bytes 6291456 | tf_op jit(solution)/shard_map/all_to_all | solution.py:485
  20.5 10.9 %collective-permute-done.1.refs_4_ = s32[4,16]{1,0:T(4,128)S(1)} collective-permute-done((s32[4,16]{1,0:T(4,128)S(1)}, s32[4,16]{1,0:T(4,128)S(1)}, u32[]{:S(2)}, u32[]{:S(2)}) %collective-permute-start.1) | collective-permute-done | bytes 288 | tf_op jit(solution)/shard_map/ppermute | solution.py:480
  31.4 3.0 %collective-permute-done.2.refs_5_ = s32[4,16]{1,0:T(4,128)S(1)} collective-permute-done((s32[4,16]{1,0:T(4,128)S(1)}, s32[4,16]{1,0:T(4,128)S(1)}, u32[]{:S(2)}, u32[]{:S(2)}) %collective-permute-start.2) | collective-permute-done | bytes 288 | tf_op jit(solution)/shard_map/ppermute | solution.py:480
  34.6 2.9 %collective-permute-start.9 = (s32[8,1,16]{2,1,0:T(1,128)S(1)}, s32[8,1,16]{2,1,0:T(1,128)S(1)}, u32[]{:S(2)}, u32[]{:S(2)}) collective-permute-start(s32[8,1,16]{2,1,0:T(1,128)S(1)} %get-tuple-element.44), channel_id=1, source_target_pairs={{0,3},{1,2},{2,1},{3,0},{4,7},{5,6},{6,5},{7,4},{8,11},{9,10},{10,... | collective-permute-start | bytes 1544 | tf_op jit(solution)/shard_map/ppermute | solution.py:480
  37.5 2.4 collective-permute-start.8
  41.4 4.1 %cut.3.refs_3_ = bf16[4,8,1,128,128]{4,3,2,1,0:T(8,128)(2,1)} custom-call(s32[8]{0:T(128)} %stack.127.at_ref, bf16[4,16,128,256]{3,2,1,0:T(8,128)(2,1)} %refs_0_.9, bf16[4,8,3,128,128]{4,3,2,1,0:T(8,128)(2,1)} %cut.2.refs_1_, s32[4,16]{1,0:T(4,128)} %get-tuple-element.43.refs_2_, s32[4,16]{1,0:T(4,128)} %copy-done.12, s32[4,16]{1,0:T(4,128)} %copy-done.13, ...), custom_call_target="tpu_custom_call" | custom-call | bytes 2097152 | tf_op jit(solution)/shard_map/cut/pallas_call | solution.py:65
  45.4 36.1 %all-to-all-done = bf16[32,3,128,128]{3,2,1,0:T(8,128)(2,1)S(1)} async-done(((bf16[32,3,128,128]{3,2,1,0:T(8,128)(2,1)}), bf16[32,3,128,128]{3,2,1,0:T(8,128)(2,1)S(1)}, u32[]{:S(2)}, u32[]{:S(2)}) %all-to-all-start) | async-done | bytes 3145760 | tf_op jit(solution)/shard_map/all_to_all | solution.py:485
  81.5 6.5 %all-to-all-start.2 = ((bf16[32,1,128,128]{3,2,1,0:T(8,128)(2,1)}), bf16[32,1,128,128]{3,2,1,0:T(8,128)(2,1)}, u32[]{:S(2)}, u32[]{:S(2)}) async-start(bf16[32,1,128,128]{3,2,1,0:T(8,128)(2,1)} %bitcast.177), calls=%async_computation.2 | async-start | bytes 2097152 | tf_op jit(solution)/shard_map/all_to_all | solution.py:485
  88.7 17.8 %x_pass.2 = (bf16[8,64,512]{2,1,0:T(8,128)(2,1)}, bf16[8,64,512]{2,1,0:T(8,128)(2,1)}, bf16[8,64,512]{2,1,0:T(8,128)(2,1)}, bf16[8,64,512]{2,1,0:T(8,128)(2,1)},...) custom-call(s32[8]{0:T(128)} %stack.127.at_ref, f32[4]{0:T(128)} %refs_0_.14, ...), custom_call_target="tpu_custom_call" | custom-call | flops 9663676416 | bytes 8388608 | tf_op jit(solution)/shard_map/x_pass/pallas_call | solution.py:65
  110.2 11.6 %y_pass.3 = (bf16[4,8,2,64,256]{4,3,2,1,0:T(8,128)(2,1)}, bf16[4,512,256]{2,1,0:T(8,128)(2,1)}) custom-call(s32[8]{0:T(128)} %stack.127.at_ref, f32[4]{0:T(128)} %refs_0_.14, bf16[3,1024,1024]{2,1,0:T(8,128)(2,1)} %refs_1_.8, bf16[8,64,512]{2,1,0:T(8,128)(2,1)} %get-tuple-element.15.refs_2_, bf16[8,64,512]{2,1,0:T(8,128)(2,1)} %copy-done.23, ...), custom_call_target="tpu_custom_call" | custom-call | flops 6442450944 | bytes 6291456 | tf_op jit(solution)/shard_map/y_pass/pallas_call | solution.py:65
  121.8 5.8 %all-to-all-start.1 = ((bf16[32,2,64,256]{3,2,1,0:T(8,128)(2,1)}), bf16[32,2,64,256]{3,2,1,0:T(8,128)(2,1)S(1)}, u32[]{:S(2)}, u32[]{:S(2)}) async-start(bf16[32,2,64,256]{3,2,1,0:T(8,128)(2,1)} %bitcast.179), calls=%async_computation.1 | async-start | bytes 4194304 | tf_op jit(solution)/shard_map/all_to_all | solution.py:485
  130.5 8.2 %y_pass.4.refs_4_.refs_3_ = bf16[4,8,5,16,256]{4,3,2,1,0:T(8,128)(2,1)} custom-call(s32[8]{0:T(128)} %stack.127.at_ref, f32[4]{0:T(128)} %refs_0_.14, bf16[3,1024,1024]{2,1,0:T(8,128)(2,1)} %refs_1_.8, bf16[8,64,512]{2,1,0:T(8,128)(2,1)} %get-tuple-element.19.refs_6_.refs_2_, bf16[8,64,512]{2,1,0:T(8,128)(2,1)} %copy-done.26, ...), custom_call_target="tpu_custom_call" | custom-call | flops 3221225472 | bytes 2621440 | tf_op jit(solution)/shard_map/y_pass/pallas_call | solution.py:65
  138.7 8.6 %x_pass.3 = (bf16[8,64,512]{2,1,0:T(8,128)(2,1)}, bf16[8,64,512]{2,1,0:T(8,128)(2,1)}) custom-call(s32[8]{0:T(128)} %stack.127.at_ref, f32[4]{0:T(128)} %refs_0_.14, bf16[3,8,2,64,1024]{4,3,2,1,0:T(8,128)(2,1)} %bitcast.183, bf16[4,8,1,128,128]{4,3,2,1,0:T(8,128)(2,1)} %bitcast.53.refs_2_, bf16[8,2,64,512]{3,2,1,0:T(8,128)(2,1)} %bitcast.184, ...), custom_call_target="tpu_custom_call" | custom-call | flops 3221225472 | bytes 2097152 | tf_op jit(solution)/shard_map/x_pass/pallas_call | solution.py:65
  150.3 8.4 %y_pass.5.refs_4_ = bf16[4,8,1,64,256]{4,3,2,1,0:T(8,128)(2,1)} custom-call(s32[8]{0:T(128)} %stack.127.at_ref, f32[4]{0:T(128)} %refs_0_.14, bf16[3,1024,1024]{2,1,0:T(8,128)(2,1)} %refs_1_.8, bf16[8,64,512]{2,1,0:T(8,128)(2,1)} %get-tuple-element.24.refs_2_, bf16[8,64,512]{2,1,0:T(8,128)(2,1)} %copy-done.25, bf16[4,512,256]{2,1,0:T(8,128)(2,1)} %get-tuple-element.22.refs_4_), custom_call_target="tpu_custom_call" | custom-call | flops 3221225472 | bytes 2097152 | tf_op jit(solution)/shard_map/y_pass/pallas_call | solution.py:65
  158.7 15.7 %all-to-all-done.1 = bf16[32,2,64,256]{3,2,1,0:T(8,128)(2,1)S(1)} async-done(((bf16[32,2,64,256]{3,2,1,0:T(8,128)(2,1)}), bf16[32,2,64,256]{3,2,1,0:T(8,128)(2,1)S(1)}, u32[]{:S(2)}, u32[]{:S(2)}) %all-to-all-start.1) | async-done | bytes 2097184 | tf_op jit(solution)/shard_map/all_to_all | solution.py:485
  176.8 38.4 %all_to_all.25 = bf16[32,5,16,256]{3,2,1,0:T(8,128)(2,1)} all-to-all(bf16[32,5,16,256]{3,2,1,0:T(8,128)(2,1)S(1)} %bitcast.174), channel_id=1, replica_groups=mesh['px'=8,'py'=4] {'py','px'}, dimensions={0} | all-to-all | bytes 2621440 | tf_op jit(solution)/shard_map/all_to_all | solution.py:485
  215.2 4.4 %all-to-all-start.4 = ((bf16[32,1,64,256]{3,2,1,0:T(8,128)(2,1)}), bf16[32,1,64,256]{3,2,1,0:T(8,128)(2,1)}, u32[]{:S(2)}, u32[]{:S(2)}) async-start(bf16[32,1,64,256]{3,2,1,0:T(8,128)(2,1)} %bitcast.175), calls=%async_computation.4 | async-start | bytes 2097152 | tf_op jit(solution)/shard_map/all_to_all | solution.py:485
  219.6 2.7 %add_flux.1.refs_5_ = f32[3,64,256]{2,1,0:T(8,128)} custom-call(s32[8]{0:T(128)} %stack.127.at_ref, f32[64,256]{1,0:T(8,128)} %refs_0_.15, f32[64,256]{1,0:T(8,128)} %refs_1_.9, bf16[4,8,5,16,256]{4,3,2,1,0:T(8,128)(2,1)} %bitcast.172, s32[8,1,16]{2,1,0:T(1,128)} %copy-done.15, s32[8,1,16]{2,1,0:T(1,128)} %copy-done.18, s32[8,1,16]{2,1,0:T(1,128)} %copy-done.17, ...), custom_call_target="tpu_custom_call" | custom-call | bytes 393216 | tf_op jit(solution)/shard_map/add_flux/pallas_call | solution.py:65
  226.4 2.7 %collective-permute-done.15 = f32[3,8,256]{2,1,0:T(8,128)S(1)} collective-permute-done((f32[3,8,256]{2,1,0:T(8,128)S(1)}, f32[3,8,256]{2,1,0:T(8,128)S(1)}, u32[]{:S(2)}, u32[]{:S(2)}) %collective-permute-start.15) | collective-permute-done | bytes 24608 | tf_op jit(solution)/shard_map/ppermute | solution.py:30
  230.2 2.4 collective-permute-start.17
  232.6 3.6 %collective-permute-start.16 = (f32[3,80,8]{2,1,0:T(8,128)S(1)}, f32[3,80,8]{2,1,0:T(8,128)S(1)}, u32[]{:S(2)}, u32[]{:S(2)}) collective-permute-start(f32[3,80,8]{2,1,0:T(8,128)S(1)} %get-tuple-element.29), channel_id=1, source_target_pairs={{0,1},{1,2},{2,3},{4,5},{5,6},{6,7},{8,9},{9,10},{10,11},{12,13},{... | collective-permute-start | bytes 23048 | tf_op jit(solution)/shard_map/ppermute | solution.py:27
  239.9 5.1 %all-to-all-done.4 = bf16[32,1,64,256]{3,2,1,0:T(8,128)(2,1)} async-done(((bf16[32,1,64,256]{3,2,1,0:T(8,128)(2,1)}), bf16[32,1,64,256]{3,2,1,0:T(8,128)(2,1)}, u32[]{:S(2)}, u32[]{:S(2)}) %all-to-all-start.4) | async-done | bytes 1048608 | tf_op jit(solution)/shard_map/all_to_all | solution.py:485
  247.3 4.7 %conduct_and_put.1 = (f32[64,256]{1,0:T(8,128)}, bf16[4,16,128,256]{3,2,1,0:T(8,128)(2,1)}) custom-call(s32[8]{0:T(128)S(1)} %copy-done.6, f32[3,80,256]{2,1,0:T(8,128)S(1)} %pad_maximum_fusion.refs_0_, f32[3,80,8]{2,1,0:T(8,128)S(1)} %collective-permute-done.16.refs_1_, ...), custom_call_target="tpu_custom_call", output_to_operand_aliasing={{1}: (5, {})} | custom-call | bytes 8519680 | tf_op jit(solution)/shard_map/conduct_and_put/pallas_call | solution.py:65
  (107 shorter events, 33.9 us)
Async XLA Ops:
  6.3 75.2 %all-to-all-start = ((bf16[32,3,128,128]{3,2,1,0:T(8,128)(2,1)}), bf16[32,3,128,128]{3,2,1,0:T(8,128)(2,1)S(1)}, u32[]{:S(2)}, u32[]{:S(2)}) async-start(bf16[32,3,128,128]{3,2,1,0:T(8,128)(2,1)} %bitcast.176), calls=%async_computation | async-start | bytes 6291456 | tf_op jit(solution)/shard_map/all_to_all | solution.py:485
  13.5 21.1 %collective-permute-start.6 = (s32[4,16]{1,0:T(4,128)S(1)}, s32[4,16]{1,0:T(4,128)S(1)}, u32[]{:S(2)}, u32[]{:S(2)}) collective-permute-start(s32[4,16]{1,0:T(4,128)S(1)} %get-tuple-element.36), channel_id=1, source_target_pairs={{0,28},{4,24},{8,20},{12,16},{16,12},{20,8},{24,4},{28,0},{1,29},{... | collective-permute-start | bytes 776 | tf_op jit(solution)/shard_map/ppermute | solution.py:480
  15.6 18.9 %collective-permute-start.5 = (s32[4,16]{1,0:T(4,128)S(1)}, s32[4,16]{1,0:T(4,128)S(1)}, u32[]{:S(2)}, u32[]{:S(2)}) collective-permute-start(s32[4,16]{1,0:T(4,128)S(1)} %get-tuple-element.37), channel_id=1, source_target_pairs={{0,24},{4,28},{8,16},{12,20},{16,8},{20,12},{24,0},{28,4},{1,25},{... | collective-permute-start | bytes 776 | tf_op jit(solution)/shard_map/ppermute | solution.py:480
  16.2 18.3 %collective-permute-start.4 = (s32[4,16]{1,0:T(4,128)S(1)}, s32[4,16]{1,0:T(4,128)S(1)}, u32[]{:S(2)}, u32[]{:S(2)}) collective-permute-start(s32[4,16]{1,0:T(4,128)S(1)} %get-tuple-element.38), channel_id=1, source_target_pairs={{0,20},{4,16},{8,28},{12,24},{16,4},{20,0},{24,12},{28,8},{1,21},{... | collective-permute-start | bytes 776 | tf_op jit(solution)/shard_map/ppermute | solution.py:480
  17.3 17.1 %collective-permute-start.3 = (s32[4,16]{1,0:T(4,128)S(1)}, s32[4,16]{1,0:T(4,128)S(1)}, u32[]{:S(2)}, u32[]{:S(2)}) collective-permute-start(s32[4,16]{1,0:T(4,128)S(1)} %get-tuple-element.39), channel_id=1, source_target_pairs={{0,16},{4,20},{8,24},{12,28},{16,0},{20,4},{24,8},{28,12},{1,17},{... | collective-permute-start | bytes 776 | tf_op jit(solution)/shard_map/ppermute | solution.py:480
  17.9 1.2 collective-permute-start
  19.0 12.4 %collective-permute-start.1 = (s32[4,16]{1,0:T(4,128)S(1)}, s32[4,16]{1,0:T(4,128)S(1)}, u32[]{:S(2)}, u32[]{:S(2)}) collective-permute-start(s32[4,16]{1,0:T(4,128)S(1)} %get-tuple-element.41), channel_id=1, source_target_pairs={{0,8},{4,12},{8,0},{12,4},{16,24},{20,28},{24,16},{28,20},{1,9},{5... | collective-permute-start | bytes 776 | tf_op jit(solution)/shard_map/ppermute | solution.py:480
  31.4 3.0 %collective-permute-start.2 = (s32[4,16]{1,0:T(4,128)S(1)}, s32[4,16]{1,0:T(4,128)S(1)}, u32[]{:S(2)}, u32[]{:S(2)}) collective-permute-start(s32[4,16]{1,0:T(4,128)S(1)} %get-tuple-element.40), channel_id=1, source_target_pairs={{0,12},{4,8},{8,4},{12,0},{16,28},{20,24},{24,20},{28,16},{1,13},{... | collective-permute-start | bytes 776 | tf_op jit(solution)/shard_map/ppermute | solution.py:480
  34.6 53.4 %collective-permute-start.9 = (s32[8,1,16]{2,1,0:T(1,128)S(1)}, s32[8,1,16]{2,1,0:T(1,128)S(1)}, u32[]{:S(2)}, u32[]{:S(2)}) collective-permute-start(s32[8,1,16]{2,1,0:T(1,128)S(1)} %get-tuple-element.44), channel_id=1, source_target_pairs={{0,3},{1,2},{2,1},{3,0},{4,7},{5,6},{6,5},{7,4},{8,11},{9,10},{10,... | collective-permute-start | bytes 1544 | tf_op jit(solution)/shard_map/ppermute | solution.py:480
  37.5 50.6 %collective-permute-start.8 = (s32[8,1,16]{2,1,0:T(1,128)S(1)}, s32[8,1,16]{2,1,0:T(1,128)S(1)}, u32[]{:S(2)}, u32[]{:S(2)}) collective-permute-start(s32[8,1,16]{2,1,0:T(1,128)S(1)} %get-tuple-element.45), channel_id=1, source_target_pairs={{0,2},{1,3},{2,0},{3,1},{4,6},{5,7},{6,4},{7,5},{8,10},{9,11},{10,... | collective-permute-start | bytes 1544 | tf_op jit(solution)/shard_map/ppermute | solution.py:480
  39.9 48.2 %collective-permute-start.7 = (s32[8,1,16]{2,1,0:T(1,128)S(1)}, s32[8,1,16]{2,1,0:T(1,128)S(1)}, u32[]{:S(2)}, u32[]{:S(2)}) collective-permute-start(s32[8,1,16]{2,1,0:T(1,128)S(1)} %get-tuple-element.46), channel_id=1, source_target_pairs={{0,1},{1,0},{2,3},{3,2},{4,5},{5,4},{6,7},{7,6},{8,9},{9,8},{10,11... | collective-permute-start | bytes 1544 | tf_op jit(solution)/shard_map/ppermute | solution.py:480
  81.5 40.3 %all-to-all-start.2 = ((bf16[32,1,128,128]{3,2,1,0:T(8,128)(2,1)}), bf16[32,1,128,128]{3,2,1,0:T(8,128)(2,1)}, u32[]{:S(2)}, u32[]{:S(2)}) async-start(bf16[32,1,128,128]{3,2,1,0:T(8,128)(2,1)} %bitcast.177), calls=%async_computation.2 | async-start | bytes 2097152 | tf_op jit(solution)/shard_map/all_to_all | solution.py:485
  106.4 2.2 collective-permute-start.10
  106.7 2.7 %collective-permute-start.11 = (bf16[8,64,512]{2,1,0:T(8,128)(2,1)}, bf16[8,64,512]{2,1,0:T(8,128)(2,1)S(1)}, u32[]{:S(2)}, u32[]{:S(2)}) collective-permute-start(bf16[8,64,512]{2,1,0:T(8,128)(2,1)} %get-tuple-element.18), channel_id=1, source_target_pairs={{0,4},{4,0},{8,12},{12,8},{16,20},{20,16},{24,28},{28,24},{1,5},{5... | collective-permute-start | bytes 1572872 | tf_op jit(solution)/shard_map/ppermute | solution.py:480
  121.8 52.5 %all-to-all-start.1 = ((bf16[32,2,64,256]{3,2,1,0:T(8,128)(2,1)}), bf16[32,2,64,256]{3,2,1,0:T(8,128)(2,1)S(1)}, u32[]{:S(2)}, u32[]{:S(2)}) async-start(bf16[32,2,64,256]{3,2,1,0:T(8,128)(2,1)} %bitcast.179), calls=%async_computation.1 | async-start | bytes 4194304 | tf_op jit(solution)/shard_map/all_to_all | solution.py:485
  127.7 2.0 collective-permute-start.12
  147.4 2.1 collective-permute-start.13
  150.3 24.0 %copy-start.5 = (s32[8]{0:T(128)S(1)}, s32[8]{0:T(128)}, u32[]{:S(2)}) copy-start(s32[8]{0:T(128)} %stack.127.at_ref) | copy-start | bytes 100
  176.8 42.8 %copy-start.2 = (bf16[4,8,5,16,256]{4,3,2,1,0:T(8,128)(2,1)}, bf16[4,8,5,16,256]{4,3,2,1,0:T(8,128)(2,1)S(1)}, u32[]{:S(2)}) copy-start(bf16[4,8,5,16,256]{4,3,2,1,0:T(8,128)(2,1)S(1)} %wall_lines.1.refs_7_) | copy-start | bytes 3932164
  215.2 29.7 %all-to-all-start.4 = ((bf16[32,1,64,256]{3,2,1,0:T(8,128)(2,1)}), bf16[32,1,64,256]{3,2,1,0:T(8,128)(2,1)}, u32[]{:S(2)}, u32[]{:S(2)}) async-start(bf16[32,1,64,256]{3,2,1,0:T(8,128)(2,1)} %bitcast.175), calls=%async_computation.4 | async-start | bytes 2097152 | tf_op jit(solution)/shard_map/all_to_all | solution.py:485
  223.1 3.4 %collective-permute-start.14 = (f32[3,8,256]{2,1,0:T(8,128)S(1)}, f32[3,8,256]{2,1,0:T(8,128)S(1)}, u32[]{:S(2)}, u32[]{:S(2)}) collective-permute-start(f32[3,8,256]{2,1,0:T(8,128)S(1)} %get-tuple-element.30), channel_id=1, source_target_pairs={{0,4},{4,8},{8,12},{12,16},{16,20},{20,24},{24,28},{1,5},{5,9},{9,... | collective-permute-start | bytes 73736 | tf_op jit(solution)/shard_map/ppermute | solution.py:27
  225.1 4.0 %collective-permute-start.15 = (f32[3,8,256]{2,1,0:T(8,128)S(1)}, f32[3,8,256]{2,1,0:T(8,128)S(1)}, u32[]{:S(2)}, u32[]{:S(2)}) collective-permute-start(f32[3,8,256]{2,1,0:T(8,128)S(1)} %get-tuple-element.31), channel_id=1, source_target_pairs={{4,0},{8,4},{12,8},{16,12},{20,16},{24,20},{28,24},{5,1},{9,5},{13... | collective-permute-start | bytes 73736 | tf_op jit(solution)/shard_map/ppermute | solution.py:30
  230.2 17.1 %collective-permute-start.17 = (f32[3,80,8]{2,1,0:T(8,128)S(1)}, f32[3,80,8]{2,1,0:T(8,128)S(1)}, u32[]{:S(2)}, u32[]{:S(2)}) collective-permute-start(f32[3,80,8]{2,1,0:T(8,128)S(1)} %get-tuple-element.28), channel_id=1, source_target_pairs={{1,0},{2,1},{3,2},{5,4},{6,5},{7,6},{9,8},{10,9},{11,10},{13,12},{... | collective-permute-start | bytes 23048 | tf_op jit(solution)/shard_map/ppermute | solution.py:30
  232.6 14.7 %collective-permute-start.16 = (f32[3,80,8]{2,1,0:T(8,128)S(1)}, f32[3,80,8]{2,1,0:T(8,128)S(1)}, u32[]{:S(2)}, u32[]{:S(2)}) collective-permute-start(f32[3,80,8]{2,1,0:T(8,128)S(1)} %get-tuple-element.29), channel_id=1, source_target_pairs={{0,1},{1,2},{2,3},{4,5},{5,6},{6,7},{8,9},{9,10},{10,11},{12,13},{... | collective-permute-start | bytes 23048 | tf_op jit(solution)/shard_map/ppermute | solution.py:27
  (25 other events, 176.8 us)

commit v4 on v3

--- a/solution.py
+++ b/solution.py
@@ -95,37 +95,81 @@
     groups = layers // across_py
     members = across_px // groups
     part = yb // members
-
-    def kernel(at, *refs):
-        for n in range(len(which)):
-            for g in range(groups):
-                for k in range(members):
-                    refs[-1][0, g * members + k, n] = refs[n][0, g, :, k * part : (k + 1) * part]
+    many = len(which)
+    shape = (across_py, groups, members, many, xb, part)
+
+    def copying(at, fields_ref, out, held, arrived, left):
+        loads = [
+            [
+                pltpu.make_async_copy(
+                    fields_ref.at[f, pl.ds(y * groups, groups), :, pl.ds(k * part, part)],
+                    held.at[y, :, k, n],
+                    arrived.at[y, k, n],
+                )
+                for k in range(members)
+                for n, f in enumerate(which)
+            ]
+            for y in range(across_py)
+        ]
+        stores = [
+            pltpu.make_async_copy(held.at[y], out.at[y], left.at[y]) for y in range(across_py)
+        ]
+        for block in loads:
+            for copy in block:
+                copy.start()
+        for block, store in zip(loads, stores):
+            for copy in block:
+                copy.wait()
+            store.start()
+        for store in stores:
+            store.wait()
+
+    def slicing(at, *refs):
+        for n in range(many):
+            for k in range(members):
+                refs[-1][0, :, k, n] = refs[n][0, :, :, k * part : (k + 1) * part]
 
     def field(f):
         return pl.BlockSpec((1, groups, xb, yb), lambda i, at: (f, i, 0, 0))
 
-    shape = (across_py, across_px, len(which), xb, part)
-    return chain.run(
-        "cut",
-        kernel,
-        [fields] * len(which),
-        [field(f) for f in which],
-        [pl.BlockSpec((1,) + shape[1:], lambda i, at: (i, 0, 0, 0, 0))],
-        [jax.ShapeDtypeStruct(shape, fields.dtype)],
-        grid=(across_py,),
-        limit=MOST_VMEM_BYTES,
-    )[0]
-
-
-def x_pass(chain, which, operators, viscosity, arrived, members, speed):
-    across_py, across_px, fields, xb, part = arrived.shape
+    if in_order(part):
+        out = chain.run(
+            "cut",
+            copying,
+            [fields],
+            [anywhere],
+            [anywhere],
+            [jax.ShapeDtypeStruct(shape, fields.dtype)],
+            scratch=[
+                pltpu.VMEM(shape, fields.dtype),
+                pltpu.SemaphoreType.DMA((across_py, members, many)),
+                pltpu.SemaphoreType.DMA((across_py,)),
+            ],
+        )[0]
+    else:
+        out = chain.run(
+            "cut",
+            slicing,
+            [fields] * many,
+            [field(f) for f in which],
+            [pl.BlockSpec((1,) + shape[1:], lambda i, at: (i, 0, 0, 0, 0, 0))],
+            [jax.ShapeDtypeStruct(shape, fields.dtype)],
+            grid=(across_py,),
+            limit=SMALL_VMEM_BYTES,
+        )[0]
+    return out.reshape((across_py, across_px) + shape[3:])
+
+
+def x_pass(chain, which, operators, viscosity, arrived, at_fields, members, speed):
+    across_py, across_px, held, xb, part = arrived.shape
+    fields = len(which)
     width = across_py * part
     length = across_px * xb
     rows = xb // members
     many = min(across_px, max(1, 256 // rows))
     steps = across_px // many
-    first = which[0] == U
+    first = speed is None
+    only = fields == 1
 
     def kernel(at, visc_ref, op_ref, arrived_ref, *refs):
         speed_ref, outs, lines = refs[0], refs[1:-1], refs[-1]
@@ -136,13 +180,16 @@
 
         @pl.when(step == 0)
         def _():
-            for n in range(fields):
-                for x in range(across_px):
-                    for y in range(across_py):
+            for x in range(across_px):
+                rows_of = slice(x * xb, (x + 1) * xb)
+                for y in range(across_py):
+                    for n, field in enumerate(which):
                         start = n * width + y * part
-                        lines[x * xb : (x + 1) * xb, start : start + part] = arrived_ref[y, x, n]
-            if first:
-                speed_ref[...] = lines[:, :width]
+                        piece = arrived_ref[y, x, 0 if only else at_fields.index(field)]
+                        lines[rows_of, start : start + part] = piece
+                    if first:
+                        piece = arrived_ref[y, x, at_fields.index(U)]
+                        speed_ref[rows_of, y * part : (y + 1) * part] = piece
 
         block = op_ref[...].reshape(3 * many * rows, length)
         whole_result = jnp.dot(block, lines[...], preferred_element_type=jnp.float32)
@@ -175,7 +222,10 @@
     in_specs = [
         smem,
         pl.BlockSpec((3, many, 1, rows, length), lambda i, at: (0,) + place_of(i, at)),
-        whole(arrived.shape),
+        pl.BlockSpec(
+            (across_py, across_px, 1 if only else held, xb, part),
+            lambda i, at: (0, 0, at_fields.index(which[0]) if only else 0, 0, 0),
+        ),
     ]
     args = [viscosity, operators.reshape(3, across_px, members, rows, length), arrived]
     out_specs = [out_block(r) for _ in which for r in range(members)]
@@ -240,13 +290,14 @@
                             speed_ref[y, :, k * part : (k + 1) * part] = lines[0, :, start : start + part]
 
         v = speed_ref[step if first else 0].astype(jnp.float32)
+        whole_result = lax.dot_general(
+            lines[...].reshape(fields * height, length),
+            op_ref[...].reshape(3 * yb, length),
+            (((1,), (1,)), ((), ())),
+            preferred_element_type=jnp.float32,
+        )
         for n, field in enumerate(which):
-            result = lax.dot_general(
-                lines[n],
-                op_ref[...].reshape(3 * yb, length),
-                (((1,), (1,)), ((), ())),
-                preferred_element_type=jnp.float32,
-            )
+            result = whole_result[n * height : (n + 1) * height]
             value = result[:, 2 * yb :] + time_step * (
                 -v * result[:, :yb] + visc_ref[field] * result[:, yb : 2 * yb]
             )
@@ -496,9 +547,9 @@
     def forward(*which):
         return exchange(cut(chain, fields, which, across_px, across_py))
 
-    def X(arrived, *which):
+    def X(arrived, at_fields, *which):
         outs, speeds[U] = x_pass(
-            chain, which, x_operators, viscosity, arrived, members, speeds.get(U)
+            chain, which, x_operators, viscosity, arrived, at_fields, members, speeds.get(U)
         )
         for f, out in zip(which, outs):
             half[f] = along("px", out)
@@ -558,12 +609,13 @@
         ],
     )
 
+    X(most, (U, V, THETA), V, THETA)
+    first = exchange(Y(V, THETA))
+    X(most, (U, V, THETA), U)
+    second = Y(U, slots=True)
+    X(last, (W,), W)
+    third = Y(W)
     chain.last += tags
-    X(most, U, V, THETA)
-    first = exchange(Y(V, THETA))
-    second = Y(U, slots=True)
-    X(last, W)
-    third = Y(W)
     second = exchange(wall_lines(chain, first, 1, wall_tile, slot, second))
     third = exchange(third)
     new_fields = put(chain, None, first, (V, THETA), 1, fields.shape)

time: 254 us -> 248 us (0.976)
  waiting for transfers between devices: 82.7 us -> 79.1 us
  starting transfers between devices: 45.7 us -> 42.6 us
    all_to_all x4, waiting for transfers between devices: 56.8 us -> 47.4 us  [exchange(): lax.all_to_all(blocks.reshape((devices,) + blocks.shape[2:]), ('py', 'px'...]
    ppermute x14, waiting for transfers between devices: 20.9 us -> 26.6 us  [along(): lax.ppermute(piece, axis, [(i, i ^ s) for i in range(lax.axis_size(axis))])]
    ppermute x14, starting transfers between devices: 13.6 us -> 10.6 us  [along(): lax.ppermute(piece, axis, [(i, i ^ s) for i in range(lax.axis_size(axis))])]
    pallas_call x12 -> x13, Pallas kernels: 75.9 us -> 77.9 us  [run(): pl.pallas_call(body, grid_spec=pltpu.PrefetchScalarGridSpec(num_scalar_pr...]
  transfers between devices with their start and end apart: 22 -> 22, of which waited for: 12 -> 12; matrix products, arithmetic and copies ran while one was open for 1% -> 1% of each run, Pallas kernels for 26% -> 28%
where the time goes in v4:
time: 248 us; the launch traced here: 246 us
  waiting for transfers between devices  79.1 us (32%)
  Pallas kernels  77.9 us (31%)
  starting transfers between devices  42.6 us (17%)
  blocking collectives  37.4 us (15%)
  local copies, waits for them, and re-layouts  6.81 us (3%)
    pallas_call x13, Pallas kernels, run(): pl.pallas_call(body, grid_spec=pltpu.PrefetchScalarGridSpec(num_scalar_pr...  77.9 us
    all_to_all x4, waiting for transfers between devices, exchange(): lax.all_to_all(blocks.reshape((devices,) + blocks.shape[2:]), ('py', 'px'...  47.4 us
    all_to_all x1, blocking collectives, exchange(): lax.all_to_all(blocks.reshape((devices,) + blocks.shape[2:]), ('py', 'px'...  37.4 us
    ppermute x14, waiting for transfers between devices, along(): lax.ppermute(piece, axis, [(i, i ^ s) for i in range(lax.axis_size(axis))])  26.6 us
    all_to_all x4, starting transfers between devices, exchange(): lax.all_to_all(blocks.reshape((devices,) + blocks.shape[2:]), ('py', 'px'...  22.7 us
    ppermute x14, starting transfers between devices, along(): lax.ppermute(piece, axis, [(i, i ^ s) for i in range(lax.axis_size(axis))])  10.6 us
    ppermute x2, starting transfers between devices, margins(): lax.ppermute(lax.slice_in_dim(block, block.shape[dim] - width, None, axis...  5.61 us
    ppermute x2, waiting for transfers between devices, margins(): lax.ppermute(lax.slice_in_dim(block, 0, width, axis=dim), axis, backward)  5.04 us
  transfers between devices with their start and end apart: 22, of which 12 were waited for; matrix products, arithmetic and copies ran while one was open for 1% of the time, Pallas kernels for 28%

profile of v4, /device:TPU:8, one launch (start us, length us, event | category | flops | bytes accessed | tf_op | source)
XLA Modules:
  0.0 246.3 jit_solution(246798680723496962)
XLA Ops:
  1.3 3.8 %cut.2.refs_1_ = bf16[4,4,2,3,128,128]{5,4,3,2,1,0:T(8,128)(2,1)} custom-call(s32[8]{0:T(128)} %stack.127.at_ref, bf16[4,16,128,256]{3,2,1,0:T(8,128)(2,1)} %refs_0_.10), custom_call_target="tpu_custom_call" | custom-call | bytes 6291456 | tf_op jit(solution)/shard_map/cut/pallas_call | solution.py:65
  5.1 6.0 %all-to-all-start = ((bf16[32,3,128,128]{3,2,1,0:T(8,128)(2,1)}), bf16[32,3,128,128]{3,2,1,0:T(8,128)(2,1)S(1)}, u32[]{:S(2)}, u32[]{:S(2)}) async-start(bf16[32,3,128,128]{3,2,1,0:T(8,128)(2,1)} %bitcast.176), calls=%async_computation | async-start | bytes 6291456 | tf_op jit(solution)/shard_map/all_to_all | solution.py:536
  17.9 12.5 %collective-permute-done.6.refs_9_ = s32[4,16]{1,0:T(4,128)S(1)} collective-permute-done((s32[4,16]{1,0:T(4,128)S(1)}, s32[4,16]{1,0:T(4,128)S(1)}, u32[]{:S(2)}, u32[]{:S(2)}) %collective-permute-start.6) | collective-permute-done | bytes 288 | tf_op jit(solution)/shard_map/ppermute | solution.py:531
  30.6 2.7 %collective-permute-done.5.refs_8_ = s32[4,16]{1,0:T(4,128)S(1)} collective-permute-done((s32[4,16]{1,0:T(4,128)S(1)}, s32[4,16]{1,0:T(4,128)S(1)}, u32[]{:S(2)}, u32[]{:S(2)}) %collective-permute-start.5) | collective-permute-done | bytes 288 | tf_op jit(solution)/shard_map/ppermute | solution.py:531
  35.0 2.8 %cut.3.refs_3_ = bf16[4,4,2,1,128,128]{5,4,3,2,1,0:T(8,128)(2,1)} custom-call(s32[8]{0:T(128)} %stack.127.at_ref, bf16[4,16,128,256]{3,2,1,0:T(8,128)(2,1)} %refs_0_.10, bf16[4,4,2,3,128,128]{5,4,3,2,1,0:T(8,128)(2,1)} %cut.2.refs_1_, s32[4,16]{1,0:T(4,128)} %get-tuple-element.43.refs_2_, s32[4,16]{1,0:T(4,128)} %copy-done.24, s32[4,16]{1,0:T(4,128)} %copy-done.22, ...), custom_call_target="tpu_custom_call" | custom-call | bytes 2097152 | tf_op jit(solution)/shard_map/cut/pallas_call | solution.py:65
  37.8 42.3 %all-to-all-done = bf16[32,3,128,128]{3,2,1,0:T(8,128)(2,1)S(1)} async-done(((bf16[32,3,128,128]{3,2,1,0:T(8,128)(2,1)}), bf16[32,3,128,128]{3,2,1,0:T(8,128)(2,1)S(1)}, u32[]{:S(2)}, u32[]{:S(2)}) %all-to-all-start) | async-done | bytes 3145760 | tf_op jit(solution)/shard_map/all_to_all | solution.py:536
  80.1 6.5 %all-to-all-start.2 = ((bf16[32,1,128,128]{3,2,1,0:T(8,128)(2,1)}), bf16[32,1,128,128]{3,2,1,0:T(8,128)(2,1)}, u32[]{:S(2)}, u32[]{:S(2)}) async-start(bf16[32,1,128,128]{3,2,1,0:T(8,128)(2,1)} %bitcast.177), calls=%async_computation.2 | async-start | bytes 2097152 | tf_op jit(solution)/shard_map/all_to_all | solution.py:536
  86.6 13.8 %x_pass.3 = (bf16[8,64,512]{2,1,0:T(8,128)(2,1)}, bf16[8,64,512]{2,1,0:T(8,128)(2,1)}, bf16[8,64,512]{2,1,0:T(8,128)(2,1)}, bf16[8,64,512]{2,1,0:T(8,128)(2,1)}, bf16[1024,512]{1,0:T(8,128)(2,1)}) custom-call(s32[8]{0:T(128)} %stack.127.at_ref, f32[4]{0:T(128)} %refs_0_.16, bf16[3,8,2,64,1024]{4,3,2,1,0:T(8,128)(2,1)} %bitcast.183, ...), custom_call_target="tpu_custom_call" | custom-call | flops 6442450944 | bytes 6291456 | tf_op jit(solution)/shard_map/x_pass/pallas_call | solution.py:65
  104.3 11.6 %y_pass.3 = (bf16[4,8,2,64,256]{4,3,2,1,0:T(8,128)(2,1)}, bf16[4,512,256]{2,1,0:T(8,128)(2,1)}) custom-call(s32[8]{0:T(128)} %stack.127.at_ref, f32[4]{0:T(128)} %refs_0_.16, bf16[3,1024,1024]{2,1,0:T(8,128)(2,1)} %refs_1_.6, bf16[8,64,512]{2,1,0:T(8,128)(2,1)} %get-tuple-element.15.refs_2_, bf16[8,64,512]{2,1,0:T(8,128)(2,1)} %copy-done.31, ...), custom_call_target="tpu_custom_call" | custom-call | flops 6442450944 | bytes 6291456 | tf_op jit(solution)/shard_map/y_pass/pallas_call | solution.py:65
  115.9 5.8 %all-to-all-start.1 = ((bf16[32,2,64,256]{3,2,1,0:T(8,128)(2,1)}), bf16[32,2,64,256]{3,2,1,0:T(8,128)(2,1)S(1)}, u32[]{:S(2)}, u32[]{:S(2)}) async-start(bf16[32,2,64,256]{3,2,1,0:T(8,128)(2,1)} %bitcast.180), calls=%async_computation.1 | async-start | bytes 4194304 | tf_op jit(solution)/shard_map/all_to_all | solution.py:536
  121.9 8.6 %x_pass.4 = (bf16[8,64,512]{2,1,0:T(8,128)(2,1)}, bf16[8,64,512]{2,1,0:T(8,128)(2,1)}) custom-call(s32[8]{0:T(128)} %stack.127.at_ref, f32[4]{0:T(128)} %refs_0_.16, bf16[3,8,2,64,1024]{4,3,2,1,0:T(8,128)(2,1)} %bitcast.184, bf16[4,8,3,128,128]{4,3,2,1,0:T(8,128)(2,1)} %bitcast.179, bf16[8,2,64,512]{3,2,1,0:T(8,128)(2,1)} %bitcast.186, ...), custom_call_target="tpu_custom_call" | custom-call | flops 3221225472 | bytes 2097152 | tf_op jit(solution)/shard_map/x_pass/pallas_call | solution.py:65
  133.4 8.2 %y_pass.4.refs_4_.refs_3_ = bf16[4,8,5,16,256]{4,3,2,1,0:T(8,128)(2,1)} custom-call(s32[8]{0:T(128)} %stack.127.at_ref, f32[4]{0:T(128)} %refs_0_.16, bf16[3,1024,1024]{2,1,0:T(8,128)(2,1)} %refs_1_.6, bf16[8,64,512]{2,1,0:T(8,128)(2,1)} %get-tuple-element.22.refs_2_, bf16[8,64,512]{2,1,0:T(8,128)(2,1)} %copy-done.30, ...), custom_call_target="tpu_custom_call" | custom-call | flops 3221225472 | bytes 2621440 | tf_op jit(solution)/shard_map/y_pass/pallas_call | solution.py:65
  141.7 8.6 %x_pass.5 = (bf16[8,64,512]{2,1,0:T(8,128)(2,1)}, bf16[8,64,512]{2,1,0:T(8,128)(2,1)}) custom-call(s32[8]{0:T(128)} %stack.127.at_ref, f32[4]{0:T(128)} %refs_0_.16, bf16[3,8,2,64,1024]{4,3,2,1,0:T(8,128)(2,1)} %bitcast.185, bf16[4,8,1,128,128]{4,3,2,1,0:T(8,128)(2,1)} %bitcast.26.refs_2_, bf16[8,2,64,512]{3,2,1,0:T(8,128)(2,1)} %bitcast.187, ...), custom_call_target="tpu_custom_call" | custom-call | flops 3221225472 | bytes 2097152 | tf_op jit(solution)/shard_map/x_pass/pallas_call | solution.py:65
  155.3 8.3 %y_pass.5.refs_4_ = bf16[4,8,1,64,256]{4,3,2,1,0:T(8,128)(2,1)} custom-call(s32[8]{0:T(128)} %stack.127.at_ref, f32[4]{0:T(128)} %refs_0_.16, bf16[3,1024,1024]{2,1,0:T(8,128)(2,1)} %refs_1_.6, bf16[8,64,512]{2,1,0:T(8,128)(2,1)} %get-tuple-element.24.refs_2_, bf16[8,64,512]{2,1,0:T(8,128)(2,1)} %copy-done.29, bf16[4,512,256]{2,1,0:T(8,128)(2,1)} %get-tuple-element.21.refs_4_), custom_call_target="tpu_custom_call" | custom-call | flops 3221225472 | bytes 2097152 | tf_op jit(solution)/shard_map/y_pass/pallas_call | solution.py:65
  163.6 6.1 %collective-permute-done.13.refs_8_.refs_6_ = s32[8,1,16]{2,1,0:T(1,128)S(1)} collective-permute-done((s32[8,1,16]{2,1,0:T(1,128)S(1)}, s32[8,1,16]{2,1,0:T(1,128)S(1)}, u32[]{:S(2)}, u32[]{:S(2)}) %collective-permute-start.13) | collective-permute-done | bytes 544 | tf_op jit(solution)/shard_map/ppermute | solution.py:531
  172.3 37.4 %all_to_all.25 = bf16[32,5,16,256]{3,2,1,0:T(8,128)(2,1)} all-to-all(bf16[32,5,16,256]{3,2,1,0:T(8,128)(2,1)S(1)} %bitcast.174), channel_id=1, replica_groups=mesh['px'=8,'py'=4] {'py','px'}, dimensions={0} | all-to-all | bytes 2621440 | tf_op jit(solution)/shard_map/all_to_all | solution.py:536
  209.6 4.3 %all-to-all-start.4 = ((bf16[32,1,64,256]{3,2,1,0:T(8,128)(2,1)}), bf16[32,1,64,256]{3,2,1,0:T(8,128)(2,1)}, u32[]{:S(2)}, u32[]{:S(2)}) async-start(bf16[32,1,64,256]{3,2,1,0:T(8,128)(2,1)} %bitcast.175), calls=%async_computation.4 | async-start | bytes 2097152 | tf_op jit(solution)/shard_map/all_to_all | solution.py:536
  213.9 2.7 %add_flux.1.refs_5_ = f32[3,64,256]{2,1,0:T(8,128)} custom-call(s32[8]{0:T(128)} %stack.127.at_ref, f32[64,256]{1,0:T(8,128)} %refs_0_.17, f32[64,256]{1,0:T(8,128)} %refs_1_.7, bf16[4,8,5,16,256]{4,3,2,1,0:T(8,128)(2,1)} %bitcast.172, s32[8,1,16]{2,1,0:T(1,128)} %copy-done.7, s32[8,1,16]{2,1,0:T(1,128)} %copy-done.10, s32[8,1,16]{2,1,0:T(1,128)} %copy-done.9, ...), custom_call_target="tpu_custom_call" | custom-call | bytes 393216 | tf_op jit(solution)/shard_map/add_flux/pallas_call | solution.py:65
  220.7 2.7 %collective-permute-done.15 = f32[3,8,256]{2,1,0:T(8,128)S(1)} collective-permute-done((f32[3,8,256]{2,1,0:T(8,128)S(1)}, f32[3,8,256]{2,1,0:T(8,128)S(1)}, u32[]{:S(2)}, u32[]{:S(2)}) %collective-permute-start.15) | collective-permute-done | bytes 24608 | tf_op jit(solution)/shard_map/ppermute | solution.py:30
  224.5 2.4 collective-permute-start.17
  226.9 3.6 %collective-permute-start.16 = (f32[3,80,8]{2,1,0:T(8,128)S(1)}, f32[3,80,8]{2,1,0:T(8,128)S(1)}, u32[]{:S(2)}, u32[]{:S(2)}) collective-permute-start(f32[3,80,8]{2,1,0:T(8,128)S(1)} %get-tuple-element.29), channel_id=1, source_target_pairs={{0,1},{1,2},{2,3},{4,5},{5,6},{6,7},{8,9},{9,10},{10,11},{12,13},{... | collective-permute-start | bytes 23048 | tf_op jit(solution)/shard_map/ppermute | solution.py:27
  234.2 5.1 %all-to-all-done.4 = bf16[32,1,64,256]{3,2,1,0:T(8,128)(2,1)} async-done(((bf16[32,1,64,256]{3,2,1,0:T(8,128)(2,1)}), bf16[32,1,64,256]{3,2,1,0:T(8,128)(2,1)}, u32[]{:S(2)}, u32[]{:S(2)}) %all-to-all-start.4) | async-done | bytes 1048608 | tf_op jit(solution)/shard_map/all_to_all | solution.py:536
  239.3 2.3 collective-permute-done.17.refs_2_
  241.6 4.7 %conduct_and_put.1 = (f32[64,256]{1,0:T(8,128)}, bf16[4,16,128,256]{3,2,1,0:T(8,128)(2,1)}) custom-call(s32[8]{0:T(128)S(1)} %copy-done.6, f32[3,80,256]{2,1,0:T(8,128)S(1)} %pad_maximum_fusion.refs_0_, f32[3,80,8]{2,1,0:T(8,128)S(1)} %collective-permute-done.16.refs_1_, ...), custom_call_target="tpu_custom_call", output_to_operand_aliasing={{1}: (5, {})} | custom-call | bytes 8519680 | tf_op jit(solution)/shard_map/conduct_and_put/pallas_call | solution.py:65
  (120 shorter events, 32.3 us)
Async XLA Ops:
  5.1 75.0 %all-to-all-start = ((bf16[32,3,128,128]{3,2,1,0:T(8,128)(2,1)}), bf16[32,3,128,128]{3,2,1,0:T(8,128)(2,1)S(1)}, u32[]{:S(2)}, u32[]{:S(2)}) async-start(bf16[32,3,128,128]{3,2,1,0:T(8,128)(2,1)} %bitcast.176), calls=%async_computation | async-start | bytes 6291456 | tf_op jit(solution)/shard_map/all_to_all | solution.py:536
  12.2 18.2 %collective-permute-start.6 = (s32[4,16]{1,0:T(4,128)S(1)}, s32[4,16]{1,0:T(4,128)S(1)}, u32[]{:S(2)}, u32[]{:S(2)}) collective-permute-start(s32[4,16]{1,0:T(4,128)S(1)} %get-tuple-element.36), channel_id=1, source_target_pairs={{0,28},{4,24},{8,20},{12,16},{16,12},{20,8},{24,4},{28,0},{1,29},{... | collective-permute-start | bytes 776 | tf_op jit(solution)/shard_map/ppermute | solution.py:531
  14.4 18.9 %collective-permute-start.5 = (s32[4,16]{1,0:T(4,128)S(1)}, s32[4,16]{1,0:T(4,128)S(1)}, u32[]{:S(2)}, u32[]{:S(2)}) collective-permute-start(s32[4,16]{1,0:T(4,128)S(1)} %get-tuple-element.37), channel_id=1, source_target_pairs={{0,24},{4,28},{8,16},{12,20},{16,8},{20,12},{24,0},{28,4},{1,25},{... | collective-permute-start | bytes 776 | tf_op jit(solution)/shard_map/ppermute | solution.py:531
  14.9 18.3 %collective-permute-start.4 = (s32[4,16]{1,0:T(4,128)S(1)}, s32[4,16]{1,0:T(4,128)S(1)}, u32[]{:S(2)}, u32[]{:S(2)}) collective-permute-start(s32[4,16]{1,0:T(4,128)S(1)} %get-tuple-element.38), channel_id=1, source_target_pairs={{0,20},{4,16},{8,28},{12,24},{16,4},{20,0},{24,12},{28,8},{1,21},{... | collective-permute-start | bytes 776 | tf_op jit(solution)/shard_map/ppermute | solution.py:531
  16.1 17.2 %collective-permute-start.3 = (s32[4,16]{1,0:T(4,128)S(1)}, s32[4,16]{1,0:T(4,128)S(1)}, u32[]{:S(2)}, u32[]{:S(2)}) collective-permute-start(s32[4,16]{1,0:T(4,128)S(1)} %get-tuple-element.39), channel_id=1, source_target_pairs={{0,16},{4,20},{8,24},{12,28},{16,0},{20,4},{24,8},{28,12},{1,17},{... | collective-permute-start | bytes 776 | tf_op jit(solution)/shard_map/ppermute | solution.py:531
  16.6 16.7 %collective-permute-start.2 = (s32[4,16]{1,0:T(4,128)S(1)}, s32[4,16]{1,0:T(4,128)S(1)}, u32[]{:S(2)}, u32[]{:S(2)}) collective-permute-start(s32[4,16]{1,0:T(4,128)S(1)} %get-tuple-element.40), channel_id=1, source_target_pairs={{0,12},{4,8},{8,4},{12,0},{16,28},{20,24},{24,20},{28,16},{1,13},{... | collective-permute-start | bytes 776 | tf_op jit(solution)/shard_map/ppermute | solution.py:531
  30.4 3.6 %collective-permute-start.1 = (s32[4,16]{1,0:T(4,128)S(1)}, s32[4,16]{1,0:T(4,128)S(1)}, u32[]{:S(2)}, u32[]{:S(2)}) collective-permute-start(s32[4,16]{1,0:T(4,128)S(1)} %get-tuple-element.41), channel_id=1, source_target_pairs={{0,8},{4,12},{8,0},{12,4},{16,24},{20,28},{24,16},{28,20},{1,9},{5... | collective-permute-start | bytes 776 | tf_op jit(solution)/shard_map/ppermute | solution.py:531
  33.3 1.2 collective-permute-start
  80.1 35.7 %all-to-all-start.2 = ((bf16[32,1,128,128]{3,2,1,0:T(8,128)(2,1)}), bf16[32,1,128,128]{3,2,1,0:T(8,128)(2,1)}, u32[]{:S(2)}, u32[]{:S(2)}) async-start(bf16[32,1,128,128]{3,2,1,0:T(8,128)(2,1)} %bitcast.177), calls=%async_computation.2 | async-start | bytes 2097152 | tf_op jit(solution)/shard_map/all_to_all | solution.py:536
  100.5 2.2 collective-permute-start.7
  100.7 2.7 %collective-permute-start.8 = (bf16[8,64,512]{2,1,0:T(8,128)(2,1)}, bf16[8,64,512]{2,1,0:T(8,128)(2,1)S(1)}, u32[]{:S(2)}, u32[]{:S(2)}) collective-permute-start(bf16[8,64,512]{2,1,0:T(8,128)(2,1)} %get-tuple-element.18), channel_id=1, source_target_pairs={{0,4},{4,0},{8,12},{12,8},{16,20},{20,16},{24,28},{28,24},{1,5},{5... | collective-permute-start | bytes 1572872 | tf_op jit(solution)/shard_map/ppermute | solution.py:531
  115.9 53.9 %all-to-all-start.1 = ((bf16[32,2,64,256]{3,2,1,0:T(8,128)(2,1)}), bf16[32,2,64,256]{3,2,1,0:T(8,128)(2,1)S(1)}, u32[]{:S(2)}, u32[]{:S(2)}) async-start(bf16[32,2,64,256]{3,2,1,0:T(8,128)(2,1)} %bitcast.180), calls=%async_computation.1 | async-start | bytes 4194304 | tf_op jit(solution)/shard_map/all_to_all | solution.py:536
  130.5 2.1 collective-permute-start.9
  150.2 4.3 %collective-permute-start.10 = (bf16[8,64,512]{2,1,0:T(8,128)(2,1)}, bf16[8,64,512]{2,1,0:T(8,128)(2,1)S(1)}, u32[]{:S(2)}, u32[]{:S(2)}) collective-permute-start(bf16[8,64,512]{2,1,0:T(8,128)(2,1)} %get-tuple-element.25), channel_id=1, source_target_pairs={{0,4},{4,0},{8,12},{12,8},{16,20},{20,16},{24,28},{28,24},{1,5},{5... | collective-permute-start | bytes 1572872 | tf_op jit(solution)/shard_map/ppermute | solution.py:531
  150.5 19.2 %collective-permute-start.13 = (s32[8,1,16]{2,1,0:T(1,128)S(1)}, s32[8,1,16]{2,1,0:T(1,128)S(1)}, u32[]{:S(2)}, u32[]{:S(2)}) collective-permute-start(s32[8,1,16]{2,1,0:T(1,128)S(1)} %get-tuple-element.44), channel_id=1, source_target_pairs={{0,3},{1,2},{2,1},{3,0},{4,7},{5,6},{6,5},{7,4},{8,11},{9,10},{10,... | collective-permute-start | bytes 1544 | tf_op jit(solution)/shard_map/ppermute | solution.py:531
  152.1 17.6 %collective-permute-start.12 = (s32[8,1,16]{2,1,0:T(1,128)S(1)}, s32[8,1,16]{2,1,0:T(1,128)S(1)}, u32[]{:S(2)}, u32[]{:S(2)}) collective-permute-start(s32[8,1,16]{2,1,0:T(1,128)S(1)} %get-tuple-element.45), channel_id=1, source_target_pairs={{0,2},{1,3},{2,0},{3,1},{4,6},{5,7},{6,4},{7,5},{8,10},{9,11},{10,... | collective-permute-start | bytes 1544 | tf_op jit(solution)/shard_map/ppermute | solution.py:531
  153.3 16.4 %collective-permute-start.11 = (s32[8,1,16]{2,1,0:T(1,128)S(1)}, s32[8,1,16]{2,1,0:T(1,128)S(1)}, u32[]{:S(2)}, u32[]{:S(2)}) collective-permute-start(s32[8,1,16]{2,1,0:T(1,128)S(1)} %get-tuple-element.46), channel_id=1, source_target_pairs={{0,1},{1,0},{2,3},{3,2},{4,5},{5,4},{6,7},{7,6},{8,9},{9,8},{10,11... | collective-permute-start | bytes 1544 | tf_op jit(solution)/shard_map/ppermute | solution.py:531
  169.7 39.9 %copy-start.8 = (s32[8,1,16]{2,1,0:T(1,128)}, s32[8,1,16]{2,1,0:T(1,128)S(1)}, u32[]{:S(2)}) copy-start(s32[8,1,16]{2,1,0:T(1,128)S(1)} %collective-permute-done.13.refs_8_.refs_6_) | copy-start | bytes 1540
  172.2 41.7 %copy-start.2 = (bf16[4,8,5,16,256]{4,3,2,1,0:T(8,128)(2,1)}, bf16[4,8,5,16,256]{4,3,2,1,0:T(8,128)(2,1)S(1)}, u32[]{:S(2)}) copy-start(bf16[4,8,5,16,256]{4,3,2,1,0:T(8,128)(2,1)S(1)} %wall_lines.1.refs_7_) | copy-start | bytes 3932164
  209.6 29.6 %all-to-all-start.4 = ((bf16[32,1,64,256]{3,2,1,0:T(8,128)(2,1)}), bf16[32,1,64,256]{3,2,1,0:T(8,128)(2,1)}, u32[]{:S(2)}, u32[]{:S(2)}) async-start(bf16[32,1,64,256]{3,2,1,0:T(8,128)(2,1)} %bitcast.175), calls=%async_computation.4 | async-start | bytes 2097152 | tf_op jit(solution)/shard_map/all_to_all | solution.py:536
  217.4 3.4 %collective-permute-start.14 = (f32[3,8,256]{2,1,0:T(8,128)S(1)}, f32[3,8,256]{2,1,0:T(8,128)S(1)}, u32[]{:S(2)}, u32[]{:S(2)}) collective-permute-start(f32[3,8,256]{2,1,0:T(8,128)S(1)} %get-tuple-element.30), channel_id=1, source_target_pairs={{0,4},{4,8},{8,12},{12,16},{16,20},{20,24},{24,28},{1,5},{5,9},{9,... | collective-permute-start | bytes 73736 | tf_op jit(solution)/shard_map/ppermute | solution.py:27
  219.4 4.0 %collective-permute-start.15 = (f32[3,8,256]{2,1,0:T(8,128)S(1)}, f32[3,8,256]{2,1,0:T(8,128)S(1)}, u32[]{:S(2)}, u32[]{:S(2)}) collective-permute-start(f32[3,8,256]{2,1,0:T(8,128)S(1)} %get-tuple-element.31), channel_id=1, source_target_pairs={{4,0},{8,4},{12,8},{16,12},{20,16},{24,20},{28,24},{5,1},{9,5},{13... | collective-permute-start | bytes 73736 | tf_op jit(solution)/shard_map/ppermute | solution.py:30
  224.5 17.1 %collective-permute-start.17 = (f32[3,80,8]{2,1,0:T(8,128)S(1)}, f32[3,80,8]{2,1,0:T(8,128)S(1)}, u32[]{:S(2)}, u32[]{:S(2)}) collective-permute-start(f32[3,80,8]{2,1,0:T(8,128)S(1)} %get-tuple-element.28), channel_id=1, source_target_pairs={{1,0},{2,1},{3,2},{5,4},{6,5},{7,6},{9,8},{10,9},{11,10},{13,12},{... | collective-permute-start | bytes 23048 | tf_op jit(solution)/shard_map/ppermute | solution.py:30
  226.9 14.7 %collective-permute-start.16 = (f32[3,80,8]{2,1,0:T(8,128)S(1)}, f32[3,80,8]{2,1,0:T(8,128)S(1)}, u32[]{:S(2)}, u32[]{:S(2)}) collective-permute-start(f32[3,80,8]{2,1,0:T(8,128)S(1)} %get-tuple-element.29), channel_id=1, source_target_pairs={{0,1},{1,2},{2,3},{4,5},{5,6},{6,7},{8,9},{9,10},{10,11},{12,13},{... | collective-permute-start | bytes 23048 | tf_op jit(solution)/shard_map/ppermute | solution.py:27
  (31 other events, 264.1 us)

commit v5 on v4

--- a/solution.py
+++ b/solution.py
@@ -251,7 +251,7 @@
     return [outs[n * members : (n + 1) * members] for n in range(fields)], outs[-1] if first else speed
 
 
-def y_pass(chain, which, operators, viscosity, parts, speed, yb, shape, block):
+def y_pass(chain, which, operators, viscosity, parts, speed, yb, shape):
     across_px, rows, width = parts[0][0].shape
     fields, members = len(parts), len(parts[0])
     part = yb // members
@@ -302,15 +302,12 @@
                 -v * result[:, :yb] + visc_ref[field] * result[:, yb : 2 * yb]
             )
             value = value.astype(jnp.bfloat16)
-            if len(which) == 1:
-                out[...] = value.reshape(block)
-            else:
-                out[0, :, n] = value.reshape(across_px, rows, yb)
+            out[0, :, n] = value.reshape(across_px, rows, yb)
 
     flat = [part for field_parts in parts for part in field_parts]
     in_specs = [smem, pl.BlockSpec((3, yb, length), lambda i, at: (0, i, 0))] + like(flat)
     args = [viscosity, operators, *flat]
-    out_specs = [pl.BlockSpec(block, lambda i, at: (i,) + (0,) * (len(block) - 1))]
+    out_specs = [pl.BlockSpec((1,) + shape[1:], lambda i, at: (i, 0, 0, 0, 0))]
     out_shape = [jax.ShapeDtypeStruct(shape, jnp.bfloat16)]
     if first:
         out_specs.append(whole((blocks, height, yb)))
@@ -357,98 +354,102 @@
     )[0]
 
 
-def wall_lines(chain, arrived, n, tile, slot, buffer):
+def wall_lines(chain, arrived, n, tile, slot, unit):
     across_py, across_px, _, rows, yb = arrived.shape
     count, span = tile.shape[0], across_px * across_py * rows
-    devices = across_px * across_py
-    units, unit = buffer.shape[2:4]
-
-    def kernel(at, tile_ref, slot_ref, arrived_ref, buffer_ref, out):
+    slots = across_py * across_px * unit
+
+    def kernel(at, tile_ref, slot_ref, arrived_ref, *refs):
+        outs, lines = refs[:-1], refs[-1]
         chosen = tile_ref[...] == lax.broadcasted_iota(jnp.int32, (count, span), 1)
         flux = jnp.dot(
             chosen.astype(jnp.float32).astype(jnp.bfloat16),
             arrived_ref[...].reshape(span, yb),
             preferred_element_type=jnp.float32,
         )
-        filled = slot_ref[...] == lax.broadcasted_iota(jnp.int32, (devices * unit, count), 0)
-        out[...] = (
-            jnp.dot(
-                filled.astype(jnp.float32).astype(jnp.bfloat16),
-                flux.astype(jnp.bfloat16),
-                preferred_element_type=jnp.float32,
-            )
-            .astype(jnp.bfloat16)
-            .reshape(across_py, across_px, 1, unit, yb)
-        )
+        filled = slot_ref[...] == lax.broadcasted_iota(jnp.int32, (slots, count), 0)
+        lines[...] = jnp.dot(
+            filled.astype(jnp.float32).astype(jnp.bfloat16),
+            flux.astype(jnp.bfloat16),
+            preferred_element_type=jnp.float32,
+        ).reshape(lines.shape)
+        for s in range(across_py):
+            outs[s][...] = lines[at[2] ^ s].astype(jnp.bfloat16)
 
     args = [tile.reshape(-1, 1), slot.reshape(1, -1)]
+    shape = (across_px, unit, yb)
     return chain.run(
         "wall_lines",
         kernel,
-        args + [arrived, buffer],
+        args + [arrived],
         like(args)
-        + [pl.BlockSpec((across_py, across_px, 1, rows, yb), lambda i, at: (0, 0, n, 0, 0)), anywhere],
-        [pl.BlockSpec((across_py, across_px, 1, unit, yb), lambda i, at: (0, 0, units - 1, 0, 0))],
-        [jax.ShapeDtypeStruct(buffer.shape, buffer.dtype)],
-        aliases={4: 0},
+        + [pl.BlockSpec((across_py, across_px, 1, rows, yb), lambda i, at: (0, 0, n, 0, 0))],
+        [whole(shape)] * across_py,
+        [jax.ShapeDtypeStruct(shape, jnp.bfloat16)] * across_py,
+        scratch=[pltpu.VMEM((across_py,) + shape, jnp.float32)],
         limit=SMALL_VMEM_BYTES,
-    )[0]
+    )
+
+
+def wall_columns(chain, pieces):
+    across_py, (across_px, unit, yb) = len(pieces), pieces[0].shape
+
+    def kernel(at, *refs):
+        outs = refs[across_py:]
+        for t in range(across_px):
+            for s in range(across_py):
+                outs[t][at[2] ^ s] = refs[s][at[7] ^ t]
+
+    shape = (across_py, unit, yb)
+    return chain.run(
+        "wall_columns",
+        kernel,
+        [*pieces],
+        like(pieces),
+        [whole(shape)] * across_px,
+        [jax.ShapeDtypeStruct(shape, jnp.bfloat16)] * across_px,
+        limit=SMALL_VMEM_BYTES,
+    )
 
 
 def add_flux(chain, tags, arrived, solid_temp, conductivity):
     rows, columns = solid_temp.shape
-    across_py, across_px, units, unit, _ = arrived.shape
-
-    def kernel(at, temp_ref, kappa_ref, arrived_ref, *refs):
-        tag_refs, out = refs[:-1], refs[-1]
+    across_px, (across_py, unit, _) = len(arrived), arrived[0].shape
+
+    def kernel(at, temp_ref, kappa_ref, *refs):
+        line_refs, tag_refs, out = refs[:across_px], refs[across_px:-1], refs[-1]
         out[0] = temp_ref[...]
         out[1] = kappa_ref[...]
         places = lax.broadcasted_iota(jnp.int32, (rows, unit), 0)
         source = jnp.zeros((rows, columns), jnp.float32)
         for s in range(across_py):
-            chosen = [tag_refs[s][at[7] ^ t] == places for t in range(across_px)]
-            chosen = jnp.concatenate([c.astype(jnp.float32) for c in chosen], axis=1)
+            chosen = [(tag_refs[s][t] == places).astype(jnp.float32) for t in range(across_px)]
+            lines = [line_refs[t][at[2] ^ s] for t in range(across_px)]
             source = source + jnp.dot(
-                chosen.astype(jnp.bfloat16),
-                arrived_ref[at[2] ^ s].reshape(across_px * unit, columns),
+                jnp.concatenate(chosen, axis=1).astype(jnp.bfloat16),
+                jnp.concatenate(lines, axis=0),
                 preferred_element_type=jnp.float32,
             )
         out[2] = (wall_gain * source_gain) * source
 
-    args = [solid_temp, conductivity]
-    lines = pl.BlockSpec(
-        (across_py, across_px, 1, unit, columns), lambda i, at: (0, 0, units - 1, 0, 0)
-    )
+    args = [solid_temp, conductivity, *arrived, *tags]
     return chain.run(
         "add_flux",
         kernel,
-        args + [arrived, *tags],
-        like(args) + [lines] + like(tags),
+        args,
+        like(args),
         [whole((3, rows, columns))],
         [jax.ShapeDtypeStruct((3, rows, columns), jnp.float32)],
+        limit=SMALL_VMEM_BYTES,
     )[0]
 
 
-def conduct_and_put(chain, solid, low, high, margin, buffer, arrived, field):
-    across_py, across_px, _, x_rows, _ = arrived.shape
-    members = buffer.shape[2] // x_rows
-    groups = across_px // members
+def conduct(chain, solid, low, high, margin):
     kinds, height, columns = solid.shape
     rows = height - 2 * margin
     wide = columns + -(-2 * margin // 128) * 128
 
-    def kernel(at, solid_ref, low_ref, high_ref, arrived_ref, buffer_ref, out, fields_ref, ext, sems):
-        copies = [
-            pltpu.make_async_copy(
-                arrived_ref.at[k, a, 0],
-                fields_ref.at[field, k * groups + a // members, pl.ds(a % members * x_rows, x_rows)],
-                sems.at[k, a],
-            )
-            for k in range(across_py)
-            for a in range(across_px)
-        ]
-        for copy in copies:
-            copy.start()
+    def kernel(at, solid_ref, low_ref, high_ref, out, ext):
         ext[:, :, columns:] = jnp.zeros((kinds, height, wide - columns), jnp.float32)
         ext[:, :, :columns] = solid_ref[...]
         ext[:, :, columns : columns + margin] = high_ref[...]
@@ -469,27 +470,18 @@
                 change = change + face * (pltpu.roll(t, shift, dim) - t)
             t = t + change
         out[...] = t[margin : margin + rows, :columns]
-        for copy in copies:
-            copy.wait()
-
-    args = [solid, low, high, arrived]
+
+    args = [solid, low, high]
     return chain.run(
-        "conduct_and_put",
-        kernel,
-        args + [buffer],
-        like(args) + [anywhere],
-        [whole((rows, columns)), anywhere],
-        [
-            jax.ShapeDtypeStruct((rows, columns), jnp.float32),
-            jax.ShapeDtypeStruct(buffer.shape, buffer.dtype),
-        ],
-        scratch=[
-            pltpu.VMEM((kinds, height, wide), jnp.float32),
-            pltpu.SemaphoreType.DMA((across_py, across_px)),
-        ],
-        aliases={5: 1},
+        "conduct",
+        kernel,
+        args,
+        like(args),
+        [whole((rows, columns))],
+        [jax.ShapeDtypeStruct((rows, columns), jnp.float32)],
+        scratch=[pltpu.VMEM((kinds, height, wide), jnp.float32)],
         limit=SMALL_VMEM_BYTES,
-    )
+    )[0]
 
 
 def on_device(
@@ -559,15 +551,8 @@
         y_columns = y_columns.reshape(3, -1, across_py, members, yb // members)
         y_columns = y_columns.swapaxes(2, 3).reshape(y_operators.shape)
 
-    x_rows = xb // members
-    unit = min(16, x_rows)
-
-    def Y(*which, slots=False):
-        shape = (across_py, across_px, len(which), x_rows, yb)
-        block = (1,) + shape[1:]
-        if slots:
-            shape = (across_py, across_px, x_rows // unit + 1, unit, yb)
-            block = (1, across_px, x_rows // unit, unit, yb)
+    def Y(*which):
+        shape = (across_py, across_px, len(which), xb // members, yb)
         out, speeds[V] = y_pass(
             chain,
             which,
@@ -577,7 +562,6 @@
             speeds.get(V),
             yb,
             shape,
-            block,
         )
         return out
 
@@ -585,8 +569,7 @@
 
     count = wall_tile.shape[0]
     owner = wall_owner[:, 0]
-    capacity = max(2, 4 * count // devices)
-    assert capacity <= unit
+    unit = max(2, 4 * count // devices)
     order = jnp.arange(count, dtype=jnp.int32)
     earlier = (owner[:, None] == owner[None, :]) & (order[None, :] < order[:, None])
     position = jnp.sum(earlier.astype(jnp.int32), axis=1)
@@ -612,21 +595,19 @@
     X(most, (U, V, THETA), V, THETA)
     first = exchange(Y(V, THETA))
     X(most, (U, V, THETA), U)
-    second = Y(U, slots=True)
     X(last, (W,), W)
-    third = Y(W)
+    second = Y(U, W)
     chain.last += tags
-    second = exchange(wall_lines(chain, first, 1, wall_tile, slot, second))
-    third = exchange(third)
+    flux = along("py", wall_lines(chain, first, 1, wall_tile, slot, unit))
+    flux, second = lax.optimization_barrier((wall_columns(chain, flux), second))
+    second = exchange(second)
+    solid = add_flux(chain, tags, along("px", flux), solid_temp, conductivity)
     new_fields = put(chain, None, first, (V, THETA), 1, fields.shape)
-    solid = add_flux(chain, tags, second, solid_temp, conductivity)
     low, high = margins(solid, "px", 1, margin)
     solid = jnp.concatenate([low, solid, high], axis=1)
-    new_fields = put(chain, new_fields, second, (U,), x_rows // unit, fields.shape)
     low, high = margins(solid, "py", 2, margin)
-    new_solid, new_fields = conduct_and_put(
-        chain, solid, low, high, margin, new_fields, third, W
-    )
+    new_solid = conduct(chain, solid, low, high, margin)
+    new_fields = put(chain, new_fields, second, (U, W), 1, fields.shape)
     return new_fields, new_solid
 
 

time: 248 us -> 244 us (0.984)
  blocking collectives: 37.4 us -> 0 us
  waiting for transfers between devices: 79.1 us -> 111 us
  starting transfers between devices: 42.6 us -> 54 us
  Pallas kernels: 77.9 us -> 71.1 us
    all_to_all x1 -> x0, blocking collectives: 37.4 us -> none  [exchange(): lax.all_to_all(blocks.reshape((devices,) + blocks.shape[2:]), ('py', 'px'...]
    ppermute x14 -> x24, waiting for transfers between devices: 26.6 us -> 49.6 us  [along(): lax.ppermute(piece, axis, [(i, i ^ s) for i in range(lax.axis_size(axis))])]
    ppermute x2, waiting for transfers between devices: 0.01 us -> 13.9 us  [margins(): lax.ppermute(lax.slice_in_dim(block, block.shape[dim] - width, None, axis...]
    ppermute x14 -> x24, starting transfers between devices: 10.6 us -> 20.7 us  [along(): lax.ppermute(piece, axis, [(i, i ^ s) for i in range(lax.axis_size(axis))])]
    pallas_call x13, Pallas kernels: 77.9 us -> 71.1 us  [run(): pl.pallas_call(body, grid_spec=pltpu.PrefetchScalarGridSpec(num_scalar_pr...]
    all_to_all x4, waiting for transfers between devices: 47.4 us -> 42.7 us  [exchange(): lax.all_to_all(blocks.reshape((devices,) + blocks.shape[2:]), ('py', 'px'...]
  transfers between devices with their start and end apart: 22 -> 32, of which waited for: 12 -> 19; matrix products, arithmetic and copies ran while one was open for 1% -> 1% of each run, Pallas kernels for 28% -> 26%
where the time goes in v5:
time: 244 us; the launch traced here: 243 us
  waiting for transfers between devices  111 us (45%)
  Pallas kernels  71.1 us (29%)
  starting transfers between devices  54 us (22%)
  local copies, waits for them, and re-layouts  5.68 us (2%)
    pallas_call x13, Pallas kernels, run(): pl.pallas_call(body, grid_spec=pltpu.PrefetchScalarGridSpec(num_scalar_pr...  71.1 us
    ppermute x24, waiting for transfers between devices, along(): lax.ppermute(piece, axis, [(i, i ^ s) for i in range(lax.axis_size(axis))])  49.6 us
    all_to_all x4, waiting for transfers between devices, exchange(): lax.all_to_all(blocks.reshape((devices,) + blocks.shape[2:]), ('py', 'px'...  42.7 us
    all_to_all x4, starting transfers between devices, exchange(): lax.all_to_all(blocks.reshape((devices,) + blocks.shape[2:]), ('py', 'px'...  23 us
    ppermute x24, starting transfers between devices, along(): lax.ppermute(piece, axis, [(i, i ^ s) for i in range(lax.axis_size(axis))])  20.7 us
    ppermute x2, waiting for transfers between devices, margins(): lax.ppermute(lax.slice_in_dim(block, block.shape[dim] - width, None, axis...  13.9 us
    ppermute x2, starting transfers between devices, margins(): lax.ppermute(lax.slice_in_dim(block, block.shape[dim] - width, None, axis...  6.27 us
  transfers between devices with their start and end apart: 32, of which 19 were waited for; matrix products, arithmetic and copies ran while one was open for 1% of the time, Pallas kernels for 26%

profile of v5, /device:TPU:8, one launch (start us, length us, event | category | flops | bytes accessed | tf_op | source)
XLA Modules:
  0.0 243.0 jit_solution(8268308287960942756)
XLA Ops:
  1.3 3.8 %cut.2.refs_1_ = bf16[4,4,2,3,128,128]{5,4,3,2,1,0:T(8,128)(2,1)} custom-call(s32[8]{0:T(128)} %stack.127.at_ref, bf16[4,16,128,256]{3,2,1,0:T(8,128)(2,1)} %refs_0_.9), custom_call_target="tpu_custom_call" | custom-call | bytes 6291456 | tf_op jit(solution)/shard_map/cut/pallas_call | solution.py:65
  5.1 6.0 %all-to-all-start = ((bf16[32,3,128,128]{3,2,1,0:T(8,128)(2,1)}), bf16[32,3,128,128]{3,2,1,0:T(8,128)(2,1)S(1)}, u32[]{:S(2)}, u32[]{:S(2)}) async-start(bf16[32,3,128,128]{3,2,1,0:T(8,128)(2,1)} %bitcast.169), calls=%async_computation | async-start | bytes 6291456 | tf_op jit(solution)/shard_map/all_to_all | solution.py:528
  18.2 11.9 %collective-permute-done.1.refs_4_ = s32[4,16]{1,0:T(4,128)S(1)} collective-permute-done((s32[4,16]{1,0:T(4,128)S(1)}, s32[4,16]{1,0:T(4,128)S(1)}, u32[]{:S(2)}, u32[]{:S(2)}) %collective-permute-start.1) | collective-permute-done | bytes 288 | tf_op jit(solution)/shard_map/ppermute | solution.py:523
  30.3 2.9 %collective-permute-done.5.refs_8_ = s32[4,16]{1,0:T(4,128)S(1)} collective-permute-done((s32[4,16]{1,0:T(4,128)S(1)}, s32[4,16]{1,0:T(4,128)S(1)}, u32[]{:S(2)}, u32[]{:S(2)}) %collective-permute-start.5) | collective-permute-done | bytes 288 | tf_op jit(solution)/shard_map/ppermute | solution.py:523
  34.6 2.8 %cut.3.refs_3_ = bf16[4,4,2,1,128,128]{5,4,3,2,1,0:T(8,128)(2,1)} custom-call(s32[8]{0:T(128)} %stack.127.at_ref, bf16[4,16,128,256]{3,2,1,0:T(8,128)(2,1)} %refs_0_.9, bf16[4,4,2,3,128,128]{5,4,3,2,1,0:T(8,128)(2,1)} %cut.2.refs_1_, s32[4,16]{1,0:T(4,128)} %get-tuple-element.81.refs_2_, s32[4,16]{1,0:T(4,128)} %copy-done.17, s32[4,16]{1,0:T(4,128)} %copy-done.15, ...), custom_call_target="tpu_custom_call" | custom-call | bytes 2097152 | tf_op jit(solution)/shard_map/cut/pallas_call | solution.py:65
  37.4 42.7 %all-to-all-done = bf16[32,3,128,128]{3,2,1,0:T(8,128)(2,1)S(1)} async-done(((bf16[32,3,128,128]{3,2,1,0:T(8,128)(2,1)}), bf16[32,3,128,128]{3,2,1,0:T(8,128)(2,1)S(1)}, u32[]{:S(2)}, u32[]{:S(2)}) %all-to-all-start) | async-done | bytes 3145760 | tf_op jit(solution)/shard_map/all_to_all | solution.py:528
  80.1 6.5 %all-to-all-start.2 = ((bf16[32,1,128,128]{3,2,1,0:T(8,128)(2,1)}), bf16[32,1,128,128]{3,2,1,0:T(8,128)(2,1)}, u32[]{:S(2)}, u32[]{:S(2)}) async-start(bf16[32,1,128,128]{3,2,1,0:T(8,128)(2,1)} %bitcast.170), calls=%async_computation.2 | async-start | bytes 2097152 | tf_op jit(solution)/shard_map/all_to_all | solution.py:528
  86.6 13.8 %x_pass.3 = (bf16[8,64,512]{2,1,0:T(8,128)(2,1)}, bf16[8,64,512]{2,1,0:T(8,128)(2,1)}, bf16[8,64,512]{2,1,0:T(8,128)(2,1)}, bf16[8,64,512]{2,1,0:T(8,128)(2,1)}, bf16[1024,512]{1,0:T(8,128)(2,1)}) custom-call(s32[8]{0:T(128)} %stack.127.at_ref, f32[4]{0:T(128)} %refs_0_.14, bf16[3,8,2,64,1024]{4,3,2,1,0:T(8,128)(2,1)} %bitcast.176, ...), custom_call_target="tpu_custom_call" | custom-call | flops 6442450944 | bytes 6291456 | tf_op jit(solution)/shard_map/x_pass/pallas_call | solution.py:65
  104.2 11.6 %y_pass.2 = (bf16[4,8,2,64,256]{4,3,2,1,0:T(8,128)(2,1)}, bf16[4,512,256]{2,1,0:T(8,128)(2,1)}) custom-call(s32[8]{0:T(128)} %stack.127.at_ref, f32[4]{0:T(128)} %refs_0_.14, bf16[3,1024,1024]{2,1,0:T(8,128)(2,1)} %refs_1_.4, bf16[8,64,512]{2,1,0:T(8,128)(2,1)} %get-tuple-element.34.refs_2_, bf16[8,64,512]{2,1,0:T(8,128)(2,1)} %copy-done.25, ...), custom_call_target="tpu_custom_call" | custom-call | flops 6442450944 | bytes 6291456 | tf_op jit(solution)/shard_map/y_pass/pallas_call | solution.py:65
  115.8 5.8 %all-to-all-start.1 = ((bf16[32,2,64,256]{3,2,1,0:T(8,128)(2,1)}), bf16[32,2,64,256]{3,2,1,0:T(8,128)(2,1)S(1)}, u32[]{:S(2)}, u32[]{:S(2)}) async-start(bf16[32,2,64,256]{3,2,1,0:T(8,128)(2,1)} %bitcast.173), calls=%async_computation.1 | async-start | bytes 4194304 | tf_op jit(solution)/shard_map/all_to_all | solution.py:528
  121.9 8.5 %x_pass.4 = (bf16[8,64,512]{2,1,0:T(8,128)(2,1)}, bf16[8,64,512]{2,1,0:T(8,128)(2,1)}) custom-call(s32[8]{0:T(128)} %stack.127.at_ref, f32[4]{0:T(128)} %refs_0_.14, bf16[3,8,2,64,1024]{4,3,2,1,0:T(8,128)(2,1)} %bitcast.177, bf16[4,8,3,128,128]{4,3,2,1,0:T(8,128)(2,1)} %bitcast.172, bf16[8,2,64,512]{3,2,1,0:T(8,128)(2,1)} %bitcast.179, ...), custom_call_target="tpu_custom_call" | custom-call | flops 3221225472 | bytes 2097152 | tf_op jit(solution)/shard_map/x_pass/pallas_call | solution.py:65
  130.5 8.6 %x_pass.5 = (bf16[8,64,512]{2,1,0:T(8,128)(2,1)}, bf16[8,64,512]{2,1,0:T(8,128)(2,1)}) custom-call(s32[8]{0:T(128)} %stack.127.at_ref, f32[4]{0:T(128)} %refs_0_.14, bf16[3,8,2,64,1024]{4,3,2,1,0:T(8,128)(2,1)} %bitcast.178, bf16[4,8,1,128,128]{4,3,2,1,0:T(8,128)(2,1)} %bitcast.26.refs_2_, bf16[8,2,64,512]{3,2,1,0:T(8,128)(2,1)} %bitcast.180, ...), custom_call_target="tpu_custom_call" | custom-call | flops 3221225472 | bytes 2097152 | tf_op jit(solution)/shard_map/x_pass/pallas_call | solution.py:65
  140.1 2.7 %collective-permute-start.12 = (s32[8,1,16]{2,1,0:T(1,128)S(1)}, s32[8,1,16]{2,1,0:T(1,128)S(1)}, u32[]{:S(2)}, u32[]{:S(2)}) collective-permute-start(s32[8,1,16]{2,1,0:T(1,128)S(1)} %get-tuple-element.83), channel_id=1, source_target_pairs={{0,2},{1,3},{2,0},{3,1},{4,6},{5,7},{6,4},{7,5},{8,10},{9,11},{10,... | collective-permute-start | bytes 1544 | tf_op jit(solution)/shard_map/ppermute | solution.py:523
  144.3 11.7 %y_pass.3.refs_3_ = bf16[4,8,2,64,256]{4,3,2,1,0:T(8,128)(2,1)} custom-call(s32[8]{0:T(128)} %stack.127.at_ref, f32[4]{0:T(128)} %refs_0_.14, bf16[3,1024,1024]{2,1,0:T(8,128)(2,1)} %refs_1_.4, bf16[8,64,512]{2,1,0:T(8,128)(2,1)} %get-tuple-element.41.refs_4_.refs_2_, bf16[8,64,512]{2,1,0:T(8,128)(2,1)} %copy-done.24, ...), custom_call_target="tpu_custom_call" | custom-call | flops 6442450944 | bytes 4194304 | tf_op jit(solution)/shard_map/y_pass/pallas_call | solution.py:65
  157.6 10.4 %collective-permute-done.12.refs_6_.refs_12_ = s32[8,1,16]{2,1,0:T(1,128)S(1)} collective-permute-done((s32[8,1,16]{2,1,0:T(1,128)S(1)}, s32[8,1,16]{2,1,0:T(1,128)S(1)}, u32[]{:S(2)}, u32[]{:S(2)}) %collective-permute-start.12) | collective-permute-done | bytes 544 | tf_op jit(solution)/shard_map/ppermute | solution.py:523
  177.2 2.6 %collective-permute-done.15.refs_2_ = bf16[8,16,256]{2,1,0:T(8,128)(2,1)S(1)} collective-permute-done((bf16[8,16,256]{2,1,0:T(8,128)(2,1)S(1)}, bf16[8,16,256]{2,1,0:T(8,128)(2,1)S(1)}, u32[]{:S(2)}, u32[]{:S(2)}) %collective-permute-start.15) | collective-permute-done | bytes 65568 | tf_op jit(solution)/shard_map/ppermute | solution.py:523
  182.5 4.6 %all-to-all-start.3 = ((bf16[32,2,64,256]{3,2,1,0:T(8,128)(2,1)}), bf16[32,2,64,256]{3,2,1,0:T(8,128)(2,1)}, u32[]{:S(2)}, u32[]{:S(2)}) async-start(bf16[32,2,64,256]{3,2,1,0:T(8,128)(2,1)} %bitcast.168), calls=%async_computation.3 | async-start | bytes 4194304 | tf_op jit(solution)/shard_map/all_to_all | solution.py:528
  193.1 8.1 %collective-permute-done.18.refs_4_ = bf16[4,16,256]{2,1,0:T(8,128)(2,1)S(1)} collective-permute-done((bf16[4,16,256]{2,1,0:T(8,128)(2,1)S(1)}, bf16[4,16,256]{2,1,0:T(8,128)(2,1)S(1)}, u32[]{:S(2)}, u32[]{:S(2)}) %collective-permute-start.18) | collective-permute-done | bytes 32800 | tf_op jit(solution)/shard_map/ppermute | solution.py:523
  209.1 2.7 %collective-permute-done.25 = f32[3,8,256]{2,1,0:T(8,128)S(1)} collective-permute-done((f32[3,8,256]{2,1,0:T(8,128)S(1)}, f32[3,8,256]{2,1,0:T(8,128)S(1)}, u32[]{:S(2)}, u32[]{:S(2)}) %collective-permute-start.25) | collective-permute-done | bytes 24608 | tf_op jit(solution)/shard_map/ppermute | solution.py:30
  211.9 5.0 %collective-permute-start.26 = (f32[3,80,8]{2,1,0:T(8,128)S(1)}, f32[3,80,8]{2,1,0:T(8,128)S(1)}, u32[]{:S(2)}, u32[]{:S(2)}) collective-permute-start(f32[3,80,8]{2,1,0:T(8,128)S(1)} %get-tuple-element.67), channel_id=1, source_target_pairs={{0,1},{1,2},{2,3},{4,5},{5,6},{6,7},{8,9},{9,10},{10,11},{12,13},{... | collective-permute-start | bytes 23048 | tf_op jit(solution)/shard_map/ppermute | solution.py:27
  216.9 2.8 %collective-permute-start.27 = (f32[3,80,8]{2,1,0:T(8,128)S(1)}, f32[3,80,8]{2,1,0:T(8,128)S(1)}, u32[]{:S(2)}, u32[]{:S(2)}) collective-permute-start(f32[3,80,8]{2,1,0:T(8,128)S(1)} %get-tuple-element.66), channel_id=1, source_target_pairs={{1,0},{2,1},{3,2},{5,4},{6,5},{7,6},{9,8},{10,9},{11,10},{13,12},{... | collective-permute-start | bytes 23048 | tf_op jit(solution)/shard_map/ppermute | solution.py:30
  221.8 13.9 %collective-permute-done.26.refs_1_ = f32[3,80,8]{2,1,0:T(8,128)S(1)} collective-permute-done((f32[3,80,8]{2,1,0:T(8,128)S(1)}, f32[3,80,8]{2,1,0:T(8,128)S(1)}, u32[]{:S(2)}, u32[]{:S(2)}) %collective-permute-start.26) | collective-permute-done | bytes 7712 | tf_op jit(solution)/shard_map/ppermute | solution.py:27
  237.4 2.4 conduct.1
  239.8 3.2 %put.3 = bf16[4,16,128,256]{3,2,1,0:T(8,128)(2,1)} custom-call(s32[8]{0:T(128)S(1)} %copy-done.3, bf16[4,8,2,64,256]{4,3,2,1,0:T(8,128)(2,1)} %bitcast.56.refs_0_, bf16[4,16,128,256]{3,2,1,0:T(8,128)(2,1)} %put.2.refs_1_), custom_call_target="tpu_custom_call", output_to_operand_aliasing={{}: (2, {})} | custom-call | bytes 8388608 | tf_op jit(solution)/shard_map/put/pallas_call | solution.py:65
  (127 shorter events, 46.7 us)
Async XLA Ops:
  5.1 75.0 %all-to-all-start = ((bf16[32,3,128,128]{3,2,1,0:T(8,128)(2,1)}), bf16[32,3,128,128]{3,2,1,0:T(8,128)(2,1)S(1)}, u32[]{:S(2)}, u32[]{:S(2)}) async-start(bf16[32,3,128,128]{3,2,1,0:T(8,128)(2,1)} %bitcast.169), calls=%async_computation | async-start | bytes 6291456 | tf_op jit(solution)/shard_map/all_to_all | solution.py:528
  12.4 17.7 %collective-permute-start.1 = (s32[4,16]{1,0:T(4,128)S(1)}, s32[4,16]{1,0:T(4,128)S(1)}, u32[]{:S(2)}, u32[]{:S(2)}) collective-permute-start(s32[4,16]{1,0:T(4,128)S(1)} %get-tuple-element.79), channel_id=1, source_target_pairs={{0,8},{4,12},{8,0},{12,4},{16,24},{20,28},{24,16},{28,20},{1,9},{5... | collective-permute-start | bytes 776 | tf_op jit(solution)/shard_map/ppermute | solution.py:523
  13.8 16.4 %collective-permute-start.2 = (s32[4,16]{1,0:T(4,128)S(1)}, s32[4,16]{1,0:T(4,128)S(1)}, u32[]{:S(2)}, u32[]{:S(2)}) collective-permute-start(s32[4,16]{1,0:T(4,128)S(1)} %get-tuple-element.78), channel_id=1, source_target_pairs={{0,12},{4,8},{8,4},{12,0},{16,28},{20,24},{24,20},{28,16},{1,13},{... | collective-permute-start | bytes 776 | tf_op jit(solution)/shard_map/ppermute | solution.py:523
  14.1 16.2 %collective-permute-start.3 = (s32[4,16]{1,0:T(4,128)S(1)}, s32[4,16]{1,0:T(4,128)S(1)}, u32[]{:S(2)}, u32[]{:S(2)}) collective-permute-start(s32[4,16]{1,0:T(4,128)S(1)} %get-tuple-element.77), channel_id=1, source_target_pairs={{0,16},{4,20},{8,24},{12,28},{16,0},{20,4},{24,8},{28,12},{1,17},{... | collective-permute-start | bytes 776 | tf_op jit(solution)/shard_map/ppermute | solution.py:523
  15.5 14.7 %collective-permute-start.4 = (s32[4,16]{1,0:T(4,128)S(1)}, s32[4,16]{1,0:T(4,128)S(1)}, u32[]{:S(2)}, u32[]{:S(2)}) collective-permute-start(s32[4,16]{1,0:T(4,128)S(1)} %get-tuple-element.76), channel_id=1, source_target_pairs={{0,20},{4,16},{8,28},{12,24},{16,4},{20,0},{24,12},{28,8},{1,21},{... | collective-permute-start | bytes 776 | tf_op jit(solution)/shard_map/ppermute | solution.py:523
  15.9 17.3 %collective-permute-start.5 = (s32[4,16]{1,0:T(4,128)S(1)}, s32[4,16]{1,0:T(4,128)S(1)}, u32[]{:S(2)}, u32[]{:S(2)}) collective-permute-start(s32[4,16]{1,0:T(4,128)S(1)} %get-tuple-element.75), channel_id=1, source_target_pairs={{0,24},{4,28},{8,16},{12,20},{16,8},{20,12},{24,0},{28,4},{1,25},{... | collective-permute-start | bytes 776 | tf_op jit(solution)/shard_map/ppermute | solution.py:523
  80.1 35.7 %all-to-all-start.2 = ((bf16[32,1,128,128]{3,2,1,0:T(8,128)(2,1)}), bf16[32,1,128,128]{3,2,1,0:T(8,128)(2,1)}, u32[]{:S(2)}, u32[]{:S(2)}) async-start(bf16[32,1,128,128]{3,2,1,0:T(8,128)(2,1)} %bitcast.170), calls=%async_computation.2 | async-start | bytes 2097152 | tf_op jit(solution)/shard_map/all_to_all | solution.py:528
  115.8 53.9 %all-to-all-start.1 = ((bf16[32,2,64,256]{3,2,1,0:T(8,128)(2,1)}), bf16[32,2,64,256]{3,2,1,0:T(8,128)(2,1)S(1)}, u32[]{:S(2)}, u32[]{:S(2)}) async-start(bf16[32,2,64,256]{3,2,1,0:T(8,128)(2,1)} %bitcast.173), calls=%async_computation.1 | async-start | bytes 4194304 | tf_op jit(solution)/shard_map/all_to_all | solution.py:528
  139.1 4.2 %collective-permute-start.10 = (bf16[8,64,512]{2,1,0:T(8,128)(2,1)}, bf16[8,64,512]{2,1,0:T(8,128)(2,1)S(1)}, u32[]{:S(2)}, u32[]{:S(2)}) collective-permute-start(bf16[8,64,512]{2,1,0:T(8,128)(2,1)} %get-tuple-element.44), channel_id=1, source_target_pairs={{0,4},{4,0},{8,12},{12,8},{16,20},{20,16},{24,28},{28,24},{1,5},{5... | collective-permute-start | bytes 1572872 | tf_op jit(solution)/shard_map/ppermute | solution.py:523
  139.8 17.8 %collective-permute-start.11 = (s32[8,1,16]{2,1,0:T(1,128)S(1)}, s32[8,1,16]{2,1,0:T(1,128)S(1)}, u32[]{:S(2)}, u32[]{:S(2)}) collective-permute-start(s32[8,1,16]{2,1,0:T(1,128)S(1)} %get-tuple-element.84), channel_id=1, source_target_pairs={{0,1},{1,0},{2,3},{3,2},{4,5},{5,4},{6,7},{7,6},{8,9},{9,8},{10,11... | collective-permute-start | bytes 1544 | tf_op jit(solution)/shard_map/ppermute | solution.py:523
  140.1 27.9 %collective-permute-start.12 = (s32[8,1,16]{2,1,0:T(1,128)S(1)}, s32[8,1,16]{2,1,0:T(1,128)S(1)}, u32[]{:S(2)}, u32[]{:S(2)}) collective-permute-start(s32[8,1,16]{2,1,0:T(1,128)S(1)} %get-tuple-element.83), channel_id=1, source_target_pairs={{0,2},{1,3},{2,0},{3,1},{4,6},{5,7},{6,4},{7,5},{8,10},{9,11},{10,... | collective-permute-start | bytes 1544 | tf_op jit(solution)/shard_map/ppermute | solution.py:523
  142.8 26.9 %collective-permute-start.13 = (s32[8,1,16]{2,1,0:T(1,128)S(1)}, s32[8,1,16]{2,1,0:T(1,128)S(1)}, u32[]{:S(2)}, u32[]{:S(2)}) collective-permute-start(s32[8,1,16]{2,1,0:T(1,128)S(1)} %get-tuple-element.82), channel_id=1, source_target_pairs={{0,3},{1,2},{2,1},{3,0},{4,7},{5,6},{6,5},{7,4},{8,11},{9,10},{10,... | collective-permute-start | bytes 1544 | tf_op jit(solution)/shard_map/ppermute | solution.py:523
  172.6 4.6 %collective-permute-start.14 = (bf16[8,16,256]{2,1,0:T(8,128)(2,1)S(1)}, bf16[8,16,256]{2,1,0:T(8,128)(2,1)S(1)}, u32[]{:S(2)}, u32[]{:S(2)}) collective-permute-start(bf16[8,16,256]{2,1,0:T(8,128)(2,1)S(1)} %get-tuple-element.46), channel_id=1, source_target_pairs={{0,1},{1,0},{2,3},{3,2},{4,5},{5,4},{6,7},{7,6},{8,9},{9,8},{10,11... | collective-permute-start | bytes 196616 | tf_op jit(solution)/shard_map/ppermute | solution.py:523
  174.1 5.7 %collective-permute-start.15 = (bf16[8,16,256]{2,1,0:T(8,128)(2,1)S(1)}, bf16[8,16,256]{2,1,0:T(8,128)(2,1)S(1)}, u32[]{:S(2)}, u32[]{:S(2)}) collective-permute-start(bf16[8,16,256]{2,1,0:T(8,128)(2,1)S(1)} %get-tuple-element.47), channel_id=1, source_target_pairs={{0,2},{1,3},{2,0},{3,1},{4,6},{5,7},{6,4},{7,5},{8,10},{9,11},{10,... | collective-permute-start | bytes 196616 | tf_op jit(solution)/shard_map/ppermute | solution.py:523
  175.0 6.9 %collective-permute-start.16 = (bf16[8,16,256]{2,1,0:T(8,128)(2,1)S(1)}, bf16[8,16,256]{2,1,0:T(8,128)(2,1)S(1)}, u32[]{:S(2)}, u32[]{:S(2)}) collective-permute-start(bf16[8,16,256]{2,1,0:T(8,128)(2,1)S(1)} %get-tuple-element.48), channel_id=1, source_target_pairs={{0,3},{1,2},{2,1},{3,0},{4,7},{5,6},{6,5},{7,4},{8,11},{9,10},{10,... | collective-permute-start | bytes 196616 | tf_op jit(solution)/shard_map/ppermute | solution.py:523
  182.5 57.3 %all-to-all-start.3 = ((bf16[32,2,64,256]{3,2,1,0:T(8,128)(2,1)}), bf16[32,2,64,256]{3,2,1,0:T(8,128)(2,1)}, u32[]{:S(2)}, u32[]{:S(2)}) async-start(bf16[32,2,64,256]{3,2,1,0:T(8,128)(2,1)} %bitcast.168), calls=%async_computation.3 | async-start | bytes 4194304 | tf_op jit(solution)/shard_map/all_to_all | solution.py:528
  187.3 14.0 %collective-permute-start.18 = (bf16[4,16,256]{2,1,0:T(8,128)(2,1)S(1)}, bf16[4,16,256]{2,1,0:T(8,128)(2,1)S(1)}, u32[]{:S(2)}, u32[]{:S(2)}) collective-permute-start(bf16[4,16,256]{2,1,0:T(8,128)(2,1)S(1)} %get-tuple-element.60), channel_id=1, source_target_pairs={{0,8},{4,12},{8,0},{12,4},{16,24},{20,28},{24,16},{28,20},{1,9},{5... | collective-permute-start | bytes 98312 | tf_op jit(solution)/shard_map/ppermute | solution.py:523
  188.7 13.0 %collective-permute-start.19 = (bf16[4,16,256]{2,1,0:T(8,128)(2,1)S(1)}, bf16[4,16,256]{2,1,0:T(8,128)(2,1)S(1)}, u32[]{:S(2)}, u32[]{:S(2)}) collective-permute-start(bf16[4,16,256]{2,1,0:T(8,128)(2,1)S(1)} %get-tuple-element.61), channel_id=1, source_target_pairs={{0,12},{4,8},{8,4},{12,0},{16,28},{20,24},{24,20},{28,16},{1,13},{... | collective-permute-start | bytes 98312 | tf_op jit(solution)/shard_map/ppermute | solution.py:523
  189.0 12.8 %collective-permute-start.20 = (bf16[4,16,256]{2,1,0:T(8,128)(2,1)S(1)}, bf16[4,16,256]{2,1,0:T(8,128)(2,1)S(1)}, u32[]{:S(2)}, u32[]{:S(2)}) collective-permute-start(bf16[4,16,256]{2,1,0:T(8,128)(2,1)S(1)} %get-tuple-element.62), channel_id=1, source_target_pairs={{0,16},{4,20},{8,24},{12,28},{16,0},{20,4},{24,8},{28,12},{1,17},{... | collective-permute-start | bytes 98312 | tf_op jit(solution)/shard_map/ppermute | solution.py:523
  190.4 11.4 %collective-permute-start.21 = (bf16[4,16,256]{2,1,0:T(8,128)(2,1)S(1)}, bf16[4,16,256]{2,1,0:T(8,128)(2,1)S(1)}, u32[]{:S(2)}, u32[]{:S(2)}) collective-permute-start(bf16[4,16,256]{2,1,0:T(8,128)(2,1)S(1)} %get-tuple-element.63), channel_id=1, source_target_pairs={{0,20},{4,16},{8,28},{12,24},{16,4},{20,0},{24,12},{28,8},{1,21},{... | collective-permute-start | bytes 98312 | tf_op jit(solution)/shard_map/ppermute | solution.py:523
  190.8 13.0 %collective-permute-start.22 = (bf16[4,16,256]{2,1,0:T(8,128)(2,1)S(1)}, bf16[4,16,256]{2,1,0:T(8,128)(2,1)S(1)}, u32[]{:S(2)}, u32[]{:S(2)}) collective-permute-start(bf16[4,16,256]{2,1,0:T(8,128)(2,1)S(1)} %get-tuple-element.64), channel_id=1, source_target_pairs={{0,24},{4,28},{8,16},{12,20},{16,8},{20,12},{24,0},{28,4},{1,25},{... | collective-permute-start | bytes 98312 | tf_op jit(solution)/shard_map/ppermute | solution.py:523
  201.3 4.3 %collective-permute-start.23 = (bf16[4,16,256]{2,1,0:T(8,128)(2,1)S(1)}, bf16[4,16,256]{2,1,0:T(8,128)(2,1)S(1)}, u32[]{:S(2)}, u32[]{:S(2)}) collective-permute-start(bf16[4,16,256]{2,1,0:T(8,128)(2,1)S(1)} %get-tuple-element.65), channel_id=1, source_target_pairs={{0,28},{4,24},{8,20},{12,16},{16,12},{20,8},{24,4},{28,0},{1,29},{... | collective-permute-start | bytes 98312 | tf_op jit(solution)/shard_map/ppermute | solution.py:523
  211.9 23.9 %collective-permute-start.26 = (f32[3,80,8]{2,1,0:T(8,128)S(1)}, f32[3,80,8]{2,1,0:T(8,128)S(1)}, u32[]{:S(2)}, u32[]{:S(2)}) collective-permute-start(f32[3,80,8]{2,1,0:T(8,128)S(1)} %get-tuple-element.67), channel_id=1, source_target_pairs={{0,1},{1,2},{2,3},{4,5},{5,6},{6,7},{8,9},{9,10},{10,11},{12,13},{... | collective-permute-start | bytes 23048 | tf_op jit(solution)/shard_map/ppermute | solution.py:27
  216.9 20.5 %collective-permute-start.27 = (f32[3,80,8]{2,1,0:T(8,128)S(1)}, f32[3,80,8]{2,1,0:T(8,128)S(1)}, u32[]{:S(2)}, u32[]{:S(2)}) collective-permute-start(f32[3,80,8]{2,1,0:T(8,128)S(1)} %get-tuple-element.66), channel_id=1, source_target_pairs={{1,0},{2,1},{3,2},{5,4},{6,5},{7,6},{9,8},{10,9},{11,10},{13,12},{... | collective-permute-start | bytes 23048 | tf_op jit(solution)/shard_map/ppermute | solution.py:30
  (35 other events, 250.2 us)

commit v6 on v5

--- a/solution.py
+++ b/solution.py
@@ -265,7 +265,8 @@
         if first:
             out, speed_ref, lines = rest
         else:
-            speed_ref, out, lines = rest
+            speed_ref, out, mark, lines = rest
+            mark[...] = jnp.zeros_like(mark)
         step = pl.program_id(0)
 
         @pl.when(step == 0)
@@ -315,6 +316,8 @@
     else:
         in_specs.append(pl.BlockSpec((1, height, yb), lambda i, at: (i, 0, 0)))
         args.append(speed)
+        out_specs.append(whole((8, 128)))
+        out_shape.append(jax.ShapeDtypeStruct((8, 128), jnp.float32))
     outs = chain.run(
         "y_pass",
         kernel,
@@ -599,8 +602,9 @@
     second = Y(U, W)
     chain.last += tags
     flux = along("py", wall_lines(chain, first, 1, wall_tile, slot, unit))
-    flux, second = lax.optimization_barrier((wall_columns(chain, flux), second))
+    flux, second = lax.optimization_barrier((flux, second))
     second = exchange(second)
+    flux = wall_columns(chain, flux)
     solid = add_flux(chain, tags, along("px", flux), solid_temp, conductivity)
     new_fields = put(chain, None, first, (V, THETA), 1, fields.shape)
     low, high = margins(solid, "px", 1, margin)

time: 244 us -> 242 us (level)
  no operation moved by 1% of the time
where the time goes in v6:
time: 242 us
  waiting for transfers between devices  110 us (45%)
  Pallas kernels  71.2 us (29%)
  starting transfers between devices  54 us (22%)
  local copies, waits for them, and re-layouts  4.85 us (2%)
    pallas_call x13, Pallas kernels, run(): pl.pallas_call(body, grid_spec=pltpu.PrefetchScalarGridSpec(num_scalar_pr...  71.2 us
    ppermute x24, waiting for transfers between devices, along(): lax.ppermute(piece, axis, [(i, i ^ s) for i in range(lax.axis_size(axis))])  49 us
    all_to_all x4, waiting for transfers between devices, exchange(): lax.all_to_all(blocks.reshape((devices,) + blocks.shape[2:]), ('py', 'px'...  42.7 us
    all_to_all x4, starting transfers between devices, exchange(): lax.all_to_all(blocks.reshape((devices,) + blocks.shape[2:]), ('py', 'px'...  22.9 us
    ppermute x24, starting transfers between devices, along(): lax.ppermute(piece, axis, [(i, i ^ s) for i in range(lax.axis_size(axis))])  20.7 us
    ppermute x2, waiting for transfers between devices, margins(): lax.ppermute(lax.slice_in_dim(block, block.shape[dim] - width, None, axis...  13.9 us
    ppermute x2, starting transfers between devices, margins(): lax.ppermute(lax.slice_in_dim(block, block.shape[dim] - width, None, axis...  6.28 us
  transfers between devices with their start and end apart: 32, of which 19 were waited for; matrix products, arithmetic and copies ran while one was open for 1% of the time, Pallas kernels for 26%

profile of v6, /device:TPU:8, one launch (start us, length us, event | category | flops | bytes accessed | tf_op | source)
XLA Modules:
  0.0 241.5 jit_solution(1682328290043741991)
XLA Ops:
  1.3 3.8 %cut.2.refs_1_ = bf16[4,4,2,3,128,128]{5,4,3,2,1,0:T(8,128)(2,1)} custom-call(s32[8]{0:T(128)} %stack.127.at_ref, bf16[4,16,128,256]{3,2,1,0:T(8,128)(2,1)} %refs_0_.9), custom_call_target="tpu_custom_call" | custom-call | bytes 6291456 | tf_op jit(solution)/shard_map/cut/pallas_call | solution.py:65
  5.1 6.0 %all-to-all-start = ((bf16[32,3,128,128]{3,2,1,0:T(8,128)(2,1)}), bf16[32,3,128,128]{3,2,1,0:T(8,128)(2,1)S(1)}, u32[]{:S(2)}, u32[]{:S(2)}) async-start(bf16[32,3,128,128]{3,2,1,0:T(8,128)(2,1)} %bitcast.168), calls=%async_computation | async-start | bytes 6291456 | tf_op jit(solution)/shard_map/all_to_all | solution.py:531
  18.3 11.9 %collective-permute-done.1.refs_4_ = s32[4,16]{1,0:T(4,128)S(1)} collective-permute-done((s32[4,16]{1,0:T(4,128)S(1)}, s32[4,16]{1,0:T(4,128)S(1)}, u32[]{:S(2)}, u32[]{:S(2)}) %collective-permute-start.1) | collective-permute-done | bytes 288 | tf_op jit(solution)/shard_map/ppermute | solution.py:526
  30.3 2.9 %collective-permute-done.5.refs_8_ = s32[4,16]{1,0:T(4,128)S(1)} collective-permute-done((s32[4,16]{1,0:T(4,128)S(1)}, s32[4,16]{1,0:T(4,128)S(1)}, u32[]{:S(2)}, u32[]{:S(2)}) %collective-permute-start.5) | collective-permute-done | bytes 288 | tf_op jit(solution)/shard_map/ppermute | solution.py:526
  34.7 2.8 %cut.3.refs_3_ = bf16[4,4,2,1,128,128]{5,4,3,2,1,0:T(8,128)(2,1)} custom-call(s32[8]{0:T(128)} %stack.127.at_ref, bf16[4,16,128,256]{3,2,1,0:T(8,128)(2,1)} %refs_0_.9, bf16[4,4,2,3,128,128]{5,4,3,2,1,0:T(8,128)(2,1)} %cut.2.refs_1_, s32[4,16]{1,0:T(4,128)} %get-tuple-element.77.refs_2_, s32[4,16]{1,0:T(4,128)} %copy-done.17, s32[4,16]{1,0:T(4,128)} %copy-done.15, ...), custom_call_target="tpu_custom_call" | custom-call | bytes 2097152 | tf_op jit(solution)/shard_map/cut/pallas_call | solution.py:65
  37.4 42.7 %all-to-all-done = bf16[32,3,128,128]{3,2,1,0:T(8,128)(2,1)S(1)} async-done(((bf16[32,3,128,128]{3,2,1,0:T(8,128)(2,1)}), bf16[32,3,128,128]{3,2,1,0:T(8,128)(2,1)S(1)}, u32[]{:S(2)}, u32[]{:S(2)}) %all-to-all-start) | async-done | bytes 3145760 | tf_op jit(solution)/shard_map/all_to_all | solution.py:531
  80.2 6.5 %all-to-all-start.2 = ((bf16[32,1,128,128]{3,2,1,0:T(8,128)(2,1)}), bf16[32,1,128,128]{3,2,1,0:T(8,128)(2,1)}, u32[]{:S(2)}, u32[]{:S(2)}) async-start(bf16[32,1,128,128]{3,2,1,0:T(8,128)(2,1)} %bitcast.169), calls=%async_computation.2 | async-start | bytes 2097152 | tf_op jit(solution)/shard_map/all_to_all | solution.py:531
  86.7 13.8 %x_pass.3 = (bf16[8,64,512]{2,1,0:T(8,128)(2,1)}, bf16[8,64,512]{2,1,0:T(8,128)(2,1)}, bf16[8,64,512]{2,1,0:T(8,128)(2,1)}, bf16[8,64,512]{2,1,0:T(8,128)(2,1)}, bf16[1024,512]{1,0:T(8,128)(2,1)}) custom-call(s32[8]{0:T(128)} %stack.127.at_ref, f32[4]{0:T(128)} %refs_0_.14, bf16[3,8,2,64,1024]{4,3,2,1,0:T(8,128)(2,1)} %bitcast.176, ...), custom_call_target="tpu_custom_call" | custom-call | flops 6442450944 | bytes 6291456 | tf_op jit(solution)/shard_map/x_pass/pallas_call | solution.py:65
  104.3 11.6 %y_pass.2 = (bf16[4,8,2,64,256]{4,3,2,1,0:T(8,128)(2,1)}, bf16[4,512,256]{2,1,0:T(8,128)(2,1)}) custom-call(s32[8]{0:T(128)} %stack.127.at_ref, f32[4]{0:T(128)} %refs_0_.14, bf16[3,1024,1024]{2,1,0:T(8,128)(2,1)} %refs_1_.4, bf16[8,64,512]{2,1,0:T(8,128)(2,1)} %get-tuple-element.32.refs_2_, bf16[8,64,512]{2,1,0:T(8,128)(2,1)} %copy-done.25, ...), custom_call_target="tpu_custom_call" | custom-call | flops 6442450944 | bytes 6291456 | tf_op jit(solution)/shard_map/y_pass/pallas_call | solution.py:65
  115.9 5.8 %all-to-all-start.1 = ((bf16[32,2,64,256]{3,2,1,0:T(8,128)(2,1)}), bf16[32,2,64,256]{3,2,1,0:T(8,128)(2,1)S(1)}, u32[]{:S(2)}, u32[]{:S(2)}) async-start(bf16[32,2,64,256]{3,2,1,0:T(8,128)(2,1)} %bitcast.172), calls=%async_computation.1 | async-start | bytes 4194304 | tf_op jit(solution)/shard_map/all_to_all | solution.py:531
  122.0 8.5 %x_pass.4 = (bf16[8,64,512]{2,1,0:T(8,128)(2,1)}, bf16[8,64,512]{2,1,0:T(8,128)(2,1)}) custom-call(s32[8]{0:T(128)} %stack.127.at_ref, f32[4]{0:T(128)} %refs_0_.14, bf16[3,8,2,64,1024]{4,3,2,1,0:T(8,128)(2,1)} %bitcast.177, bf16[4,8,3,128,128]{4,3,2,1,0:T(8,128)(2,1)} %bitcast.171, bf16[8,2,64,512]{3,2,1,0:T(8,128)(2,1)} %bitcast.179, ...), custom_call_target="tpu_custom_call" | custom-call | flops 3221225472 | bytes 2097152 | tf_op jit(solution)/shard_map/x_pass/pallas_call | solution.py:65
  130.6 8.6 %x_pass.5 = (bf16[8,64,512]{2,1,0:T(8,128)(2,1)}, bf16[8,64,512]{2,1,0:T(8,128)(2,1)}) custom-call(s32[8]{0:T(128)} %stack.127.at_ref, f32[4]{0:T(128)} %refs_0_.14, bf16[3,8,2,64,1024]{4,3,2,1,0:T(8,128)(2,1)} %bitcast.178, bf16[4,8,1,128,128]{4,3,2,1,0:T(8,128)(2,1)} %bitcast.26.refs_2_, bf16[8,2,64,512]{3,2,1,0:T(8,128)(2,1)} %bitcast.180, ...), custom_call_target="tpu_custom_call" | custom-call | flops 3221225472 | bytes 2097152 | tf_op jit(solution)/shard_map/x_pass/pallas_call | solution.py:65
  140.2 2.7 %collective-permute-start.12 = (s32[8,1,16]{2,1,0:T(1,128)S(1)}, s32[8,1,16]{2,1,0:T(1,128)S(1)}, u32[]{:S(2)}, u32[]{:S(2)}) collective-permute-start(s32[8,1,16]{2,1,0:T(1,128)S(1)} %get-tuple-element.79), channel_id=1, source_target_pairs={{0,2},{1,3},{2,0},{3,1},{4,6},{5,7},{6,4},{7,5},{8,10},{9,11},{10,... | collective-permute-start | bytes 1544 | tf_op jit(solution)/shard_map/ppermute | solution.py:526
  144.4 11.7 %y_pass.3 = (bf16[4,8,2,64,256]{4,3,2,1,0:T(8,128)(2,1)}, f32[8,128]{1,0:T(8,128)}) custom-call(s32[8]{0:T(128)} %stack.127.at_ref, f32[4]{0:T(128)} %refs_0_.14, bf16[3,1024,1024]{2,1,0:T(8,128)(2,1)} %refs_1_.4, bf16[8,64,512]{2,1,0:T(8,128)(2,1)} %get-tuple-element.39.refs_4_.refs_2_, bf16[8,64,512]{2,1,0:T(8,128)(2,1)} %copy-done.24, ...), custom_call_target="tpu_custom_call" | custom-call | flops 6442450944 | bytes 4202496 | tf_op jit(solution)/shard_map/y_pass/pallas_call | solution.py:65
  157.7 10.4 %collective-permute-done.12.refs_6_.refs_12_ = s32[8,1,16]{2,1,0:T(1,128)S(1)} collective-permute-done((s32[8,1,16]{2,1,0:T(1,128)S(1)}, s32[8,1,16]{2,1,0:T(1,128)S(1)}, u32[]{:S(2)}, u32[]{:S(2)}) %collective-permute-start.12) | collective-permute-done | bytes 544 | tf_op jit(solution)/shard_map/ppermute | solution.py:526
  176.3 2.6 %collective-permute-done.15.refs_2_ = bf16[8,16,256]{2,1,0:T(8,128)(2,1)S(1)} collective-permute-done((bf16[8,16,256]{2,1,0:T(8,128)(2,1)S(1)}, bf16[8,16,256]{2,1,0:T(8,128)(2,1)S(1)}, u32[]{:S(2)}, u32[]{:S(2)}) %collective-permute-start.15) | collective-permute-done | bytes 65568 | tf_op jit(solution)/shard_map/ppermute | solution.py:526
  181.1 4.6 %all-to-all-start.3 = ((bf16[32,2,64,256]{3,2,1,0:T(8,128)(2,1)}), bf16[32,2,64,256]{3,2,1,0:T(8,128)(2,1)}, u32[]{:S(2)}, u32[]{:S(2)}) async-start(bf16[32,2,64,256]{3,2,1,0:T(8,128)(2,1)} %bitcast.173), calls=%async_computation.3 | async-start | bytes 4194304 | tf_op jit(solution)/shard_map/all_to_all | solution.py:531
  192.3 7.5 %collective-permute-done.18.refs_4_ = bf16[4,16,256]{2,1,0:T(8,128)(2,1)S(1)} collective-permute-done((bf16[4,16,256]{2,1,0:T(8,128)(2,1)S(1)}, bf16[4,16,256]{2,1,0:T(8,128)(2,1)S(1)}, u32[]{:S(2)}, u32[]{:S(2)}) %collective-permute-start.18) | collective-permute-done | bytes 32800 | tf_op jit(solution)/shard_map/ppermute | solution.py:526
  207.7 2.7 %collective-permute-done.25 = f32[3,8,256]{2,1,0:T(8,128)S(1)} collective-permute-done((f32[3,8,256]{2,1,0:T(8,128)S(1)}, f32[3,8,256]{2,1,0:T(8,128)S(1)}, u32[]{:S(2)}, u32[]{:S(2)}) %collective-permute-start.25) | collective-permute-done | bytes 24608 | tf_op jit(solution)/shard_map/ppermute | solution.py:30
  210.5 5.0 %collective-permute-start.26 = (f32[3,80,8]{2,1,0:T(8,128)S(1)}, f32[3,80,8]{2,1,0:T(8,128)S(1)}, u32[]{:S(2)}, u32[]{:S(2)}) collective-permute-start(f32[3,80,8]{2,1,0:T(8,128)S(1)} %get-tuple-element.63), channel_id=1, source_target_pairs={{0,1},{1,2},{2,3},{4,5},{5,6},{6,7},{8,9},{9,10},{10,11},{12,13},{... | collective-permute-start | bytes 23048 | tf_op jit(solution)/shard_map/ppermute | solution.py:27
  215.4 2.8 %collective-permute-start.27 = (f32[3,80,8]{2,1,0:T(8,128)S(1)}, f32[3,80,8]{2,1,0:T(8,128)S(1)}, u32[]{:S(2)}, u32[]{:S(2)}) collective-permute-start(f32[3,80,8]{2,1,0:T(8,128)S(1)} %get-tuple-element.62), channel_id=1, source_target_pairs={{1,0},{2,1},{3,2},{5,4},{6,5},{7,6},{9,8},{10,9},{11,10},{13,12},{... | collective-permute-start | bytes 23048 | tf_op jit(solution)/shard_map/ppermute | solution.py:30
  220.4 13.9 %collective-permute-done.26.refs_1_ = f32[3,80,8]{2,1,0:T(8,128)S(1)} collective-permute-done((f32[3,80,8]{2,1,0:T(8,128)S(1)}, f32[3,80,8]{2,1,0:T(8,128)S(1)}, u32[]{:S(2)}, u32[]{:S(2)}) %collective-permute-start.26) | collective-permute-done | bytes 7712 | tf_op jit(solution)/shard_map/ppermute | solution.py:27
  236.0 2.4 conduct.1
  238.4 3.2 %put.3 = bf16[4,16,128,256]{3,2,1,0:T(8,128)(2,1)} custom-call(s32[8]{0:T(128)S(1)} %copy-done.2, bf16[4,8,2,64,256]{4,3,2,1,0:T(8,128)(2,1)} %bitcast.56.refs_0_, bf16[4,16,128,256]{3,2,1,0:T(8,128)(2,1)} %put.2.refs_1_), custom_call_target="tpu_custom_call", output_to_operand_aliasing={{}: (2, {})} | custom-call | bytes 8388608 | tf_op jit(solution)/shard_map/put/pallas_call | solution.py:65
  (127 shorter events, 45.9 us)
Async XLA Ops:
  5.1 75.0 %all-to-all-start = ((bf16[32,3,128,128]{3,2,1,0:T(8,128)(2,1)}), bf16[32,3,128,128]{3,2,1,0:T(8,128)(2,1)S(1)}, u32[]{:S(2)}, u32[]{:S(2)}) async-start(bf16[32,3,128,128]{3,2,1,0:T(8,128)(2,1)} %bitcast.168), calls=%async_computation | async-start | bytes 6291456 | tf_op jit(solution)/shard_map/all_to_all | solution.py:531
  12.4 17.7 %collective-permute-start.1 = (s32[4,16]{1,0:T(4,128)S(1)}, s32[4,16]{1,0:T(4,128)S(1)}, u32[]{:S(2)}, u32[]{:S(2)}) collective-permute-start(s32[4,16]{1,0:T(4,128)S(1)} %get-tuple-element.75), channel_id=1, source_target_pairs={{0,8},{4,12},{8,0},{12,4},{16,24},{20,28},{24,16},{28,20},{1,9},{5... | collective-permute-start | bytes 776 | tf_op jit(solution)/shard_map/ppermute | solution.py:526
  13.9 16.4 %collective-permute-start.2 = (s32[4,16]{1,0:T(4,128)S(1)}, s32[4,16]{1,0:T(4,128)S(1)}, u32[]{:S(2)}, u32[]{:S(2)}) collective-permute-start(s32[4,16]{1,0:T(4,128)S(1)} %get-tuple-element.74), channel_id=1, source_target_pairs={{0,12},{4,8},{8,4},{12,0},{16,28},{20,24},{24,20},{28,16},{1,13},{... | collective-permute-start | bytes 776 | tf_op jit(solution)/shard_map/ppermute | solution.py:526
  14.1 16.2 %collective-permute-start.3 = (s32[4,16]{1,0:T(4,128)S(1)}, s32[4,16]{1,0:T(4,128)S(1)}, u32[]{:S(2)}, u32[]{:S(2)}) collective-permute-start(s32[4,16]{1,0:T(4,128)S(1)} %get-tuple-element.73), channel_id=1, source_target_pairs={{0,16},{4,20},{8,24},{12,28},{16,0},{20,4},{24,8},{28,12},{1,17},{... | collective-permute-start | bytes 776 | tf_op jit(solution)/shard_map/ppermute | solution.py:526
  15.6 14.7 %collective-permute-start.4 = (s32[4,16]{1,0:T(4,128)S(1)}, s32[4,16]{1,0:T(4,128)S(1)}, u32[]{:S(2)}, u32[]{:S(2)}) collective-permute-start(s32[4,16]{1,0:T(4,128)S(1)} %get-tuple-element.72), channel_id=1, source_target_pairs={{0,20},{4,16},{8,28},{12,24},{16,4},{20,0},{24,12},{28,8},{1,21},{... | collective-permute-start | bytes 776 | tf_op jit(solution)/shard_map/ppermute | solution.py:526
  15.9 17.3 %collective-permute-start.5 = (s32[4,16]{1,0:T(4,128)S(1)}, s32[4,16]{1,0:T(4,128)S(1)}, u32[]{:S(2)}, u32[]{:S(2)}) collective-permute-start(s32[4,16]{1,0:T(4,128)S(1)} %get-tuple-element.71), channel_id=1, source_target_pairs={{0,24},{4,28},{8,16},{12,20},{16,8},{20,12},{24,0},{28,4},{1,25},{... | collective-permute-start | bytes 776 | tf_op jit(solution)/shard_map/ppermute | solution.py:526
  80.2 35.7 %all-to-all-start.2 = ((bf16[32,1,128,128]{3,2,1,0:T(8,128)(2,1)}), bf16[32,1,128,128]{3,2,1,0:T(8,128)(2,1)}, u32[]{:S(2)}, u32[]{:S(2)}) async-start(bf16[32,1,128,128]{3,2,1,0:T(8,128)(2,1)} %bitcast.169), calls=%async_computation.2 | async-start | bytes 2097152 | tf_op jit(solution)/shard_map/all_to_all | solution.py:531
  115.9 53.9 %all-to-all-start.1 = ((bf16[32,2,64,256]{3,2,1,0:T(8,128)(2,1)}), bf16[32,2,64,256]{3,2,1,0:T(8,128)(2,1)S(1)}, u32[]{:S(2)}, u32[]{:S(2)}) async-start(bf16[32,2,64,256]{3,2,1,0:T(8,128)(2,1)} %bitcast.172), calls=%async_computation.1 | async-start | bytes 4194304 | tf_op jit(solution)/shard_map/all_to_all | solution.py:531
  139.2 4.2 %collective-permute-start.10 = (bf16[8,64,512]{2,1,0:T(8,128)(2,1)}, bf16[8,64,512]{2,1,0:T(8,128)(2,1)S(1)}, u32[]{:S(2)}, u32[]{:S(2)}) collective-permute-start(bf16[8,64,512]{2,1,0:T(8,128)(2,1)} %get-tuple-element.42), channel_id=1, source_target_pairs={{0,4},{4,0},{8,12},{12,8},{16,20},{20,16},{24,28},{28,24},{1,5},{5... | collective-permute-start | bytes 1572872 | tf_op jit(solution)/shard_map/ppermute | solution.py:526
  139.9 17.8 %collective-permute-start.11 = (s32[8,1,16]{2,1,0:T(1,128)S(1)}, s32[8,1,16]{2,1,0:T(1,128)S(1)}, u32[]{:S(2)}, u32[]{:S(2)}) collective-permute-start(s32[8,1,16]{2,1,0:T(1,128)S(1)} %get-tuple-element.80), channel_id=1, source_target_pairs={{0,1},{1,0},{2,3},{3,2},{4,5},{5,4},{6,7},{7,6},{8,9},{9,8},{10,11... | collective-permute-start | bytes 1544 | tf_op jit(solution)/shard_map/ppermute | solution.py:526
  140.2 27.9 %collective-permute-start.12 = (s32[8,1,16]{2,1,0:T(1,128)S(1)}, s32[8,1,16]{2,1,0:T(1,128)S(1)}, u32[]{:S(2)}, u32[]{:S(2)}) collective-permute-start(s32[8,1,16]{2,1,0:T(1,128)S(1)} %get-tuple-element.79), channel_id=1, source_target_pairs={{0,2},{1,3},{2,0},{3,1},{4,6},{5,7},{6,4},{7,5},{8,10},{9,11},{10,... | collective-permute-start | bytes 1544 | tf_op jit(solution)/shard_map/ppermute | solution.py:526
  142.9 26.9 %collective-permute-start.13 = (s32[8,1,16]{2,1,0:T(1,128)S(1)}, s32[8,1,16]{2,1,0:T(1,128)S(1)}, u32[]{:S(2)}, u32[]{:S(2)}) collective-permute-start(s32[8,1,16]{2,1,0:T(1,128)S(1)} %get-tuple-element.78), channel_id=1, source_target_pairs={{0,3},{1,2},{2,1},{3,0},{4,7},{5,6},{6,5},{7,4},{8,11},{9,10},{10,... | collective-permute-start | bytes 1544 | tf_op jit(solution)/shard_map/ppermute | solution.py:526
  171.7 4.6 %collective-permute-start.14 = (bf16[8,16,256]{2,1,0:T(8,128)(2,1)S(1)}, bf16[8,16,256]{2,1,0:T(8,128)(2,1)S(1)}, u32[]{:S(2)}, u32[]{:S(2)}) collective-permute-start(bf16[8,16,256]{2,1,0:T(8,128)(2,1)S(1)} %get-tuple-element.45), channel_id=1, source_target_pairs={{0,1},{1,0},{2,3},{3,2},{4,5},{5,4},{6,7},{7,6},{8,9},{9,8},{10,11... | collective-permute-start | bytes 196616 | tf_op jit(solution)/shard_map/ppermute | solution.py:526
  173.2 5.7 %collective-permute-start.15 = (bf16[8,16,256]{2,1,0:T(8,128)(2,1)S(1)}, bf16[8,16,256]{2,1,0:T(8,128)(2,1)S(1)}, u32[]{:S(2)}, u32[]{:S(2)}) collective-permute-start(bf16[8,16,256]{2,1,0:T(8,128)(2,1)S(1)} %get-tuple-element.46), channel_id=1, source_target_pairs={{0,2},{1,3},{2,0},{3,1},{4,6},{5,7},{6,4},{7,5},{8,10},{9,11},{10,... | collective-permute-start | bytes 196616 | tf_op jit(solution)/shard_map/ppermute | solution.py:526
  174.1 6.9 %collective-permute-start.16 = (bf16[8,16,256]{2,1,0:T(8,128)(2,1)S(1)}, bf16[8,16,256]{2,1,0:T(8,128)(2,1)S(1)}, u32[]{:S(2)}, u32[]{:S(2)}) collective-permute-start(bf16[8,16,256]{2,1,0:T(8,128)(2,1)S(1)} %get-tuple-element.47), channel_id=1, source_target_pairs={{0,3},{1,2},{2,1},{3,0},{4,7},{5,6},{6,5},{7,4},{8,11},{9,10},{10,... | collective-permute-start | bytes 196616 | tf_op jit(solution)/shard_map/ppermute | solution.py:526
  181.1 57.3 %all-to-all-start.3 = ((bf16[32,2,64,256]{3,2,1,0:T(8,128)(2,1)}), bf16[32,2,64,256]{3,2,1,0:T(8,128)(2,1)}, u32[]{:S(2)}, u32[]{:S(2)}) async-start(bf16[32,2,64,256]{3,2,1,0:T(8,128)(2,1)} %bitcast.173), calls=%async_computation.3 | async-start | bytes 4194304 | tf_op jit(solution)/shard_map/all_to_all | solution.py:531
  186.4 13.4 %collective-permute-start.18 = (bf16[4,16,256]{2,1,0:T(8,128)(2,1)S(1)}, bf16[4,16,256]{2,1,0:T(8,128)(2,1)S(1)}, u32[]{:S(2)}, u32[]{:S(2)}) collective-permute-start(bf16[4,16,256]{2,1,0:T(8,128)(2,1)S(1)} %get-tuple-element.56), channel_id=1, source_target_pairs={{0,8},{4,12},{8,0},{12,4},{16,24},{20,28},{24,16},{28,20},{1,9},{5... | collective-permute-start | bytes 98312 | tf_op jit(solution)/shard_map/ppermute | solution.py:526
  187.9 12.5 %collective-permute-start.19 = (bf16[4,16,256]{2,1,0:T(8,128)(2,1)S(1)}, bf16[4,16,256]{2,1,0:T(8,128)(2,1)S(1)}, u32[]{:S(2)}, u32[]{:S(2)}) collective-permute-start(bf16[4,16,256]{2,1,0:T(8,128)(2,1)S(1)} %get-tuple-element.57), channel_id=1, source_target_pairs={{0,12},{4,8},{8,4},{12,0},{16,28},{20,24},{24,20},{28,16},{1,13},{... | collective-permute-start | bytes 98312 | tf_op jit(solution)/shard_map/ppermute | solution.py:526
  188.2 12.2 %collective-permute-start.20 = (bf16[4,16,256]{2,1,0:T(8,128)(2,1)S(1)}, bf16[4,16,256]{2,1,0:T(8,128)(2,1)S(1)}, u32[]{:S(2)}, u32[]{:S(2)}) collective-permute-start(bf16[4,16,256]{2,1,0:T(8,128)(2,1)S(1)} %get-tuple-element.58), channel_id=1, source_target_pairs={{0,16},{4,20},{8,24},{12,28},{16,0},{20,4},{24,8},{28,12},{1,17},{... | collective-permute-start | bytes 98312 | tf_op jit(solution)/shard_map/ppermute | solution.py:526
  189.6 10.8 %collective-permute-start.21 = (bf16[4,16,256]{2,1,0:T(8,128)(2,1)S(1)}, bf16[4,16,256]{2,1,0:T(8,128)(2,1)S(1)}, u32[]{:S(2)}, u32[]{:S(2)}) collective-permute-start(bf16[4,16,256]{2,1,0:T(8,128)(2,1)S(1)} %get-tuple-element.59), channel_id=1, source_target_pairs={{0,20},{4,16},{8,28},{12,24},{16,4},{20,0},{24,12},{28,8},{1,21},{... | collective-permute-start | bytes 98312 | tf_op jit(solution)/shard_map/ppermute | solution.py:526
  190.0 12.4 %collective-permute-start.22 = (bf16[4,16,256]{2,1,0:T(8,128)(2,1)S(1)}, bf16[4,16,256]{2,1,0:T(8,128)(2,1)S(1)}, u32[]{:S(2)}, u32[]{:S(2)}) collective-permute-start(bf16[4,16,256]{2,1,0:T(8,128)(2,1)S(1)} %get-tuple-element.60), channel_id=1, source_target_pairs={{0,24},{4,28},{8,16},{12,20},{16,8},{20,12},{24,0},{28,4},{1,25},{... | collective-permute-start | bytes 98312 | tf_op jit(solution)/shard_map/ppermute | solution.py:526
  199.8 4.3 %collective-permute-start.23 = (bf16[4,16,256]{2,1,0:T(8,128)(2,1)S(1)}, bf16[4,16,256]{2,1,0:T(8,128)(2,1)S(1)}, u32[]{:S(2)}, u32[]{:S(2)}) collective-permute-start(bf16[4,16,256]{2,1,0:T(8,128)(2,1)S(1)} %get-tuple-element.61), channel_id=1, source_target_pairs={{0,28},{4,24},{8,20},{12,16},{16,12},{20,8},{24,4},{28,0},{1,29},{... | collective-permute-start | bytes 98312 | tf_op jit(solution)/shard_map/ppermute | solution.py:526
  210.5 23.9 %collective-permute-start.26 = (f32[3,80,8]{2,1,0:T(8,128)S(1)}, f32[3,80,8]{2,1,0:T(8,128)S(1)}, u32[]{:S(2)}, u32[]{:S(2)}) collective-permute-start(f32[3,80,8]{2,1,0:T(8,128)S(1)} %get-tuple-element.63), channel_id=1, source_target_pairs={{0,1},{1,2},{2,3},{4,5},{5,6},{6,7},{8,9},{9,10},{10,11},{12,13},{... | collective-permute-start | bytes 23048 | tf_op jit(solution)/shard_map/ppermute | solution.py:27
  215.4 20.5 %collective-permute-start.27 = (f32[3,80,8]{2,1,0:T(8,128)S(1)}, f32[3,80,8]{2,1,0:T(8,128)S(1)}, u32[]{:S(2)}, u32[]{:S(2)}) collective-permute-start(f32[3,80,8]{2,1,0:T(8,128)S(1)} %get-tuple-element.62), channel_id=1, source_target_pairs={{1,0},{2,1},{3,2},{5,4},{6,5},{7,6},{9,8},{10,9},{11,10},{13,12},{... | collective-permute-start | bytes 23048 | tf_op jit(solution)/shard_map/ppermute | solution.py:30
  (35 other events, 250.5 us)

commit v7 on v6

--- a/solution.py
+++ b/solution.py
@@ -357,35 +357,50 @@
     )[0]
 
 
-def wall_lines(chain, arrived, n, tile, slot, unit):
+def wall_places(chain, tile, slot, span, slots):
+    count = tile.shape[0]
+
+    def kernel(at, tile_ref, slot_ref, chosen, filled):
+        places = lax.broadcasted_iota(jnp.int32, (count, span), 1)
+        chosen[...] = (tile_ref[...] == places).astype(jnp.float32).astype(jnp.bfloat16)
+        places = lax.broadcasted_iota(jnp.int32, (slots, count), 0)
+        filled[...] = (slot_ref[...] == places).astype(jnp.float32).astype(jnp.bfloat16)
+
+    args = [tile.reshape(-1, 1), slot.reshape(1, -1)]
+    shapes = [(count, span), (slots, count)]
+    return chain.run(
+        "wall_places",
+        kernel,
+        args,
+        like(args),
+        [whole(shape) for shape in shapes],
+        [jax.ShapeDtypeStruct(shape, jnp.bfloat16) for shape in shapes],
+        limit=SMALL_VMEM_BYTES,
+    )
+
+
+def wall_lines(chain, arrived, n, chosen, filled, unit):
     across_py, across_px, _, rows, yb = arrived.shape
-    count, span = tile.shape[0], across_px * across_py * rows
-    slots = across_py * across_px * unit
-
-    def kernel(at, tile_ref, slot_ref, arrived_ref, *refs):
+
+    def kernel(at, chosen_ref, filled_ref, arrived_ref, *refs):
         outs, lines = refs[:-1], refs[-1]
-        chosen = tile_ref[...] == lax.broadcasted_iota(jnp.int32, (count, span), 1)
         flux = jnp.dot(
-            chosen.astype(jnp.float32).astype(jnp.bfloat16),
-            arrived_ref[...].reshape(span, yb),
+            chosen_ref[...],
+            arrived_ref[...].reshape(chosen.shape[1], yb),
             preferred_element_type=jnp.float32,
         )
-        filled = slot_ref[...] == lax.broadcasted_iota(jnp.int32, (slots, count), 0)
         lines[...] = jnp.dot(
-            filled.astype(jnp.float32).astype(jnp.bfloat16),
-            flux.astype(jnp.bfloat16),
-            preferred_element_type=jnp.float32,
+            filled_ref[...], flux.astype(jnp.bfloat16), preferred_element_type=jnp.float32
         ).reshape(lines.shape)
         for s in range(across_py):
             outs[s][...] = lines[at[2] ^ s].astype(jnp.bfloat16)
 
-    args = [tile.reshape(-1, 1), slot.reshape(1, -1)]
     shape = (across_px, unit, yb)
     return chain.run(
         "wall_lines",
         kernel,
-        args + [arrived],
-        like(args)
+        [chosen, filled, arrived],
+        like([chosen, filled])
         + [pl.BlockSpec((across_py, across_px, 1, rows, yb), lambda i, at: (0, 0, n, 0, 0))],
         [whole(shape)] * across_py,
         [jax.ShapeDtypeStruct(shape, jnp.bfloat16)] * across_py,
@@ -600,8 +615,9 @@
     X(most, (U, V, THETA), U)
     X(last, (W,), W)
     second = Y(U, W)
+    chosen, filled = wall_places(chain, wall_tile, slot, layers * xb, devices * unit)
     chain.last += tags
-    flux = along("py", wall_lines(chain, first, 1, wall_tile, slot, unit))
+    flux = along("py", wall_lines(chain, first, 1, chosen, filled, unit))
     flux, second = lax.optimization_barrier((flux, second))
     second = exchange(second)
     flux = wall_columns(chain, flux)

time: 242 us -> 242 us (level)
    pallas_call x13 -> x14, Pallas kernels: 71.2 us -> 71.8 us  [run(): pl.pallas_call(body, grid_spec=pltpu.PrefetchScalarGridSpec(num_scalar_pr...]
where the time goes in v7:
time: 242 us; the launch traced here: 241 us
  waiting for transfers between devices  109 us (45%)
  Pallas kernels  71.8 us (30%)
  starting transfers between devices  54 us (22%)
  local copies, waits for them, and re-layouts  4.76 us (2%)
    pallas_call x14, Pallas kernels, run(): pl.pallas_call(body, grid_spec=pltpu.PrefetchScalarGridSpec(num_scalar_pr...  71.8 us
    ppermute x24, waiting for transfers between devices, along(): lax.ppermute(piece, axis, [(i, i ^ s) for i in range(lax.axis_size(axis))])  47.5 us
    all_to_all x4, waiting for transfers between devices, exchange(): lax.all_to_all(blocks.reshape((devices,) + blocks.shape[2:]), ('py', 'px'...  42.7 us
    all_to_all x4, starting transfers between devices, exchange(): lax.all_to_all(blocks.reshape((devices,) + blocks.shape[2:]), ('py', 'px'...  22.9 us
    ppermute x24, starting transfers between devices, along(): lax.ppermute(piece, axis, [(i, i ^ s) for i in range(lax.axis_size(axis))])  20.7 us
    ppermute x2, waiting for transfers between devices, margins(): lax.ppermute(lax.slice_in_dim(block, block.shape[dim] - width, None, axis...  13.9 us
    ppermute x2, starting transfers between devices, margins(): lax.ppermute(lax.slice_in_dim(block, block.shape[dim] - width, None, axis...  6.27 us
  transfers between devices with their start and end apart: 32, of which 19 were waited for; matrix products, arithmetic and copies ran while one was open for 1% of the time, Pallas kernels for 26%

profile of v7, /device:TPU:8, one launch (start us, length us, event | category | flops | bytes accessed | tf_op | source)
XLA Modules:
  0.0 240.7 jit_solution(5217840575138896092)
XLA Ops:
  1.3 3.8 %cut.2.refs_1_ = bf16[4,4,2,3,128,128]{5,4,3,2,1,0:T(8,128)(2,1)} custom-call(s32[8]{0:T(128)} %stack.127.at_ref, bf16[4,16,128,256]{3,2,1,0:T(8,128)(2,1)} %refs_0_.9), custom_call_target="tpu_custom_call" | custom-call | bytes 6291456 | tf_op jit(solution)/shard_map/cut/pallas_call | solution.py:65
  5.1 6.0 %all-to-all-start = ((bf16[32,3,128,128]{3,2,1,0:T(8,128)(2,1)}), bf16[32,3,128,128]{3,2,1,0:T(8,128)(2,1)S(1)}, u32[]{:S(2)}, u32[]{:S(2)}) async-start(bf16[32,3,128,128]{3,2,1,0:T(8,128)(2,1)} %bitcast.168), calls=%async_computation | async-start | bytes 6291456 | tf_op jit(solution)/shard_map/all_to_all | solution.py:546
  18.2 11.9 %collective-permute-done.1.refs_4_ = s32[4,16]{1,0:T(4,128)S(1)} collective-permute-done((s32[4,16]{1,0:T(4,128)S(1)}, s32[4,16]{1,0:T(4,128)S(1)}, u32[]{:S(2)}, u32[]{:S(2)}) %collective-permute-start.1) | collective-permute-done | bytes 288 | tf_op jit(solution)/shard_map/ppermute | solution.py:541
  30.3 2.9 %collective-permute-done.5.refs_8_ = s32[4,16]{1,0:T(4,128)S(1)} collective-permute-done((s32[4,16]{1,0:T(4,128)S(1)}, s32[4,16]{1,0:T(4,128)S(1)}, u32[]{:S(2)}, u32[]{:S(2)}) %collective-permute-start.5) | collective-permute-done | bytes 288 | tf_op jit(solution)/shard_map/ppermute | solution.py:541
  34.6 2.8 %cut.3.refs_3_ = bf16[4,4,2,1,128,128]{5,4,3,2,1,0:T(8,128)(2,1)} custom-call(s32[8]{0:T(128)} %stack.127.at_ref, bf16[4,16,128,256]{3,2,1,0:T(8,128)(2,1)} %refs_0_.9, bf16[4,4,2,3,128,128]{5,4,3,2,1,0:T(8,128)(2,1)} %cut.2.refs_1_, s32[4,16]{1,0:T(4,128)} %get-tuple-element.81.refs_2_, s32[4,16]{1,0:T(4,128)} %copy-done.17, s32[4,16]{1,0:T(4,128)} %copy-done.15, ...), custom_call_target="tpu_custom_call" | custom-call | bytes 2097152 | tf_op jit(solution)/shard_map/cut/pallas_call | solution.py:65
  37.3 42.7 %all-to-all-done = bf16[32,3,128,128]{3,2,1,0:T(8,128)(2,1)S(1)} async-done(((bf16[32,3,128,128]{3,2,1,0:T(8,128)(2,1)}), bf16[32,3,128,128]{3,2,1,0:T(8,128)(2,1)S(1)}, u32[]{:S(2)}, u32[]{:S(2)}) %all-to-all-start) | async-done | bytes 3145760 | tf_op jit(solution)/shard_map/all_to_all | solution.py:546
  80.1 6.5 %all-to-all-start.1 = ((bf16[32,1,128,128]{3,2,1,0:T(8,128)(2,1)}), bf16[32,1,128,128]{3,2,1,0:T(8,128)(2,1)}, u32[]{:S(2)}, u32[]{:S(2)}) async-start(bf16[32,1,128,128]{3,2,1,0:T(8,128)(2,1)} %bitcast.169), calls=%async_computation.1 | async-start | bytes 2097152 | tf_op jit(solution)/shard_map/all_to_all | solution.py:546
  86.6 13.8 %x_pass.3 = (bf16[8,64,512]{2,1,0:T(8,128)(2,1)}, bf16[8,64,512]{2,1,0:T(8,128)(2,1)}, bf16[8,64,512]{2,1,0:T(8,128)(2,1)}, bf16[8,64,512]{2,1,0:T(8,128)(2,1)}, bf16[1024,512]{1,0:T(8,128)(2,1)}) custom-call(s32[8]{0:T(128)} %stack.127.at_ref, f32[4]{0:T(128)} %refs_0_.14, bf16[3,8,2,64,1024]{4,3,2,1,0:T(8,128)(2,1)} %bitcast.176, ...), custom_call_target="tpu_custom_call" | custom-call | flops 6442450944 | bytes 6291456 | tf_op jit(solution)/shard_map/x_pass/pallas_call | solution.py:65
  104.2 11.6 %y_pass.2 = (bf16[4,8,2,64,256]{4,3,2,1,0:T(8,128)(2,1)}, bf16[4,512,256]{2,1,0:T(8,128)(2,1)}) custom-call(s32[8]{0:T(128)} %stack.127.at_ref, f32[4]{0:T(128)} %refs_0_.14, bf16[3,1024,1024]{2,1,0:T(8,128)(2,1)} %refs_1_.4, bf16[8,64,512]{2,1,0:T(8,128)(2,1)} %get-tuple-element.35.refs_2_, bf16[8,64,512]{2,1,0:T(8,128)(2,1)} %copy-done.25, ...), custom_call_target="tpu_custom_call" | custom-call | flops 6442450944 | bytes 6291456 | tf_op jit(solution)/shard_map/y_pass/pallas_call | solution.py:65
  115.8 5.8 %all-to-all-start.2 = ((bf16[32,2,64,256]{3,2,1,0:T(8,128)(2,1)}), bf16[32,2,64,256]{3,2,1,0:T(8,128)(2,1)S(1)}, u32[]{:S(2)}, u32[]{:S(2)}) async-start(bf16[32,2,64,256]{3,2,1,0:T(8,128)(2,1)} %bitcast.172), calls=%async_computation.2 | async-start | bytes 4194304 | tf_op jit(solution)/shard_map/all_to_all | solution.py:546
  121.9 8.5 %x_pass.4 = (bf16[8,64,512]{2,1,0:T(8,128)(2,1)}, bf16[8,64,512]{2,1,0:T(8,128)(2,1)}) custom-call(s32[8]{0:T(128)} %stack.127.at_ref, f32[4]{0:T(128)} %refs_0_.14, bf16[3,8,2,64,1024]{4,3,2,1,0:T(8,128)(2,1)} %bitcast.177, bf16[4,8,3,128,128]{4,3,2,1,0:T(8,128)(2,1)} %bitcast.171, bf16[8,2,64,512]{3,2,1,0:T(8,128)(2,1)} %bitcast.179, ...), custom_call_target="tpu_custom_call" | custom-call | flops 3221225472 | bytes 2097152 | tf_op jit(solution)/shard_map/x_pass/pallas_call | solution.py:65
  130.5 8.6 %x_pass.5 = (bf16[8,64,512]{2,1,0:T(8,128)(2,1)}, bf16[8,64,512]{2,1,0:T(8,128)(2,1)}) custom-call(s32[8]{0:T(128)} %stack.127.at_ref, f32[4]{0:T(128)} %refs_0_.14, bf16[3,8,2,64,1024]{4,3,2,1,0:T(8,128)(2,1)} %bitcast.178, bf16[4,8,1,128,128]{4,3,2,1,0:T(8,128)(2,1)} %bitcast.24.refs_2_, bf16[8,2,64,512]{3,2,1,0:T(8,128)(2,1)} %bitcast.180, ...), custom_call_target="tpu_custom_call" | custom-call | flops 3221225472 | bytes 2097152 | tf_op jit(solution)/shard_map/x_pass/pallas_call | solution.py:65
  140.1 2.7 %collective-permute-start.12 = (s32[8,1,16]{2,1,0:T(1,128)S(1)}, s32[8,1,16]{2,1,0:T(1,128)S(1)}, u32[]{:S(2)}, u32[]{:S(2)}) collective-permute-start(s32[8,1,16]{2,1,0:T(1,128)S(1)} %get-tuple-element.83), channel_id=1, source_target_pairs={{0,2},{1,3},{2,0},{3,1},{4,6},{5,7},{6,4},{7,5},{8,10},{9,11},{10,... | collective-permute-start | bytes 1544 | tf_op jit(solution)/shard_map/ppermute | solution.py:541
  144.3 11.7 %y_pass.3 = (bf16[4,8,2,64,256]{4,3,2,1,0:T(8,128)(2,1)}, f32[8,128]{1,0:T(8,128)}) custom-call(s32[8]{0:T(128)} %stack.127.at_ref, f32[4]{0:T(128)} %refs_0_.14, bf16[3,1024,1024]{2,1,0:T(8,128)(2,1)} %refs_1_.4, bf16[8,64,512]{2,1,0:T(8,128)(2,1)} %get-tuple-element.40.refs_4_.refs_2_, bf16[8,64,512]{2,1,0:T(8,128)(2,1)} %copy-done.24, ...), custom_call_target="tpu_custom_call" | custom-call | flops 6442450944 | bytes 4202496 | tf_op jit(solution)/shard_map/y_pass/pallas_call | solution.py:65
  157.6 10.4 %collective-permute-done.12.refs_5_.refs_12_ = s32[8,1,16]{2,1,0:T(1,128)S(1)} collective-permute-done((s32[8,1,16]{2,1,0:T(1,128)S(1)}, s32[8,1,16]{2,1,0:T(1,128)S(1)}, u32[]{:S(2)}, u32[]{:S(2)}) %collective-permute-start.12) | collective-permute-done | bytes 544 | tf_op jit(solution)/shard_map/ppermute | solution.py:541
  175.5 2.6 %collective-permute-done.15.refs_2_ = bf16[8,16,256]{2,1,0:T(8,128)(2,1)S(1)} collective-permute-done((bf16[8,16,256]{2,1,0:T(8,128)(2,1)S(1)}, bf16[8,16,256]{2,1,0:T(8,128)(2,1)S(1)}, u32[]{:S(2)}, u32[]{:S(2)}) %collective-permute-start.15) | collective-permute-done | bytes 65568 | tf_op jit(solution)/shard_map/ppermute | solution.py:541
  180.2 4.6 %all-to-all-start.3 = ((bf16[32,2,64,256]{3,2,1,0:T(8,128)(2,1)}), bf16[32,2,64,256]{3,2,1,0:T(8,128)(2,1)}, u32[]{:S(2)}, u32[]{:S(2)}) async-start(bf16[32,2,64,256]{3,2,1,0:T(8,128)(2,1)} %bitcast.173), calls=%async_computation.3 | async-start | bytes 4194304 | tf_op jit(solution)/shard_map/all_to_all | solution.py:546
  191.5 7.5 %collective-permute-done.18.refs_4_ = bf16[4,16,256]{2,1,0:T(8,128)(2,1)S(1)} collective-permute-done((bf16[4,16,256]{2,1,0:T(8,128)(2,1)S(1)}, bf16[4,16,256]{2,1,0:T(8,128)(2,1)S(1)}, u32[]{:S(2)}, u32[]{:S(2)}) %collective-permute-start.18) | collective-permute-done | bytes 32800 | tf_op jit(solution)/shard_map/ppermute | solution.py:541
  206.8 2.7 %collective-permute-done.25 = f32[3,8,256]{2,1,0:T(8,128)S(1)} collective-permute-done((f32[3,8,256]{2,1,0:T(8,128)S(1)}, f32[3,8,256]{2,1,0:T(8,128)S(1)}, u32[]{:S(2)}, u32[]{:S(2)}) %collective-permute-start.25) | collective-permute-done | bytes 24608 | tf_op jit(solution)/shard_map/ppermute | solution.py:30
  209.6 5.0 %collective-permute-start.26 = (f32[3,80,8]{2,1,0:T(8,128)S(1)}, f32[3,80,8]{2,1,0:T(8,128)S(1)}, u32[]{:S(2)}, u32[]{:S(2)}) collective-permute-start(f32[3,80,8]{2,1,0:T(8,128)S(1)} %get-tuple-element.67), channel_id=1, source_target_pairs={{0,1},{1,2},{2,3},{4,5},{5,6},{6,7},{8,9},{9,10},{10,11},{12,13},{... | collective-permute-start | bytes 23048 | tf_op jit(solution)/shard_map/ppermute | solution.py:27
  214.6 2.8 %collective-permute-start.27 = (f32[3,80,8]{2,1,0:T(8,128)S(1)}, f32[3,80,8]{2,1,0:T(8,128)S(1)}, u32[]{:S(2)}, u32[]{:S(2)}) collective-permute-start(f32[3,80,8]{2,1,0:T(8,128)S(1)} %get-tuple-element.66), channel_id=1, source_target_pairs={{1,0},{2,1},{3,2},{5,4},{6,5},{7,6},{9,8},{10,9},{11,10},{13,12},{... | collective-permute-start | bytes 23048 | tf_op jit(solution)/shard_map/ppermute | solution.py:30
  219.5 13.9 %collective-permute-done.26.refs_1_ = f32[3,80,8]{2,1,0:T(8,128)S(1)} collective-permute-done((f32[3,80,8]{2,1,0:T(8,128)S(1)}, f32[3,80,8]{2,1,0:T(8,128)S(1)}, u32[]{:S(2)}, u32[]{:S(2)}) %collective-permute-start.26) | collective-permute-done | bytes 7712 | tf_op jit(solution)/shard_map/ppermute | solution.py:27
  235.1 2.4 conduct.1
  237.5 3.2 %put.3 = bf16[4,16,128,256]{3,2,1,0:T(8,128)(2,1)} custom-call(s32[8]{0:T(128)S(1)} %copy-done.2, bf16[4,8,2,64,256]{4,3,2,1,0:T(8,128)(2,1)} %bitcast.56.refs_0_, bf16[4,16,128,256]{3,2,1,0:T(8,128)(2,1)} %put.2.refs_1_), custom_call_target="tpu_custom_call", output_to_operand_aliasing={{}: (2, {})} | custom-call | bytes 8388608 | tf_op jit(solution)/shard_map/put/pallas_call | solution.py:65
  (128 shorter events, 45.0 us)
Async XLA Ops:
  5.1 75.0 %all-to-all-start = ((bf16[32,3,128,128]{3,2,1,0:T(8,128)(2,1)}), bf16[32,3,128,128]{3,2,1,0:T(8,128)(2,1)S(1)}, u32[]{:S(2)}, u32[]{:S(2)}) async-start(bf16[32,3,128,128]{3,2,1,0:T(8,128)(2,1)} %bitcast.168), calls=%async_computation | async-start | bytes 6291456 | tf_op jit(solution)/shard_map/all_to_all | solution.py:546
  12.4 17.7 %collective-permute-start.1 = (s32[4,16]{1,0:T(4,128)S(1)}, s32[4,16]{1,0:T(4,128)S(1)}, u32[]{:S(2)}, u32[]{:S(2)}) collective-permute-start(s32[4,16]{1,0:T(4,128)S(1)} %get-tuple-element.79), channel_id=1, source_target_pairs={{0,8},{4,12},{8,0},{12,4},{16,24},{20,28},{24,16},{28,20},{1,9},{5... | collective-permute-start | bytes 776 | tf_op jit(solution)/shard_map/ppermute | solution.py:541
  13.8 16.4 %collective-permute-start.2 = (s32[4,16]{1,0:T(4,128)S(1)}, s32[4,16]{1,0:T(4,128)S(1)}, u32[]{:S(2)}, u32[]{:S(2)}) collective-permute-start(s32[4,16]{1,0:T(4,128)S(1)} %get-tuple-element.78), channel_id=1, source_target_pairs={{0,12},{4,8},{8,4},{12,0},{16,28},{20,24},{24,20},{28,16},{1,13},{... | collective-permute-start | bytes 776 | tf_op jit(solution)/shard_map/ppermute | solution.py:541
  14.1 16.2 %collective-permute-start.3 = (s32[4,16]{1,0:T(4,128)S(1)}, s32[4,16]{1,0:T(4,128)S(1)}, u32[]{:S(2)}, u32[]{:S(2)}) collective-permute-start(s32[4,16]{1,0:T(4,128)S(1)} %get-tuple-element.77), channel_id=1, source_target_pairs={{0,16},{4,20},{8,24},{12,28},{16,0},{20,4},{24,8},{28,12},{1,17},{... | collective-permute-start | bytes 776 | tf_op jit(solution)/shard_map/ppermute | solution.py:541
  15.5 14.7 %collective-permute-start.4 = (s32[4,16]{1,0:T(4,128)S(1)}, s32[4,16]{1,0:T(4,128)S(1)}, u32[]{:S(2)}, u32[]{:S(2)}) collective-permute-start(s32[4,16]{1,0:T(4,128)S(1)} %get-tuple-element.76), channel_id=1, source_target_pairs={{0,20},{4,16},{8,28},{12,24},{16,4},{20,0},{24,12},{28,8},{1,21},{... | collective-permute-start | bytes 776 | tf_op jit(solution)/shard_map/ppermute | solution.py:541
  15.9 17.3 %collective-permute-start.5 = (s32[4,16]{1,0:T(4,128)S(1)}, s32[4,16]{1,0:T(4,128)S(1)}, u32[]{:S(2)}, u32[]{:S(2)}) collective-permute-start(s32[4,16]{1,0:T(4,128)S(1)} %get-tuple-element.75), channel_id=1, source_target_pairs={{0,24},{4,28},{8,16},{12,20},{16,8},{20,12},{24,0},{28,4},{1,25},{... | collective-permute-start | bytes 776 | tf_op jit(solution)/shard_map/ppermute | solution.py:541
  80.1 35.7 %all-to-all-start.1 = ((bf16[32,1,128,128]{3,2,1,0:T(8,128)(2,1)}), bf16[32,1,128,128]{3,2,1,0:T(8,128)(2,1)}, u32[]{:S(2)}, u32[]{:S(2)}) async-start(bf16[32,1,128,128]{3,2,1,0:T(8,128)(2,1)} %bitcast.169), calls=%async_computation.1 | async-start | bytes 2097152 | tf_op jit(solution)/shard_map/all_to_all | solution.py:546
  115.8 53.9 %all-to-all-start.2 = ((bf16[32,2,64,256]{3,2,1,0:T(8,128)(2,1)}), bf16[32,2,64,256]{3,2,1,0:T(8,128)(2,1)S(1)}, u32[]{:S(2)}, u32[]{:S(2)}) async-start(bf16[32,2,64,256]{3,2,1,0:T(8,128)(2,1)} %bitcast.172), calls=%async_computation.2 | async-start | bytes 4194304 | tf_op jit(solution)/shard_map/all_to_all | solution.py:546
  139.1 4.2 %collective-permute-start.10 = (bf16[8,64,512]{2,1,0:T(8,128)(2,1)}, bf16[8,64,512]{2,1,0:T(8,128)(2,1)S(1)}, u32[]{:S(2)}, u32[]{:S(2)}) collective-permute-start(bf16[8,64,512]{2,1,0:T(8,128)(2,1)} %get-tuple-element.43), channel_id=1, source_target_pairs={{0,4},{4,0},{8,12},{12,8},{16,20},{20,16},{24,28},{28,24},{1,5},{5... | collective-permute-start | bytes 1572872 | tf_op jit(solution)/shard_map/ppermute | solution.py:541
  139.8 17.8 %collective-permute-start.11 = (s32[8,1,16]{2,1,0:T(1,128)S(1)}, s32[8,1,16]{2,1,0:T(1,128)S(1)}, u32[]{:S(2)}, u32[]{:S(2)}) collective-permute-start(s32[8,1,16]{2,1,0:T(1,128)S(1)} %get-tuple-element.84), channel_id=1, source_target_pairs={{0,1},{1,0},{2,3},{3,2},{4,5},{5,4},{6,7},{7,6},{8,9},{9,8},{10,11... | collective-permute-start | bytes 1544 | tf_op jit(solution)/shard_map/ppermute | solution.py:541
  140.1 27.9 %collective-permute-start.12 = (s32[8,1,16]{2,1,0:T(1,128)S(1)}, s32[8,1,16]{2,1,0:T(1,128)S(1)}, u32[]{:S(2)}, u32[]{:S(2)}) collective-permute-start(s32[8,1,16]{2,1,0:T(1,128)S(1)} %get-tuple-element.83), channel_id=1, source_target_pairs={{0,2},{1,3},{2,0},{3,1},{4,6},{5,7},{6,4},{7,5},{8,10},{9,11},{10,... | collective-permute-start | bytes 1544 | tf_op jit(solution)/shard_map/ppermute | solution.py:541
  142.8 26.9 %collective-permute-start.13 = (s32[8,1,16]{2,1,0:T(1,128)S(1)}, s32[8,1,16]{2,1,0:T(1,128)S(1)}, u32[]{:S(2)}, u32[]{:S(2)}) collective-permute-start(s32[8,1,16]{2,1,0:T(1,128)S(1)} %get-tuple-element.82), channel_id=1, source_target_pairs={{0,3},{1,2},{2,1},{3,0},{4,7},{5,6},{6,5},{7,4},{8,11},{9,10},{10,... | collective-permute-start | bytes 1544 | tf_op jit(solution)/shard_map/ppermute | solution.py:541
  170.9 4.6 %collective-permute-start.14 = (bf16[8,16,256]{2,1,0:T(8,128)(2,1)S(1)}, bf16[8,16,256]{2,1,0:T(8,128)(2,1)S(1)}, u32[]{:S(2)}, u32[]{:S(2)}) collective-permute-start(bf16[8,16,256]{2,1,0:T(8,128)(2,1)S(1)} %get-tuple-element.49), channel_id=1, source_target_pairs={{0,1},{1,0},{2,3},{3,2},{4,5},{5,4},{6,7},{7,6},{8,9},{9,8},{10,11... | collective-permute-start | bytes 196616 | tf_op jit(solution)/shard_map/ppermute | solution.py:541
  172.4 5.7 %collective-permute-start.15 = (bf16[8,16,256]{2,1,0:T(8,128)(2,1)S(1)}, bf16[8,16,256]{2,1,0:T(8,128)(2,1)S(1)}, u32[]{:S(2)}, u32[]{:S(2)}) collective-permute-start(bf16[8,16,256]{2,1,0:T(8,128)(2,1)S(1)} %get-tuple-element.50), channel_id=1, source_target_pairs={{0,2},{1,3},{2,0},{3,1},{4,6},{5,7},{6,4},{7,5},{8,10},{9,11},{10,... | collective-permute-start | bytes 196616 | tf_op jit(solution)/shard_map/ppermute | solution.py:541
  173.3 6.9 %collective-permute-start.16 = (bf16[8,16,256]{2,1,0:T(8,128)(2,1)S(1)}, bf16[8,16,256]{2,1,0:T(8,128)(2,1)S(1)}, u32[]{:S(2)}, u32[]{:S(2)}) collective-permute-start(bf16[8,16,256]{2,1,0:T(8,128)(2,1)S(1)} %get-tuple-element.51), channel_id=1, source_target_pairs={{0,3},{1,2},{2,1},{3,0},{4,7},{5,6},{6,5},{7,4},{8,11},{9,10},{10,... | collective-permute-start | bytes 196616 | tf_op jit(solution)/shard_map/ppermute | solution.py:541
  180.2 57.3 %all-to-all-start.3 = ((bf16[32,2,64,256]{3,2,1,0:T(8,128)(2,1)}), bf16[32,2,64,256]{3,2,1,0:T(8,128)(2,1)}, u32[]{:S(2)}, u32[]{:S(2)}) async-start(bf16[32,2,64,256]{3,2,1,0:T(8,128)(2,1)} %bitcast.173), calls=%async_computation.3 | async-start | bytes 4194304 | tf_op jit(solution)/shard_map/all_to_all | solution.py:546
  185.6 13.4 %collective-permute-start.18 = (bf16[4,16,256]{2,1,0:T(8,128)(2,1)S(1)}, bf16[4,16,256]{2,1,0:T(8,128)(2,1)S(1)}, u32[]{:S(2)}, u32[]{:S(2)}) collective-permute-start(bf16[4,16,256]{2,1,0:T(8,128)(2,1)S(1)} %get-tuple-element.60), channel_id=1, source_target_pairs={{0,8},{4,12},{8,0},{12,4},{16,24},{20,28},{24,16},{28,20},{1,9},{5... | collective-permute-start | bytes 98312 | tf_op jit(solution)/shard_map/ppermute | solution.py:541
  187.1 12.5 %collective-permute-start.19 = (bf16[4,16,256]{2,1,0:T(8,128)(2,1)S(1)}, bf16[4,16,256]{2,1,0:T(8,128)(2,1)S(1)}, u32[]{:S(2)}, u32[]{:S(2)}) collective-permute-start(bf16[4,16,256]{2,1,0:T(8,128)(2,1)S(1)} %get-tuple-element.61), channel_id=1, source_target_pairs={{0,12},{4,8},{8,4},{12,0},{16,28},{20,24},{24,20},{28,16},{1,13},{... | collective-permute-start | bytes 98312 | tf_op jit(solution)/shard_map/ppermute | solution.py:541
  187.3 12.2 %collective-permute-start.20 = (bf16[4,16,256]{2,1,0:T(8,128)(2,1)S(1)}, bf16[4,16,256]{2,1,0:T(8,128)(2,1)S(1)}, u32[]{:S(2)}, u32[]{:S(2)}) collective-permute-start(bf16[4,16,256]{2,1,0:T(8,128)(2,1)S(1)} %get-tuple-element.62), channel_id=1, source_target_pairs={{0,16},{4,20},{8,24},{12,28},{16,0},{20,4},{24,8},{28,12},{1,17},{... | collective-permute-start | bytes 98312 | tf_op jit(solution)/shard_map/ppermute | solution.py:541
  188.8 10.8 %collective-permute-start.21 = (bf16[4,16,256]{2,1,0:T(8,128)(2,1)S(1)}, bf16[4,16,256]{2,1,0:T(8,128)(2,1)S(1)}, u32[]{:S(2)}, u32[]{:S(2)}) collective-permute-start(bf16[4,16,256]{2,1,0:T(8,128)(2,1)S(1)} %get-tuple-element.63), channel_id=1, source_target_pairs={{0,20},{4,16},{8,28},{12,24},{16,4},{20,0},{24,12},{28,8},{1,21},{... | collective-permute-start | bytes 98312 | tf_op jit(solution)/shard_map/ppermute | solution.py:541
  189.1 12.4 %collective-permute-start.22 = (bf16[4,16,256]{2,1,0:T(8,128)(2,1)S(1)}, bf16[4,16,256]{2,1,0:T(8,128)(2,1)S(1)}, u32[]{:S(2)}, u32[]{:S(2)}) collective-permute-start(bf16[4,16,256]{2,1,0:T(8,128)(2,1)S(1)} %get-tuple-element.64), channel_id=1, source_target_pairs={{0,24},{4,28},{8,16},{12,20},{16,8},{20,12},{24,0},{28,4},{1,25},{... | collective-permute-start | bytes 98312 | tf_op jit(solution)/shard_map/ppermute | solution.py:541
  199.0 4.3 %collective-permute-start.23 = (bf16[4,16,256]{2,1,0:T(8,128)(2,1)S(1)}, bf16[4,16,256]{2,1,0:T(8,128)(2,1)S(1)}, u32[]{:S(2)}, u32[]{:S(2)}) collective-permute-start(bf16[4,16,256]{2,1,0:T(8,128)(2,1)S(1)} %get-tuple-element.65), channel_id=1, source_target_pairs={{0,28},{4,24},{8,20},{12,16},{16,12},{20,8},{24,4},{28,0},{1,29},{... | collective-permute-start | bytes 98312 | tf_op jit(solution)/shard_map/ppermute | solution.py:541
  209.6 23.9 %collective-permute-start.26 = (f32[3,80,8]{2,1,0:T(8,128)S(1)}, f32[3,80,8]{2,1,0:T(8,128)S(1)}, u32[]{:S(2)}, u32[]{:S(2)}) collective-permute-start(f32[3,80,8]{2,1,0:T(8,128)S(1)} %get-tuple-element.67), channel_id=1, source_target_pairs={{0,1},{1,2},{2,3},{4,5},{5,6},{6,7},{8,9},{9,10},{10,11},{12,13},{... | collective-permute-start | bytes 23048 | tf_op jit(solution)/shard_map/ppermute | solution.py:27
  214.6 20.5 %collective-permute-start.27 = (f32[3,80,8]{2,1,0:T(8,128)S(1)}, f32[3,80,8]{2,1,0:T(8,128)S(1)}, u32[]{:S(2)}, u32[]{:S(2)}) collective-permute-start(f32[3,80,8]{2,1,0:T(8,128)S(1)} %get-tuple-element.66), channel_id=1, source_target_pairs={{1,0},{2,1},{3,2},{5,4},{6,5},{7,6},{9,8},{10,9},{11,10},{13,12},{... | collective-permute-start | bytes 23048 | tf_op jit(solution)/shard_map/ppermute | solution.py:30
  (35 other events, 236.8 us)
